TPU v7x, 256 devices: a whole 4x4x8 slice. The times are simulated.
256 devices in a mesh: dp: 4 (over y), tm: 16 (over z, core), rows: 4 (over x).
Axes of the slice: x: 4, y: 4, z: 8, core: 2. Of those that a mesh axis runs over, the one named last changes fastest.
Arguments:
- latents: bfloat16 [8, 32, 8, 192, 128], P('dp', 'tm', 'rows'), may hold values from -6 to 6
- slot_tile: int32 [4], replicated, may hold values from 0 to 7, as said below
- norm_gain: float32 [192], replicated, may hold values from 0.1 to 1.9
- conv_weight: bfloat16 [3, 3, 3, 192, 192], replicated, may hold values from -0.078125 to 0.078125
- up_weight: bfloat16 [3, 3, 96, 192], replicated, may hold values from -0.15625 to 0.15625
Outputs:
- pixels: bfloat16 [8, 32, 16, 96, 256], P('dp', 'tm', 'rows')
Inputs may be any that keep to these rules, and one draw needn't show every extreme that they name: `slot_tile`: the values are distinct tile indices; tile 0 and tile 8 - 1 are always among them.
All inputs are finite; a program needn't handle non-finite values.
Results may differ from a plain program's by a relative error of at most 0.0052.
Values may be sent and summed in bfloat16 or wider, within the bound.
No kernel may reach another device: no remote copies, remote signals or barrier semaphores. Data moves between devices by JAX's collectives and lax.ppermute only.
A program may use at most 128 MiB of HBM per device.

v0:
```python
import jax
import jax.numpy as jnp
from jax import lax
from jax.sharding import PartitionSpec as P


def padded_2(value, sides, width):
    for axis, dim in sides:
        count, length = (lax.axis_size(axis), value.shape[dim])
        up = [(i, (i + 1) % count) for i in range(count - 1)]
        down = [(j, i) for i, j in up]
        last = lax.slice_in_dim(value, length - width, length, axis=dim)
        first = lax.slice_in_dim(value, 0, width, axis=dim)
        before = lax.ppermute(last, axis, up)
        after = lax.ppermute(first, axis, down)
        value = jnp.concatenate([before, value, after], axis=dim)
    return value


def passed_along(block, axis, distance):
    devices = range(lax.axis_size(axis))
    route = [(i - distance, i) for i in devices if i - distance in devices]
    return lax.ppermute(block, axis, route)


def activate(features, norm_gain):
    values = features.astype(jnp.float32)
    meansq = jnp.mean(values * values, axis=-2, keepdims=True)
    normed = values * lax.rsqrt(meansq + 1e-06) * norm_gain[:, None]
    return jax.nn.silu(normed).astype(jnp.bfloat16)


def causal_conv(activated, conv_weight):
    frames = activated.shape[1] - 2
    height = activated.shape[2] - 2
    cols = activated.shape[4]
    padded = jnp.pad(activated, ((0, 0), (0, 0), (0, 0), (0, 0), (1, 1)))
    total = jnp.zeros((activated.shape[0], frames, height, conv_weight.shape[3], cols), jnp.float32)
    for tap_time in range(3):
        for tap_row in range(3):
            for tap_col in range(3):
                window = padded[
                    :,
                    tap_time : tap_time + frames,
                    tap_row : tap_row + height,
                    :,
                    tap_col : tap_col + cols,
                ]
                total = total + jnp.einsum(
                    "sfrcw,oc->sfrow",
                    window,
                    conv_weight[tap_time, tap_row, tap_col],
                    preferred_element_type=jnp.float32,
                )
    return total


def upsample_conv(hidden_ext, up_weight):
    height = hidden_ext.shape[2] - 2
    cols = hidden_ext.shape[4]
    upsampled = jnp.repeat(jnp.repeat(hidden_ext, 2, axis=2), 2, axis=4)
    upsampled = upsampled[:, :, 1:-1]
    upsampled = jnp.pad(upsampled, ((0, 0), (0, 0), (0, 0), (0, 0), (1, 1)))
    result = jnp.zeros(
        (hidden_ext.shape[0], hidden_ext.shape[1], 2 * height, up_weight.shape[2], 2 * cols),
        jnp.float32,
    )
    for tap_row in range(3):
        for tap_col in range(3):
            window = upsampled[
                :, :, tap_row : tap_row + 2 * height, :, tap_col : tap_col + 2 * cols
            ]
            result = result + jnp.einsum(
                "sfrcw,oc->sfrow",
                window,
                up_weight[tap_row, tap_col],
                preferred_element_type=jnp.float32,
            )
    return result.astype(jnp.bfloat16)


def decode_block(block, norm_gain, conv_weight, up_weight):
    rim_width = 1
    extended = padded_2(block, (("rows", 2),), rim_width)
    previous = passed_along(extended, "tm", 1)
    stacked = jnp.concatenate([previous, extended], axis=1)
    activated = activate(stacked, norm_gain)
    conv_terms = causal_conv(activated, conv_weight)
    residual_part = extended[:, :, 1:-1].astype(jnp.float32)
    hidden = (residual_part + conv_terms).astype(jnp.bfloat16)
    hidden_ext = padded_2(hidden, (("rows", 2),), 1)
    return upsample_conv(hidden_ext, up_weight)


def on_device(latents, slot_tile, norm_gain, conv_weight, up_weight):
    own_tiles = latents.shape[0]
    group_index = lax.axis_index("dp")
    tile_ids = group_index * own_tiles + jnp.arange(own_tiles, dtype=jnp.int32)
    matches = slot_tile[None, :] == tile_ids[:, None]
    is_valid = jnp.any(matches, axis=1)
    result = decode_block(latents, norm_gain, conv_weight, up_weight)
    keep_mask = is_valid.astype(jnp.bfloat16)[:, None, None, None, None]
    return result * keep_mask


def solution(mesh):
    placed = (P("dp", "tm", "rows", None, None), P(), P(), P(), P())
    return jax.shard_map(
        on_device,
        mesh=mesh,
        in_specs=placed,
        out_specs=P("dp", "tm", "rows", None, None),
        check_vma=False,
    )
```

profile of v0, /device:TPU:110, one launch (start us, length us, event | category | flops | bytes accessed | tf_op | source)
XLA Modules:
  0.0 77.0 jit_solution(6533084053498813523)
XLA Ops:
  0.0 1.1 %fusion.173 = (bf16[2,2,1,192,128]{4,3,2,1,0:T(8,128)(2,1)S(1)}, bf16[2,2,1,192,128]{4,3,2,1,0:T(8,128)(2,1)S(1)}) fusion(bf16[2,2,2,192,128]{4,3,2,1,0:T(8,128)(2,1)} %param.5), kind=kLoop, calls=%fused_computation.219 | loop fusion | bytes 786432 | tf_op jit(solution)/shard_map/slice | solution.py:13
  1.1 1.3 %collective-permute-start = (bf16[2,2,1,192,128]{4,3,2,1,0:T(8,128)(2,1)S(1)}, bf16[2,2,1,192,128]{4,3,2,1,0:T(8,128)(2,1)S(1)}, u32[]{:S(2)}, u32[]{:S(2)}) collective-permute-start(bf16[2,2,1,192,128]{4,3,2,1,0:T(8,128)(2,1)S(1)} %get-tuple-element.11), channel_id=1, source_target_pairs={{0,1},{1,2},{2,3},{4,5},{5,6},{6,7},{8,9},{9,10},{10,11},{12,13},{... | collective-permute-start | bytes 589832 | tf_op jit(solution)/shard_map/ppermute | solution.py:14
  2.4 4.6 %collective-permute-start.1 = (bf16[2,2,1,192,128]{4,3,2,1,0:T(8,128)(2,1)S(1)}, bf16[2,2,1,192,128]{4,3,2,1,0:T(8,128)(2,1)S(1)}, u32[]{:S(2)}, u32[]{:S(2)}) collective-permute-start(bf16[2,2,1,192,128]{4,3,2,1,0:T(8,128)(2,1)S(1)} %get-tuple-element.10), channel_id=1, source_target_pairs={{1,0},{2,1},{3,2},{5,4},{6,5},{7,6},{9,8},{10,9},{11,10},{13,12},{... | collective-permute-start | bytes 589832 | tf_op jit(solution)/shard_map/ppermute | solution.py:15
  6.9 2.7 %collective-permute-done = bf16[2,2,1,192,128]{4,3,2,1,0:T(8,128)(2,1)S(1)} collective-permute-done((bf16[2,2,1,192,128]{4,3,2,1,0:T(8,128)(2,1)S(1)}, bf16[2,2,1,192,128]{4,3,2,1,0:T(8,128)(2,1)S(1)}, u32[]{:S(2)}, u32[]{:S(2)}) %collective-permute-start) | collective-permute-done | bytes 196640 | tf_op jit(solution)/shard_map/ppermute | solution.py:14
  9.6 1.1 %constant_dynamic-update-slice_fusion.1 = bf16[2,2,4,192,128]{4,3,2,1,0:T(8,128)(2,1)S(1)} fusion(bf16[2,2,4,192,128]{4,3,2,1,0:T(8,128)(2,1)S(1)} %constant_dynamic-update-slice_fusion.2, bf16[2,2,2,192,128]{4,3,2,1,0:T(8,128)(2,1)} %param.5), kind=kLoop, calls=%fused_computation.189 | loop fusion | bytes 786432
  10.8 1.9 %collective-permute-start.2 = (bf16[2,2,4,192,128]{4,3,2,1,0:T(8,128)(2,1)S(1)}, bf16[2,2,4,192,128]{4,3,2,1,0:T(8,128)(2,1)S(1)}, u32[]{:S(2)}, u32[]{:S(2)}) collective-permute-start(bf16[2,2,4,192,128]{4,3,2,1,0:T(8,128)(2,1)S(1)} %constant_dynamic-update-slice_fusion), channel_id=1, source_target_pairs={{0,4},{4,8},{8,12},{12,16},{16,20},{20,24},{24,28},{28,32},{32,36}... | collective-permute-start | bytes 2359304 | tf_op jit(solution)/shard_map/ppermute | solution.py:23
  12.8 11.4 %collective-permute-done.2 = bf16[2,2,4,192,128]{4,3,2,1,0:T(8,128)(2,1)S(1)} collective-permute-done((bf16[2,2,4,192,128]{4,3,2,1,0:T(8,128)(2,1)S(1)}, bf16[2,2,4,192,128]{4,3,2,1,0:T(8,128)(2,1)S(1)}, u32[]{:S(2)}, u32[]{:S(2)}) %collective-permute-start.2) | collective-permute-done | bytes 786464 | tf_op jit(solution)/shard_map/ppermute | solution.py:23
  24.5 1.0 %fusion.7 = bf16[2,4,4,192,128]{4,3,2,1,0:T(8,128)(2,1)S(1)} fusion(f32[192]{0:T(256)S(1)} %copy-done.6, f32[2,4,4,128]{3,2,1,0:T(4,128)S(1)} %add_rsqrt_fusion, bf16[2,2,4,192,128]{4,3,2,1,0:T(8,128)(2,1)S(1)} %constant_dynamic-update-slice_fusion, bf16[2,2,4,192,128]{4,3,2,1,0:T(8,128)(2,1)S(1)} %collective-permute-done.2), kind=kLoop, calls=%fused_computation.33 | loop fusion | flops 7077888 | bytes 3162880 | tf_op jit(solution)/shard_map/convert_element_type | solution.py:30
  30.7 1.0 %fusion.48 = f32[2,2,2,192,128]{4,3,2,1,0:T(8,128)S(1)} fusion(f32[2,2,2,128,192]{3,4,2,1,0:T(8,128)S(1)} %fusion.63, f32[2,2,2,128,192]{3,4,2,1,0:T(8,128)S(1)} %fusion.59, f32[2,2,2,128,192]{3,4,2,1,0:T(8,128)S(1)} %fusion.58, f32[2,2,2,128,192]{3,4,2,1,0:T(8,128)S(1)} %fusion.65, f32[2,2,2,128,192]{3,4,2,1,0:T(8,128)S(1)} %fusion.57, ...), kind=kOutput, calls=%fused_computation.87 | convolution fusion | flops 78643200 | bytes 15040512 | tf_op jit(solution)/shard_map/sfrcw,oc->sfrow/dot_general | solution.py:49
  32.1 0.4 fusion.29
  32.7 0.4 fusion.27
  33.7 0.4 fusion.24
  35.5 4.4 %collective-permute-start.4 = (bf16[2,2,1,192,128]{4,3,2,1,0:T(8,128)(2,1)S(1)}, bf16[2,2,1,192,128]{4,3,2,1,0:T(8,128)(2,1)S(1)}, u32[]{:S(2)}, u32[]{:S(2)}) collective-permute-start(bf16[2,2,1,192,128]{4,3,2,1,0:T(8,128)(2,1)S(1)} %get-tuple-element.9), channel_id=1, source_target_pairs={{1,0},{2,1},{3,2},{5,4},{6,5},{7,6},{9,8},{10,9},{11,10},{13,12},{... | collective-permute-start | bytes 589832 | tf_op jit(solution)/shard_map/ppermute | solution.py:15
  39.9 1.5 %collective-permute-start.3 = (bf16[2,2,1,192,128]{4,3,2,1,0:T(8,128)(2,1)S(1)}, bf16[2,2,1,192,128]{4,3,2,1,0:T(8,128)(2,1)S(1)}, u32[]{:S(2)}, u32[]{:S(2)}) collective-permute-start(bf16[2,2,1,192,128]{4,3,2,1,0:T(8,128)(2,1)S(1)} %get-tuple-element.8), channel_id=1, source_target_pairs={{0,1},{1,2},{2,3},{4,5},{5,6},{6,7},{8,9},{9,10},{10,11},{12,13},{... | collective-permute-start | bytes 589832 | tf_op jit(solution)/shard_map/ppermute | solution.py:14
  41.6 3.4 %collective-permute-done.4 = bf16[2,2,1,192,128]{4,3,2,1,0:T(8,128)(2,1)S(1)} collective-permute-done((bf16[2,2,1,192,128]{4,3,2,1,0:T(8,128)(2,1)S(1)}, bf16[2,2,1,192,128]{4,3,2,1,0:T(8,128)(2,1)S(1)}, u32[]{:S(2)}, u32[]{:S(2)}) %collective-permute-start.4) | collective-permute-done | bytes 196640 | tf_op jit(solution)/shard_map/ppermute | solution.py:15
  44.9 4.1 %collective-permute-done.3 = bf16[2,2,1,192,128]{4,3,2,1,0:T(8,128)(2,1)S(1)} collective-permute-done((bf16[2,2,1,192,128]{4,3,2,1,0:T(8,128)(2,1)S(1)}, bf16[2,2,1,192,128]{4,3,2,1,0:T(8,128)(2,1)S(1)}, u32[]{:S(2)}, u32[]{:S(2)}) %collective-permute-start.3) | collective-permute-done | bytes 196640 | tf_op jit(solution)/shard_map/ppermute | solution.py:14
  49.2 1.5 %broadcast_in_dim.4 = bf16[2,2,4,2,192,128]{5,4,3,2,1,0:T(8,128)(2,1)} broadcast(bf16[2,2,4,192,128]{4,3,2,1,0:T(8,128)(2,1)S(1)} %pad_maximum_fusion.1), dimensions={0,1,2,4,5} | broadcast | bytes 2359296 | tf_op jit(solution)/shard_map/broadcast_in_dim | solution.py:61
  50.7 3.2 %copy.16 = bf16[2,2,8,192,128]{3,2,4,1,0:T(8,128)(2,1)S(1)} copy(bf16[2,2,8,192,128]{4,3,2,1,0:T(8,128)(2,1)} %bitcast.304) | data formatting | bytes 3145728 | tf_op jit(solution)/shard_map/reshape | solution.py:61
  54.2 3.1 %slice.334 = bf16[2,2,6,192,256]{3,2,4,1,0:T(8,128)(2,1)} slice(bf16[2,2,8,192,256]{3,2,4,1,0:T(8,128)(2,1)S(1)} %bitcast.302), slice={[0:2], [0:2], [1:7], [0:192], [0:256]} | slice | bytes 4718592 | tf_op jit(solution)/shard_map/slice | solution.py:62
  57.3 4.4 %fusion.171 = (bf16[2,2,4,192,256]{3,2,4,1,0:T(4,128)(2,1)}, bf16[2,2,4,192,256]{3,2,4,1,0:T(4,128)(2,1)}, bf16[2,2,4,192,256]{3,2,4,1,0:T(4,128)(2,1)}) fusion(bf16[2,2,8,192,256]{3,2,4,1,0:T(8,128)(2,1)S(1)} %bitcast.303), kind=kLoop, calls=%fused_computation.217 | loop fusion | bytes 9437184 | tf_op jit(solution)/shard_map/slice | solution.py:70
  61.6 6.2 %copy.57 = bf16[2,2,6,192,256]{4,3,2,1,0:T(8,128)(2,1)S(1)} copy(bf16[2,2,6,192,256]{3,2,4,1,0:T(8,128)(2,1)} %slice.334) | data formatting | bytes 4718592
  67.8 0.6 fusion.18
  68.5 0.6 fusion.17
  69.1 0.6 fusion.16
  69.8 0.6 fusion.15
  70.4 0.6 fusion.14
  71.1 0.9 %copy-done.2 = bf16[2,2,4,192,256]{3,2,4,1,0:T(4,128)(2,1)S(1)} copy-done((bf16[2,2,4,192,256]{3,2,4,1,0:T(4,128)(2,1)S(1)}, bf16[2,2,4,192,256]{3,2,4,1,0:T(4,128)(2,1)}, u32[]{:S(2)}) %copy-start.2) | copy-done | bytes 1572888
  72.0 0.8 fusion.8
  72.8 0.8 fusion.10
  73.6 0.8 %copy-done = bf16[2,2,4,192,256]{3,2,4,1,0:T(4,128)(2,1)S(1)} copy-done((bf16[2,2,4,192,256]{3,2,4,1,0:T(4,128)(2,1)S(1)}, bf16[2,2,4,192,256]{3,2,4,1,0:T(4,128)(2,1)}, u32[]{:S(2)}) %copy-start) | copy-done | bytes 1572888
  74.4 0.8 fusion.12
  75.1 1.9 %fusion.43 = bf16[2,2,4,96,256]{4,3,2,1,0:T(8,128)(2,1)} fusion(bf16[2,2,6,192,256]{4,3,2,1,0:T(8,128)(2,1)S(1)} %copy.57, f32[2,2,4,256,96]{3,4,2,1,0:T(8,128)S(1)} %fusion.8, f32[2,2,4,256,96]{3,4,2,1,0:T(8,128)S(1)} %fusion.18, f32[2,2,4,256,96]{3,4,2,1,0:T(8,128)S(1)} %fusion.17, f32[2,2,4,256,96]{3,4,2,1,0:T(8,128)S(1)} %fusion.10, ...), kind=kOutput, calls=%fused_computation.82 | convolution fusion | flops 154927104 | bytes 15778304 | tf_op jit(solution)/shard_map/sfrcw,oc->sfrow/dot_general | solution.py:73
  (48 shorter events, 8.8 us)
Async XLA Ops:
  0.0 24.5 %copy-start.6 = (f32[192]{0:T(256)S(1)}, f32[192]{0:T(256)}, u32[]{:S(2)}) copy-start(f32[192]{0:T(256)} %param.7) | copy-start | bytes 2308
  1.1 8.5 %collective-permute-start = (bf16[2,2,1,192,128]{4,3,2,1,0:T(8,128)(2,1)S(1)}, bf16[2,2,1,192,128]{4,3,2,1,0:T(8,128)(2,1)S(1)}, u32[]{:S(2)}, u32[]{:S(2)}) collective-permute-start(bf16[2,2,1,192,128]{4,3,2,1,0:T(8,128)(2,1)S(1)} %get-tuple-element.11), channel_id=1, source_target_pairs={{0,1},{1,2},{2,3},{4,5},{5,6},{6,7},{8,9},{9,10},{10,11},{12,13},{... | collective-permute-start | bytes 589832 | tf_op jit(solution)/shard_map/ppermute | solution.py:14
  2.4 8.4 %collective-permute-start.1 = (bf16[2,2,1,192,128]{4,3,2,1,0:T(8,128)(2,1)S(1)}, bf16[2,2,1,192,128]{4,3,2,1,0:T(8,128)(2,1)S(1)}, u32[]{:S(2)}, u32[]{:S(2)}) collective-permute-start(bf16[2,2,1,192,128]{4,3,2,1,0:T(8,128)(2,1)S(1)} %get-tuple-element.10), channel_id=1, source_target_pairs={{1,0},{2,1},{3,2},{5,4},{6,5},{7,6},{9,8},{10,9},{11,10},{13,12},{... | collective-permute-start | bytes 589832 | tf_op jit(solution)/shard_map/ppermute | solution.py:15
  10.8 13.3 %collective-permute-start.2 = (bf16[2,2,4,192,128]{4,3,2,1,0:T(8,128)(2,1)S(1)}, bf16[2,2,4,192,128]{4,3,2,1,0:T(8,128)(2,1)S(1)}, u32[]{:S(2)}, u32[]{:S(2)}) collective-permute-start(bf16[2,2,4,192,128]{4,3,2,1,0:T(8,128)(2,1)S(1)} %constant_dynamic-update-slice_fusion), channel_id=1, source_target_pairs={{0,4},{4,8},{8,12},{12,16},{16,20},{20,24},{24,28},{28,32},{32,36}... | collective-permute-start | bytes 2359304 | tf_op jit(solution)/shard_map/ppermute | solution.py:23
  12.7 12.8 %copy-start.4 = (bf16[3,3,3,192,192]{4,3,2,1,0:T(8,128)(2,1)S(1)}, bf16[3,3,3,192,192]{4,3,2,1,0:T(8,128)(2,1)}, u32[]{:S(2)}) copy-start(bf16[3,3,3,192,192]{4,3,2,1,0:T(8,128)(2,1)} %param.8) | copy-start | bytes 5971972
  34.1 1.0 %copy-start.3 = (bf16[2,2,2,192,128]{4,3,2,1,0:T(8,128)(2,1)S(1)}, bf16[2,2,2,192,128]{4,3,2,1,0:T(8,128)(2,1)}, u32[]{:S(2)}) copy-start(bf16[2,2,2,192,128]{4,3,2,1,0:T(8,128)(2,1)} %param.5) | copy-start | bytes 1179652
  35.1 6.3 %copy-start.7 = (s32[4]{0:T(128)S(1)}, s32[4]{0:T(128)}, u32[]{:S(2)}) copy-start(s32[4]{0:T(128)} %param.6) | copy-start | bytes 52
  35.5 9.5 %collective-permute-start.4 = (bf16[2,2,1,192,128]{4,3,2,1,0:T(8,128)(2,1)S(1)}, bf16[2,2,1,192,128]{4,3,2,1,0:T(8,128)(2,1)S(1)}, u32[]{:S(2)}, u32[]{:S(2)}) collective-permute-start(bf16[2,2,1,192,128]{4,3,2,1,0:T(8,128)(2,1)S(1)} %get-tuple-element.9), channel_id=1, source_target_pairs={{1,0},{2,1},{3,2},{5,4},{6,5},{7,6},{9,8},{10,9},{11,10},{13,12},{... | collective-permute-start | bytes 589832 | tf_op jit(solution)/shard_map/ppermute | solution.py:15
  39.9 9.2 %collective-permute-start.3 = (bf16[2,2,1,192,128]{4,3,2,1,0:T(8,128)(2,1)S(1)}, bf16[2,2,1,192,128]{4,3,2,1,0:T(8,128)(2,1)S(1)}, u32[]{:S(2)}, u32[]{:S(2)}) collective-permute-start(bf16[2,2,1,192,128]{4,3,2,1,0:T(8,128)(2,1)S(1)} %get-tuple-element.8), channel_id=1, source_target_pairs={{0,1},{1,2},{2,3},{4,5},{5,6},{6,7},{8,9},{9,10},{10,11},{12,13},{... | collective-permute-start | bytes 589832 | tf_op jit(solution)/shard_map/ppermute | solution.py:14
  61.6 6.2 %copy-start.5 = (bf16[3,3,96,192]{3,2,1,0:T(8,128)(2,1)S(1)}, bf16[3,3,96,192]{3,2,1,0:T(8,128)(2,1)}, u32[]{:S(2)}) copy-start(bf16[3,3,96,192]{3,2,1,0:T(8,128)(2,1)} %param.9) | copy-start | bytes 995332
  70.4 1.6 %copy-start.2 = (bf16[2,2,4,192,256]{3,2,4,1,0:T(4,128)(2,1)S(1)}, bf16[2,2,4,192,256]{3,2,4,1,0:T(4,128)(2,1)}, u32[]{:S(2)}) copy-start(bf16[2,2,4,192,256]{3,2,4,1,0:T(4,128)(2,1)} %get-tuple-element.7) | copy-start | bytes 4718596
  71.1 1.8 %copy-start.1 = (bf16[2,2,4,192,256]{3,2,4,1,0:T(4,128)(2,1)S(1)}, bf16[2,2,4,192,256]{3,2,4,1,0:T(4,128)(2,1)}, u32[]{:S(2)}) copy-start(bf16[2,2,4,192,256]{3,2,4,1,0:T(4,128)(2,1)} %get-tuple-element.6) | copy-start | bytes 4718596
  72.8 1.6 %copy-start = (bf16[2,2,4,192,256]{3,2,4,1,0:T(4,128)(2,1)S(1)}, bf16[2,2,4,192,256]{3,2,4,1,0:T(4,128)(2,1)}, u32[]{:S(2)}) copy-start(bf16[2,2,4,192,256]{3,2,4,1,0:T(4,128)(2,1)} %get-tuple-element.5) | copy-start | bytes 4718596
where the time goes:
time: 77.5 us; the launch traced here: 77 us
  local copies, waits for them, and re-layouts  23 us (30%)
  waiting for transfers between devices  21.6 us (28%)
  matrix products  16.8 us (22%)
  starting transfers between devices  13.7 us (18%)
  other arithmetic  1.66 us (2%)
    ppermute x1, waiting for transfers between devices, passed_along(): return lax.ppermute(block, axis, route)  11.4 us
    unnamed x19, local copies, waits for them, and re-layouts  9.4 us
    dot_general x27, matrix products, causal_conv(): jnp.einsum('sfrcw,oc->sfrow', window, conv_weight[tap_time, tap_row, tap_...  9.37 us
    ppermute x2, starting transfers between devices, padded_2(): after = lax.ppermute(first, axis, down)  8.97 us
    dot_general x9, matrix products, upsample_conv(): jnp.einsum('sfrcw,oc->sfrow', window, up_weight[tap_row, tap_col], prefer...  7.38 us
    ppermute x2, waiting for transfers between devices, padded_2(): before = lax.ppermute(last, axis, up)  6.79 us
    slice x1, local copies, waits for them, and re-layouts, upsample_conv(): upsampled[:, :, tap_row:tap_row + 2 * height, :, tap_col:tap_col + 2 * cols]  4.36 us
    ppermute x2, waiting for transfers between devices, padded_2(): after = lax.ppermute(first, axis, down)  3.47 us
  transfers between devices with their start and end apart: 5, of which 5 were waited for; matrix products, arithmetic and copies ran while one was open for 2% of the time, Pallas kernels for 0%

commit v1 on v0

v1 whole, which is shorter than its diff:
```python
import functools

import jax
import jax.numpy as jnp
from jax import lax
from jax.experimental import pallas as pl
from jax.experimental.pallas import tpu as pltpu
from jax.sharding import PartitionSpec as P

C = 192
C2 = 96
W = 128
VMEM_LIMIT = 24 * 1024 * 1024


def activate(x, gain):
    meansq = jnp.mean(x * x, axis=0, keepdims=True)
    g = x * lax.rsqrt(meansq + 1e-06) * gain
    return (g * jax.nn.sigmoid(g)).astype(jnp.bfloat16)


def pair(ref, frame, row):
    return jnp.concatenate([ref[0, frame, row], ref[1, frame, row]], axis=1)


def shifted(p, by):
    lane = lax.broadcasted_iota(jnp.int32, (p.shape[0], W), 1)
    edge = 0 if by == 1 else W - 1
    halves = []
    for t in range(2):
        moved = pltpu.roll(p[:, t * W : (t + 1) * W], by % W, 1)
        halves.append(jnp.where(lane == edge, 0.0, moved))
    return jnp.concatenate(halves, axis=1)


def conv_terms(acts, w_ref, frame_out, row_out):
    acc = None
    for kt, panels in acts:
        for row in range(2):
            kh = row - row_out + 2
            if 0 <= kh <= 2:
                term = jnp.dot(w_ref[kt * 3 + kh], panels[row], preferred_element_type=jnp.float32)
                acc = term if acc is None else acc + term
    return shifted(acc[:C], 1) + acc[C : 2 * C] + shifted(acc[2 * C :], -1)


def own_kernel(x_ref, gain_ref, w_ref, s_ref):
    gain = gain_ref[...]
    xs = [[pair(x_ref, f, r).astype(jnp.float32) for r in range(2)] for f in range(2)]
    a = [[activate(xs[f][r], gain) for r in range(2)] for f in range(2)]
    for fo in range(2):
        for ro in range(4):
            acts = [(2 - (fo - fi), a[fi]) for fi in range(fo + 1)]
            total = conv_terms(acts, w_ref, fo, ro)
            if ro in (1, 2):
                total = total + xs[fo][ro - 1]
            s_ref[fo, ro] = total


def previous_kernel(x_ref, gain_ref, w_ref, s1_ref, s_ref, up_ref, down_ref):
    gain = gain_ref[...]
    a = [[activate(pair(x_ref, f, r).astype(jnp.float32), gain) for r in range(2)] for f in range(2)]
    for fo in range(2):
        for ro in range(4):
            acts = [(0, a[0]), (1, a[1])] if fo == 0 else [(0, a[1])]
            total = s1_ref[fo, ro] + conv_terms(acts, w_ref, fo, ro)
            s_ref[fo, ro] = total
            if ro < 2:
                up_ref[fo, ro] = total.astype(jnp.bfloat16)
            else:
                down_ref[fo, ro - 2] = total.astype(jnp.bfloat16)


def upsample_kernel(flag_ref, s_ref, above_ref, below_ref, w_ref, out_ref):
    keep = [flag_ref[0], flag_ref[1]]
    has = [flag_ref[2], flag_ref[3]]
    src = lax.broadcasted_iota(jnp.int32, (2 * W, 2 * W), 0)
    dst = lax.broadcasted_iota(jnp.int32, (2 * W, 2 * W), 1)
    spread = (dst == jnp.where(src < W, 2 * src, 2 * (src - W) + 1)).astype(jnp.bfloat16)
    for f in range(2):
        hidden = []
        for ro in range(4):
            there = has[0] if ro < 2 else has[1]
            got = (above_ref[f, ro] if ro < 2 else below_ref[f, ro - 2]).astype(jnp.float32)
            total = s_ref[f, ro] + got * there
            if ro in (0, 3):
                total = total * there
            hidden.append(total.astype(jnp.bfloat16))
        taps = {}
        for ro, khs in ((0, (0,)), (1, (0, 1, 2)), (2, (0, 1, 2)), (3, (2,))):
            for kh in khs:
                taps[kh, ro] = jnp.dot(w_ref[kh], hidden[ro], preferred_element_type=jnp.float32)
        for q in range(2):
            mid = taps[1, q + 1]
            for parity in range(2):
                if parity == 0:
                    rows = taps[0, q] + mid + taps[2, q + 1]
                else:
                    rows = taps[0, q + 1] + mid + taps[2, q + 2]
                k0, k1, k2 = rows[:C2], rows[C2 : 2 * C2], rows[2 * C2 :]
                even = (shifted(k0, 1) + k1 + k2).astype(jnp.bfloat16)
                odd = (k0 + k1 + shifted(k2, -1)).astype(jnp.bfloat16)
                for t in range(2):
                    both = jnp.concatenate([even[:, t * W : (t + 1) * W], odd[:, t * W : (t + 1) * W]], axis=1)
                    wide = jnp.dot(both, spread, preferred_element_type=jnp.float32)
                    out_ref[t, f, 2 * q + parity] = (wide * keep[t]).astype(jnp.bfloat16)


def call(kernel, out_shape, n_in, flops, smem_first=False):
    specs = [pl.BlockSpec(memory_space=pltpu.VMEM)] * n_in
    if smem_first:
        specs[0] = pl.BlockSpec(memory_space=pltpu.SMEM)
    several = isinstance(out_shape, tuple)
    vmem = pl.BlockSpec(memory_space=pltpu.VMEM)
    return pl.pallas_call(
        kernel,
        out_shape=out_shape,
        in_specs=specs,
        out_specs=(vmem,) * len(out_shape) if several else vmem,
        compiler_params=pltpu.CompilerParams(vmem_limit_bytes=VMEM_LIMIT),
        cost_estimate=pl.CostEstimate(flops=flops, bytes_accessed=4_000_000, transcendentals=0),
    )


def on_device(latents, slot_tile, norm_gain, conv_weight, up_weight):
    own_tiles, frames, rows = latents.shape[:3]
    tiles = lax.axis_index("dp") * own_tiles + jnp.arange(own_tiles, dtype=jnp.int32)
    keep = jnp.any(slot_tile[None, :] == tiles[:, None], axis=1).astype(jnp.float32)
    count = lax.axis_size("rows")
    me = lax.axis_index("rows")
    has = jnp.stack([me > 0, me < count - 1]).astype(jnp.float32)
    flags = jnp.concatenate([keep, has])
    gain = norm_gain[:, None]
    w = conv_weight.reshape(9, 3 * C, C)
    uw = up_weight.reshape(3, 3 * C2, C)

    steps = lax.axis_size("tm")
    previous = lax.ppermute(latents, "tm", [(i, i + 1) for i in range(steps - 1)])
    f32 = jnp.float32
    part = jax.ShapeDtypeStruct((2, 4, C, 2 * W), f32)
    half = jax.ShapeDtypeStruct((2, 2, C, 2 * W), jnp.bfloat16)
    s1 = call(own_kernel, part, 3, 1_020_000_000)(latents, gain, w)
    s, up, down = call(previous_kernel, (part, half, half), 4, 1_020_000_000)(previous, gain, w, s1)
    ring = [(i, (i + 1) % count) for i in range(count)]
    above = lax.ppermute(down, "rows", ring)
    below = lax.ppermute(up, "rows", [(j, i) for i, j in ring])
    out = jax.ShapeDtypeStruct((own_tiles, frames, 2 * rows, C2, 2 * W), jnp.bfloat16)
    return call(upsample_kernel, out, 5, 900_000_000, True)(flags, s, above, below, uw)


def solution(mesh):
    placed = (P("dp", "tm", "rows", None, None), P(), P(), P(), P())
    return jax.shard_map(
        on_device,
        mesh=mesh,
        in_specs=placed,
        out_specs=P("dp", "tm", "rows", None, None),
        check_vma=False,
    )
```

time: 77.5 us -> 29.4 us (0.38)
  the two profiles are of different devices: /device:TPU:110 before, /device:TPU:119 now
where the time goes in v1:
time: 29.4 us; the launch traced here: 29.2 us
  waiting for transfers between devices  10.8 us (37%)
  Pallas kernels  7.72 us (26%)
  starting transfers between devices  6.77 us (23%)
  local copies, waits for them, and re-layouts  3.55 us (12%)
    ppermute x1, waiting for transfers between devices, on_device(): above = lax.ppermute(down, 'rows', ring)  9.35 us
    ppermute x1, starting transfers between devices, on_device(): lax.ppermute(latents, 'tm', [(i, i + 1) for i in range(steps - 1)])  5.31 us
    pallas_call x1, Pallas kernels, on_device(): call(upsample_kernel, out, 5, 900000000, True)(flags, s, above, below, uw)  3.42 us
    unnamed x10, local copies, waits for them, and re-layouts  2.76 us
    pallas_call x1, Pallas kernels, on_device(): call(previous_kernel, (part, half, half), 4, 1020000000)  2.53 us
    pallas_call x1, Pallas kernels, on_device(): s1 = call(own_kernel, part, 3, 1020000000)(latents, gain, w)  1.77 us
    ppermute x1, waiting for transfers between devices, on_device(): below = lax.ppermute(up, 'rows', [(j, i) for i, j in ring])  1.43 us
    ppermute x1, starting transfers between devices, on_device(): below = lax.ppermute(up, 'rows', [(j, i) for i, j in ring])  1.27 us
  transfers between devices with their start and end apart: 3, of which 2 were waited for; matrix products, arithmetic and copies ran while one was open for 4% of the time, Pallas kernels for 6%

profile of v1, /device:TPU:119, one launch (start us, length us, event | category | flops | bytes accessed | tf_op | source)
XLA Modules:
  0.0 29.2 jit_solution(16481716616116398165)
XLA Ops:
  0.0 5.3 %collective-permute-start = (bf16[2,2,2,192,128]{4,3,2,1,0:T(8,128)(2,1)}, bf16[2,2,2,192,128]{4,3,2,1,0:T(8,128)(2,1)S(1)}, u32[]{:S(2)}, u32[]{:S(2)}) collective-permute-start(bf16[2,2,2,192,128]{4,3,2,1,0:T(8,128)(2,1)} %x_ref.1), channel_id=1, source_target_pairs={{0,4},{4,8},{8,12},{12,16},{16,20},{20,24},{24,28},{28,32},{32,36}... | collective-permute-start | bytes 1179656 | tf_op jit(solution)/shard_map/ppermute | solution.py:138
  5.3 0.8 %copy.9.gain_ref = f32[192,1]{1,0:T(8,128)S(1)} copy(f32[192,1]{0,1:T(1,128)} %bitcast.8) | data formatting | bytes 1536 | tf_op jit(solution)/shard_map/broadcast_in_dim | solution.py:133
  6.1 0.0 copy-start
  6.1 1.7 %copy-done = bf16[3,3,3,192,192]{4,3,2,1,0:T(8,128)(2,1)S(1)} copy-done((bf16[3,3,3,192,192]{4,3,2,1,0:T(8,128)(2,1)S(1)}, bf16[3,3,3,192,192]{4,3,2,1,0:T(8,128)(2,1)}, u32[]{:S(2)}) %copy-start) | copy-done | bytes 1990680
  7.9 0.0 copy-start.3
  7.9 1.0 %copy-done.3 = bf16[2,2,2,192,128]{4,3,2,1,0:T(8,128)(2,1)S(1)} copy-done((bf16[2,2,2,192,128]{4,3,2,1,0:T(8,128)(2,1)S(1)}, bf16[2,2,2,192,128]{4,3,2,1,0:T(8,128)(2,1)}, u32[]{:S(2)}) %copy-start.3) | copy-done | bytes 393240
  8.9 0.0 copy-start.1
  8.9 1.8 %shard_map.55.s1_ref = f32[2,4,192,256]{3,2,1,0:T(8,128)S(1)} custom-call(bf16[2,2,2,192,128]{4,3,2,1,0:T(8,128)(2,1)S(1)} %copy-done.3, f32[192,1]{1,0:T(8,128)S(1)} %copy.9.gain_ref, bf16[9,576,192]{2,1,0:T(8,128)(2,1)S(1)} %bitcast.5), custom_call_target="tpu_custom_call" | custom-call | flops 1020000000 | bytes 4000000 | tf_op jit(solution)/shard_map/pallas_call | solution.py:142
  10.6 0.0 copy-start.4
  10.7 0.0 copy-start.2
  10.7 0.0 collective-permute-done.x_ref
  10.7 0.0 copy-done.1
  10.7 2.5 %shard_map.56 = (f32[2,4,192,256]{3,2,1,0:T(8,128)S(1)}, bf16[2,2,192,256]{3,2,1,0:T(8,128)(2,1)S(1)}, bf16[2,2,192,256]{3,2,1,0:T(8,128)(2,1)}) custom-call(bf16[2,2,2,192,128]{4,3,2,1,0:T(8,128)(2,1)S(1)} %collective-permute-done.x_ref, f32[192,1]{1,0:T(8,128)S(1)} %copy.9.gain_ref, bf16[9,576,192]{2,1,0:T(8,128)(2,1)S(1)} %bitcast.6, ...), custom_call_target="tpu_custom_call" | custom-call | flops 1020000000 | bytes 4000000 | tf_op jit(solution)/shard_map/pallas_call | solution.py:143
  13.2 0.2 collective-permute-start.1
  13.4 1.3 %collective-permute-start.2 = (bf16[2,2,192,256]{3,2,1,0:T(8,128)(2,1)S(1)}, bf16[2,2,192,256]{3,2,1,0:T(8,128)(2,1)S(1)}, u32[]{:S(2)}, u32[]{:S(2)}) collective-permute-start(bf16[2,2,192,256]{3,2,1,0:T(8,128)(2,1)S(1)} %get-tuple-element.10), channel_id=1, source_target_pairs={{1,0},{2,1},{3,2},{0,3},{5,4},{6,5},{7,6},{4,7},{9,8},{10,9},{11,1... | collective-permute-start | bytes 1179656 | tf_op jit(solution)/shard_map/ppermute | solution.py:146
  14.7 0.0 copy-done.4
  14.7 0.2 compare_reduce_fusion
  14.9 0.1 add_convert_fusion.flag_ref
  15.0 9.4 %collective-permute-done.1.above_ref = bf16[2,2,192,256]{3,2,1,0:T(8,128)(2,1)S(1)} collective-permute-done((bf16[2,2,192,256]{3,2,1,0:T(8,128)(2,1)}, bf16[2,2,192,256]{3,2,1,0:T(8,128)(2,1)S(1)}, u32[]{:S(2)}, u32[]{:S(2)}) %collective-permute-start.1) | collective-permute-done | bytes 393248 | tf_op jit(solution)/shard_map/ppermute | solution.py:145
  24.3 1.4 %collective-permute-done.2.below_ref = bf16[2,2,192,256]{3,2,1,0:T(8,128)(2,1)S(1)} collective-permute-done((bf16[2,2,192,256]{3,2,1,0:T(8,128)(2,1)S(1)}, bf16[2,2,192,256]{3,2,1,0:T(8,128)(2,1)S(1)}, u32[]{:S(2)}, u32[]{:S(2)}) %collective-permute-start.2) | collective-permute-done | bytes 393248 | tf_op jit(solution)/shard_map/ppermute | solution.py:146
  25.7 0.0 copy-done.2
  25.7 3.4 %shard_map.57 = bf16[2,2,4,96,256]{4,3,2,1,0:T(8,128)(2,1)} custom-call(f32[4]{0:T(128)S(1)} %add_convert_fusion.flag_ref, f32[2,4,192,256]{3,2,1,0:T(8,128)S(1)} %get-tuple-element.8.s_ref, bf16[2,2,192,256]{3,2,1,0:T(8,128)(2,1)S(1)} %collective-permute-done.1.above_ref, bf16[2,2,192,256]{3,2,1,0:T(8,128)(2,1)S(1)} %collective-permute-done.2.below_ref, ...), custom_call_target="tpu_custom_call" | custom-call | flops 900000000 | bytes 4000000 | tf_op jit(solution)/shard_map/pallas_call | solution.py:148
  (1 shorter events, 0.0 us)
Async XLA Ops:
  0.0 10.7 %collective-permute-start = (bf16[2,2,2,192,128]{4,3,2,1,0:T(8,128)(2,1)}, bf16[2,2,2,192,128]{4,3,2,1,0:T(8,128)(2,1)S(1)}, u32[]{:S(2)}, u32[]{:S(2)}) collective-permute-start(bf16[2,2,2,192,128]{4,3,2,1,0:T(8,128)(2,1)} %x_ref.1), channel_id=1, source_target_pairs={{0,4},{4,8},{8,12},{12,16},{16,20},{20,24},{24,28},{28,32},{32,36}... | collective-permute-start | bytes 1179656 | tf_op jit(solution)/shard_map/ppermute | solution.py:138
  6.1 1.8 %copy-start = (bf16[3,3,3,192,192]{4,3,2,1,0:T(8,128)(2,1)S(1)}, bf16[3,3,3,192,192]{4,3,2,1,0:T(8,128)(2,1)}, u32[]{:S(2)}) copy-start(bf16[3,3,3,192,192]{4,3,2,1,0:T(8,128)(2,1)} %param.8) | copy-start | bytes 5971972
  7.9 1.0 %copy-start.3 = (bf16[2,2,2,192,128]{4,3,2,1,0:T(8,128)(2,1)S(1)}, bf16[2,2,2,192,128]{4,3,2,1,0:T(8,128)(2,1)}, u32[]{:S(2)}) copy-start(bf16[2,2,2,192,128]{4,3,2,1,0:T(8,128)(2,1)} %x_ref.1) | copy-start | bytes 1179652
  8.9 1.8 %copy-start.1 = (bf16[3,3,3,192,192]{4,3,2,1,0:T(8,128)(2,1)S(1)}, bf16[3,3,3,192,192]{4,3,2,1,0:T(8,128)(2,1)}, u32[]{:S(2)}) copy-start(bf16[3,3,3,192,192]{4,3,2,1,0:T(8,128)(2,1)} %param.8) | copy-start | bytes 5971972
  10.6 4.0 %copy-start.4 = (s32[4]{0:T(128)S(1)}, s32[4]{0:T(128)}, u32[]{:S(2)}) copy-start(s32[4]{0:T(128)} %param.6) | copy-start | bytes 52
  10.7 15.1 %copy-start.2 = (bf16[3,3,96,192]{3,2,1,0:T(8,128)(2,1)S(1)}, bf16[3,3,96,192]{3,2,1,0:T(8,128)(2,1)}, u32[]{:S(2)}) copy-start(bf16[3,3,96,192]{3,2,1,0:T(8,128)(2,1)} %param.9) | copy-start | bytes 995332
  13.2 11.1 %collective-permute-start.1 = (bf16[2,2,192,256]{3,2,1,0:T(8,128)(2,1)}, bf16[2,2,192,256]{3,2,1,0:T(8,128)(2,1)S(1)}, u32[]{:S(2)}, u32[]{:S(2)}) collective-permute-start(bf16[2,2,192,256]{3,2,1,0:T(8,128)(2,1)} %get-tuple-element.9), channel_id=1, source_target_pairs={{0,1},{1,2},{2,3},{3,0},{4,5},{5,6},{6,7},{7,4},{8,9},{9,10},{10,1... | collective-permute-start | bytes 1179656 | tf_op jit(solution)/shard_map/ppermute | solution.py:145
  13.4 12.3 %collective-permute-start.2 = (bf16[2,2,192,256]{3,2,1,0:T(8,128)(2,1)S(1)}, bf16[2,2,192,256]{3,2,1,0:T(8,128)(2,1)S(1)}, u32[]{:S(2)}, u32[]{:S(2)}) collective-permute-start(bf16[2,2,192,256]{3,2,1,0:T(8,128)(2,1)S(1)} %get-tuple-element.10), channel_id=1, source_target_pairs={{1,0},{2,1},{3,2},{0,3},{5,4},{6,5},{7,6},{4,7},{9,8},{10,9},{11,1... | collective-permute-start | bytes 1179656 | tf_op jit(solution)/shard_map/ppermute | solution.py:146

commit v2 on v1

v2 whole, which is shorter than its diff:
```python
import functools

import jax
import jax.numpy as jnp
from jax import lax
from jax.experimental import pallas as pl
from jax.experimental.pallas import tpu as pltpu
from jax.sharding import PartitionSpec as P

C = 192
C2 = 96
W = 128
VMEM_LIMIT = 16 * 1024 * 1024
AXES = ("dp", "tm", "rows")


def activate(x, gain):
    meansq = jnp.mean(x * x, axis=0, keepdims=True)
    g = x * lax.rsqrt(meansq + 1e-06) * gain
    return (g * jax.nn.sigmoid(g)).astype(jnp.bfloat16)


def column(row):
    i = lax.broadcasted_iota(jnp.int32, (C, C), 0)
    j = lax.broadcasted_iota(jnp.int32, (C, C), 1)
    return jnp.sum(jnp.where(i == j, row, 0.0), axis=1, keepdims=True)


def pair(ref, frame, row):
    return jnp.concatenate([ref[0, frame, row], ref[1, frame, row]], axis=1)


def shifted(p, by):
    lane = lax.broadcasted_iota(jnp.int32, (p.shape[0], W), 1)
    edge = 0 if by == 1 else W - 1
    halves = []
    for t in range(2):
        moved = pltpu.roll(p[:, t * W : (t + 1) * W], by % W, 1)
        halves.append(jnp.where(lane == edge, 0.0, moved))
    return jnp.concatenate(halves, axis=1)


def conv_terms(acts, w_ref, row_out):
    acc = None
    for kt, panels in acts:
        for row in range(2):
            kh = row - row_out + 2
            if 0 <= kh <= 2:
                term = jnp.dot(w_ref[kt * 3 + kh], panels[row], preferred_element_type=jnp.float32)
                acc = term if acc is None else acc + term
    return shifted(acc[:C], 1) + acc[C : 2 * C] + shifted(acc[2 * C :], -1)


def own_kernel(x_hbm, gain_hbm, w_hbm, uw_hbm, s_ref, w_ref, uw_ref, gain_ref, x_ref, sem, w_sem):
    copies = [
        pltpu.make_async_copy(x_hbm, x_ref, sem.at[0]),
        pltpu.make_async_copy(gain_hbm, gain_ref, sem.at[1]),
    ]
    order = [6, 7, 8, 3, 4, 5, 0, 1, 2]
    weights = {k: pltpu.make_async_copy(w_hbm.at[k], w_ref.at[k], w_sem.at[k]) for k in order}
    last = pltpu.make_async_copy(uw_hbm, uw_ref, sem.at[2])
    for copy in copies + [weights[k] for k in order] + [last]:
        copy.start()
    for copy in copies:
        copy.wait()
    gain = column(gain_ref[...])
    xs = [[pair(x_ref, f, r).astype(jnp.float32) for r in range(2)] for f in range(2)]
    a = [[activate(xs[f][r], gain) for r in range(2)] for f in range(2)]
    for k in order:
        weights[k].wait()
    for fo in range(2):
        for ro in range(4):
            total = conv_terms([(2 - (fo - fi), a[fi]) for fi in range(fo + 1)], w_ref, ro)
            if ro in (1, 2):
                total = total + xs[fo][ro - 1]
            s_ref[fo, ro] = total
    last.wait()


def previous_kernel(core, at_ref, x_ref, gain_ref, w_ref, s1_ref, *refs):
    s_ref, first_ref, second_ref = refs[-3:]
    tm, row = at_ref[1], at_ref[2]

    @pl.when(lax.rem(tm, 2) == core)
    def _():
        gain = column(gain_ref[...])
        a = [[activate(pair(x_ref, f, r).astype(jnp.float32), gain) for r in range(2)] for f in range(2)]
        a = [[jnp.where(tm > 0, p, jnp.zeros_like(p)) for p in ps] for ps in a]
        upper = lax.rem(row, 2) == 0
        for fo in range(2):
            acts = [(0, a[0]), (1, a[1])] if fo == 0 else [(0, a[1])]
            for k in range(2):
                sent = []
                for ro in (k, k + 2):
                    total = s1_ref[fo, ro] + conv_terms(acts, w_ref, ro)
                    s_ref[fo, ro] = total
                    sent.append(total.astype(jnp.bfloat16))
                first_ref[fo, k] = jnp.where(upper, sent[1], sent[0])
                second_ref[fo, k] = jnp.where(upper, sent[0], sent[1])


def upsample_kernel(core, rows, at_ref, slot_ref, s_ref, first_ref, second_ref, w_ref, *refs):
    out_ref, buf_ref, sem = refs[-3:]
    dp, tm, row = at_ref[0], at_ref[1], at_ref[2]

    @pl.when(lax.rem(tm, 2) == core)
    def _():
        upper = lax.rem(row, 2) == 0
        keep = []
        for t in range(2):
            tile = dp * 2 + t
            hit = slot_ref[0] == tile
            for i in range(1, slot_ref.shape[0]):
                hit = jnp.logical_or(hit, slot_ref[i] == tile)
            keep.append(jnp.where(hit, 1.0, 0.0))
        above_there = jnp.where(row > 0, 1.0, 0.0)
        below_there = jnp.where(row < rows - 1, 1.0, 0.0)
        src = lax.broadcasted_iota(jnp.int32, (2 * W, 2 * W), 0)
        dst = lax.broadcasted_iota(jnp.int32, (2 * W, 2 * W), 1)
        spread = (dst == jnp.where(src < W, 2 * src, 2 * (src - W) + 1)).astype(jnp.bfloat16)
        copies = []
        for f in range(2):
            hidden = []
            for ro in range(4):
                there = above_there if ro < 2 else below_there
                ways = first_ref[f, ro % 2], second_ref[f, ro % 2]
                got = jnp.where(upper == (ro >= 2), *ways).astype(jnp.float32)
                if ro in (0, 3):
                    total = (s_ref[f, ro] + got) * there
                else:
                    total = s_ref[f, ro] + got * there
                hidden.append(total.astype(jnp.bfloat16))
            taps = {}
            for ro, khs in ((0, (0,)), (1, (0, 1, 2)), (2, (0, 1, 2)), (3, (2,))):
                for kh in khs:
                    taps[kh, ro] = jnp.dot(w_ref[kh], hidden[ro], preferred_element_type=jnp.float32)
            for q in range(2):
                mid = taps[1, q + 1]
                for parity in range(2):
                    if parity == 0:
                        total = taps[0, q] + mid + taps[2, q + 1]
                    else:
                        total = taps[0, q + 1] + mid + taps[2, q + 2]
                    k0, k1, k2 = total[:C2], total[C2 : 2 * C2], total[2 * C2 :]
                    even = (shifted(k0, 1) + k1 + k2).astype(jnp.bfloat16)
                    odd = (k0 + k1 + shifted(k2, -1)).astype(jnp.bfloat16)
                    for t in range(2):
                        both = jnp.concatenate([even[:, t * W : (t + 1) * W], odd[:, t * W : (t + 1) * W]], axis=1)
                        wide = jnp.dot(both, spread, preferred_element_type=jnp.float32)
                        buf_ref[f, t, 2 * q + parity] = (wide * keep[t]).astype(jnp.bfloat16)
            for t in range(2):
                copy = pltpu.make_async_copy(buf_ref.at[f, t], out_ref.at[t, f], sem.at[f, t])
                copy.start()
                copies.append(copy)
        for copy in copies:
            copy.wait()


SMEM = pl.BlockSpec(memory_space=pltpu.SMEM)
VMEM = pl.BlockSpec(memory_space=pltpu.VMEM)
ANY = pl.BlockSpec(memory_space=pl.ANY)
HBM = pl.BlockSpec(memory_space=pltpu.HBM)


def call(kernel, out_shape, in_specs, flops, out_spec=VMEM, **more):
    out_specs = jax.tree.map(lambda _: out_spec, out_shape)
    return pl.pallas_call(
        kernel,
        out_shape=out_shape,
        in_specs=in_specs,
        out_specs=out_specs,
        compiler_params=pltpu.CompilerParams(vmem_limit_bytes=VMEM_LIMIT),
        cost_estimate=pl.CostEstimate(flops=flops, bytes_accessed=4_000_000, transcendentals=0),
        **more,
    )


def swap(value, partner):
    n_dp, n_tm, n_rows = (lax.axis_size(a) for a in AXES)

    def index(d, t, r):
        return (d * n_tm + t) * n_rows + r

    places = [(d, t, r) for d in range(n_dp) for t in range(n_tm) for r in range(n_rows)]
    return lax.ppermute(value, AXES, [(index(*p), index(*partner(*p))) for p in places])


def on_device(latents, slot_tile, norm_gain, conv_weight, up_weight):
    own_tiles, frames, rows = latents.shape[:3]
    n_dp, n_tm, n_rows = (lax.axis_size(a) for a in AXES)
    at = jnp.stack([lax.axis_index(a) for a in AXES]).astype(jnp.int32)
    gain = norm_gain.reshape(1, C)
    w = conv_weight.reshape(9, 3 * C, C)
    uw = up_weight.reshape(3, 3 * C2, C)

    def idle(phase):
        return lambda d: (d ^ 1) if phase == 0 else ((d + 1) % n_dp if d % 2 else (d - 1) % n_dp)

    def across_chips(d, t, r):
        if t in (0, n_tm - 1):
            return idle(0)(d), t, r
        return d, (t + 1 if t % 2 else t - 1), r

    def rows_swap(phase, core):
        def partner(d, t, r):
            if t % 2 != core:
                return idle(phase)(d), t, r
            if phase == 0:
                return d, t, r ^ 1
            return d, t, ((r + 1) % n_rows if r % 2 else (r - 1) % n_rows)

        return partner

    part = jax.ShapeDtypeStruct((2, 4, C, 2 * W), jnp.float32)
    half = jax.ShapeDtypeStruct((2, 2, C, 2 * W), jnp.bfloat16)

    from_chip = swap(latents, lambda d, t, r: (d, t ^ 1, r))
    from_z = swap(latents, across_chips)
    s1, w, uw, gain = call(
        own_kernel,
        (part, *(jax.ShapeDtypeStruct(v.shape, v.dtype) for v in (w, uw, gain))),
        [HBM] * 4,
        1_020_000_000,
        scratch_shapes=[
            pltpu.VMEM(latents.shape, latents.dtype),
            pltpu.SemaphoreType.DMA((3,)),
            pltpu.SemaphoreType.DMA((9,)),
        ],
    )(*(pltpu.with_memory_space_constraint(v, pltpu.HBM) for v in (latents, gain, w, uw)))
    specs = [SMEM] + [VMEM] * 4
    s, odd1, odd2 = call(
        functools.partial(previous_kernel, 1), (part, half, half), specs, 1_020_000_000
    )(at, from_chip, gain, w, s1)
    odd1 = swap(odd1, rows_swap(0, 1))
    odd2 = swap(odd2, rows_swap(1, 1))
    s, even1, even2 = call(
        functools.partial(previous_kernel, 0),
        (part, half, half),
        specs + [VMEM],
        1_020_000_000,
        input_output_aliases={5: 0},
    )(at, from_z, gain, w, s1, s)
    even1 = swap(even1, rows_swap(0, 0))
    even2 = swap(even2, rows_swap(1, 0))
    out = jax.ShapeDtypeStruct((own_tiles, frames, 2 * rows, C2, 2 * W), jnp.bfloat16)
    scratch = [pltpu.VMEM((2, 2, 2 * rows, C2, 2 * W), jnp.bfloat16), pltpu.SemaphoreType.DMA((2, 2))]
    specs = [SMEM, SMEM] + [VMEM] * 4
    pixels = call(
        functools.partial(upsample_kernel, 1, n_rows), out, specs, 9_000_000_000, ANY, scratch_shapes=scratch
    )(at, slot_tile, s, odd1, odd2, uw)
    return call(
        functools.partial(upsample_kernel, 0, n_rows),
        out,
        specs + [ANY],
        900_000_000,
        ANY,
        scratch_shapes=scratch,
        input_output_aliases={6: 0},
    )(at, slot_tile, s, even1, even2, uw, pixels)


def solution(mesh):
    placed = (P("dp", "tm", "rows", None, None), P(), P(), P(), P())
    return jax.shard_map(
        on_device,
        mesh=mesh,
        in_specs=placed,
        out_specs=P("dp", "tm", "rows", None, None),
        check_vma=False,
    )
```

time: 29.4 us -> 26.4 us (0.90)
  the two profiles are of different devices: /device:TPU:119 before, /device:TPU:120 now
where the time goes in v2:
time: 26.4 us
  Pallas kernels  10.6 us (40%)
  waiting for transfers between devices  9.83 us (37%)
  starting transfers between devices  5.78 us (22%)
    ppermute x6, waiting for transfers between devices, swap(): lax.ppermute(value, AXES, [(index(*p), index(*partner(*p))) for p in plac...  9.83 us
    ppermute x6, starting transfers between devices, swap(): lax.ppermute(value, AXES, [(index(*p), index(*partner(*p))) for p in plac...  5.78 us
    pallas_call x1, Pallas kernels, on_device(): call(own_kernel, (part, *(jax.ShapeDtypeStruct(v.shape, v.dtype) for v in...  3.64 us
    pallas_call x1, Pallas kernels, on_device(): call(functools.partial(upsample_kernel, 0, n_rows), out, specs + [ANY], 9...  3.41 us
    pallas_call x1, Pallas kernels, on_device(): call(functools.partial(previous_kernel, 0), (part, half, half), specs + [...  2.43 us
    pallas_call x1, Pallas kernels, on_device(): call(functools.partial(upsample_kernel, 1, n_rows), out, specs, 900000000...  0.59 us
    pallas_call x1, Pallas kernels, on_device(): call(functools.partial(previous_kernel, 1), (part, half, half), specs, 10...  0.55 us
  transfers between devices with their start and end apart: 6, of which 4 were waited for; matrix products, arithmetic and copies ran while one was open for 0% of the time, Pallas kernels for 27%

profile of v2, /device:TPU:120, one launch (start us, length us, event | category | flops | bytes accessed | tf_op | source)
XLA Modules:
  0.0 26.4 jit_solution(8113688093739111564)
XLA Ops:
  0.0 0.0 collective-permute-start.1
  0.0 0.2 collective-permute-start
  0.2 3.6 %shard_map.55 = (f32[2,4,192,256]{3,2,1,0:T(8,128)S(1)}, bf16[9,576,192]{2,1,0:T(8,128)(2,1)S(1)}, bf16[3,288,192]{2,1,0:T(8,128)(2,1)S(1)}, f32[1,192]{1,0:T(1,128)S(1)}) custom-call(bf16[2,2,2,192,128]{4,3,2,1,0:T(8,128)(2,1)} %x_hbm.1, f32[1,192]{1,0:T(1,128)} %bitcast.8, bf16[9,576,192]{2,1,0:T(8,128)(2,1)} %bitcast.6, bf16[3,288,192]{2,1,0:T(8,128)(2,1)} %bitcast.7), custom_call_target="tpu_custom_call" | custom-call | flops 1020000000 | bytes 4000000 | tf_op jit(solution)/shard_map/pallas_call | solution.py:219
  3.9 0.1 pad_add_fusion.at_ref
  4.0 0.0 collective-permute-done.1.x_ref
  4.0 0.6 %shard_map.56 = (f32[2,4,192,256]{3,2,1,0:T(8,128)S(1)}, bf16[2,2,192,256]{3,2,1,0:T(8,128)(2,1)S(1)}, bf16[2,2,192,256]{3,2,1,0:T(8,128)(2,1)S(1)}) custom-call(s32[3]{0:T(128)S(1)} %pad_add_fusion.at_ref, bf16[2,2,2,192,128]{4,3,2,1,0:T(8,128)(2,1)S(1)} %collective-permute-done.1.x_ref, f32[1,192]{1,0:T(1,128)S(1)} %get-tuple-element.15.gain_ref, ...), custom_call_target="tpu_custom_call" | custom-call | flops 1020000000 | bytes 4000000 | tf_op jit(solution)/shard_map/pallas_call | solution.py:231
  4.5 0.8 %collective-permute-start.4 = (bf16[2,2,192,256]{3,2,1,0:T(8,128)(2,1)S(1)}, bf16[2,2,192,256]{3,2,1,0:T(8,128)(2,1)S(1)}, u32[]{:S(2)}, u32[]{:S(2)}) collective-permute-start(bf16[2,2,192,256]{3,2,1,0:T(8,128)(2,1)S(1)} %get-tuple-element.23), channel_id=1, source_target_pairs={{0,64},{1,65},{2,66},{3,67},{4,5},{5,4},{6,7},{7,6},{8,72},{9,73},... | collective-permute-start | bytes 1179656 | tf_op jit(solution)/shard_map/ppermute | solution.py:185
  5.3 1.1 %collective-permute-start.5 = (bf16[2,2,192,256]{3,2,1,0:T(8,128)(2,1)S(1)}, bf16[2,2,192,256]{3,2,1,0:T(8,128)(2,1)S(1)}, u32[]{:S(2)}, u32[]{:S(2)}) collective-permute-start(bf16[2,2,192,256]{3,2,1,0:T(8,128)(2,1)S(1)} %get-tuple-element.24), channel_id=1, source_target_pairs={{0,192},{1,193},{2,194},{3,195},{4,7},{5,6},{6,5},{7,4},{8,200},{9... | collective-permute-start | bytes 1179656 | tf_op jit(solution)/shard_map/ppermute | solution.py:185
  6.4 1.0 %collective-permute-done.x_ref = bf16[2,2,2,192,128]{4,3,2,1,0:T(8,128)(2,1)S(1)} collective-permute-done((bf16[2,2,2,192,128]{4,3,2,1,0:T(8,128)(2,1)}, bf16[2,2,2,192,128]{4,3,2,1,0:T(8,128)(2,1)S(1)}, u32[]{:S(2)}, u32[]{:S(2)}) %collective-permute-start) | collective-permute-done | bytes 393248 | tf_op jit(solution)/shard_map/ppermute | solution.py:185
  7.4 0.0 copy-start
  7.4 2.4 %shard_map.57 = (f32[2,4,192,256]{3,2,1,0:T(8,128)S(1)}, bf16[2,2,192,256]{3,2,1,0:T(8,128)(2,1)S(1)}, bf16[2,2,192,256]{3,2,1,0:T(8,128)(2,1)S(1)}) custom-call(s32[3]{0:T(128)S(1)} %pad_add_fusion.at_ref, bf16[2,2,2,192,128]{4,3,2,1,0:T(8,128)(2,1)S(1)} %collective-permute-done.x_ref, ...), custom_call_target="tpu_custom_call", output_to_operand_aliasing={{0}: (5, {})} | custom-call | flops 1020000000 | bytes 4000000 | tf_op jit(solution)/shard_map/pallas_call | solution.py:236
  9.9 1.6 %collective-permute-start.2 = (bf16[2,2,192,256]{3,2,1,0:T(8,128)(2,1)S(1)}, bf16[2,2,192,256]{3,2,1,0:T(8,128)(2,1)S(1)}, u32[]{:S(2)}, u32[]{:S(2)}) collective-permute-start(bf16[2,2,192,256]{3,2,1,0:T(8,128)(2,1)S(1)} %get-tuple-element.20), channel_id=1, source_target_pairs={{0,1},{1,0},{2,3},{3,2},{4,68},{5,69},{6,70},{7,71},{8,9},{9,8},{1... | collective-permute-start | bytes 1179656 | tf_op jit(solution)/shard_map/ppermute | solution.py:185
  11.4 2.1 %collective-permute-start.3 = (bf16[2,2,192,256]{3,2,1,0:T(8,128)(2,1)S(1)}, bf16[2,2,192,256]{3,2,1,0:T(8,128)(2,1)S(1)}, u32[]{:S(2)}, u32[]{:S(2)}) collective-permute-start(bf16[2,2,192,256]{3,2,1,0:T(8,128)(2,1)S(1)} %get-tuple-element.21), channel_id=1, source_target_pairs={{0,3},{1,2},{2,1},{3,0},{4,196},{5,197},{6,198},{7,199},{8,11},{9,... | collective-permute-start | bytes 1179656 | tf_op jit(solution)/shard_map/ppermute | solution.py:185
  13.5 0.0 collective-permute-done.4.first_ref
  13.5 0.8 %collective-permute-done.5.second_ref = bf16[2,2,192,256]{3,2,1,0:T(8,128)(2,1)S(1)} collective-permute-done((bf16[2,2,192,256]{3,2,1,0:T(8,128)(2,1)S(1)}, bf16[2,2,192,256]{3,2,1,0:T(8,128)(2,1)S(1)}, u32[]{:S(2)}, u32[]{:S(2)}) %collective-permute-start.5) | collective-permute-done | bytes 393248 | tf_op jit(solution)/shard_map/ppermute | solution.py:185
  14.3 0.0 copy-done
  14.3 0.6 %shard_map.58.refs_0_ = bf16[2,2,4,96,256]{4,3,2,1,0:T(8,128)(2,1)} custom-call(s32[3]{0:T(128)S(1)} %pad_add_fusion.at_ref, s32[4]{0:T(128)S(1)} %copy-done, f32[2,4,192,256]{3,2,1,0:T(8,128)S(1)} %get-tuple-element.19.s_ref, bf16[2,2,192,256]{3,2,1,0:T(8,128)(2,1)S(1)} %collective-permute-done.4.first_ref, ...), custom_call_target="tpu_custom_call" | custom-call | flops 8999999488 | bytes 4000000 | tf_op jit(solution)/shard_map/pallas_call | solution.py:248
  14.9 5.6 %collective-permute-done.2.first_ref = bf16[2,2,192,256]{3,2,1,0:T(8,128)(2,1)S(1)} collective-permute-done((bf16[2,2,192,256]{3,2,1,0:T(8,128)(2,1)S(1)}, bf16[2,2,192,256]{3,2,1,0:T(8,128)(2,1)S(1)}, u32[]{:S(2)}, u32[]{:S(2)}) %collective-permute-start.2) | collective-permute-done | bytes 393248 | tf_op jit(solution)/shard_map/ppermute | solution.py:185
  20.5 2.4 %collective-permute-done.3.second_ref = bf16[2,2,192,256]{3,2,1,0:T(8,128)(2,1)S(1)} collective-permute-done((bf16[2,2,192,256]{3,2,1,0:T(8,128)(2,1)S(1)}, bf16[2,2,192,256]{3,2,1,0:T(8,128)(2,1)S(1)}, u32[]{:S(2)}, u32[]{:S(2)}) %collective-permute-start.3) | collective-permute-done | bytes 393248 | tf_op jit(solution)/shard_map/ppermute | solution.py:185
  23.0 3.4 %shard_map.59 = bf16[2,2,4,96,256]{4,3,2,1,0:T(8,128)(2,1)} custom-call(s32[3]{0:T(128)S(1)} %pad_add_fusion.at_ref, s32[4]{0:T(128)S(1)} %copy-done, f32[2,4,192,256]{3,2,1,0:T(8,128)S(1)} %get-tuple-element.19.s_ref, bf16[2,2,192,256]{3,2,1,0:T(8,128)(2,1)S(1)} %collective-permute-done.2.first_ref, ...), custom_call_target="tpu_custom_call", output_to_operand_aliasing={{}: (6, {})} | custom-call | flops 900000000 | bytes 4000000 | tf_op jit(solution)/shard_map/pallas_call | solution.py:251
Async XLA Ops:
  0.0 4.0 %collective-permute-start.1 = (bf16[2,2,2,192,128]{4,3,2,1,0:T(8,128)(2,1)}, bf16[2,2,2,192,128]{4,3,2,1,0:T(8,128)(2,1)S(1)}, u32[]{:S(2)}, u32[]{:S(2)}) collective-permute-start(bf16[2,2,2,192,128]{4,3,2,1,0:T(8,128)(2,1)} %x_hbm.1), channel_id=1, source_target_pairs={{0,4},{1,5},{2,6},{3,7},{4,0},{5,1},{6,2},{7,3},{8,12},{9,13},{10,... | collective-permute-start | bytes 1179656 | tf_op jit(solution)/shard_map/ppermute | solution.py:185
  0.0 7.4 %collective-permute-start = (bf16[2,2,2,192,128]{4,3,2,1,0:T(8,128)(2,1)}, bf16[2,2,2,192,128]{4,3,2,1,0:T(8,128)(2,1)S(1)}, u32[]{:S(2)}, u32[]{:S(2)}) collective-permute-start(bf16[2,2,2,192,128]{4,3,2,1,0:T(8,128)(2,1)} %x_hbm.1), channel_id=1, source_target_pairs={{0,64},{1,65},{2,66},{3,67},{4,8},{5,9},{6,10},{7,11},{8,4},{9,5},... | collective-permute-start | bytes 1179656 | tf_op jit(solution)/shard_map/ppermute | solution.py:185
  4.5 9.0 %collective-permute-start.4 = (bf16[2,2,192,256]{3,2,1,0:T(8,128)(2,1)S(1)}, bf16[2,2,192,256]{3,2,1,0:T(8,128)(2,1)S(1)}, u32[]{:S(2)}, u32[]{:S(2)}) collective-permute-start(bf16[2,2,192,256]{3,2,1,0:T(8,128)(2,1)S(1)} %get-tuple-element.23), channel_id=1, source_target_pairs={{0,64},{1,65},{2,66},{3,67},{4,5},{5,4},{6,7},{7,6},{8,72},{9,73},... | collective-permute-start | bytes 1179656 | tf_op jit(solution)/shard_map/ppermute | solution.py:185
  5.3 9.0 %collective-permute-start.5 = (bf16[2,2,192,256]{3,2,1,0:T(8,128)(2,1)S(1)}, bf16[2,2,192,256]{3,2,1,0:T(8,128)(2,1)S(1)}, u32[]{:S(2)}, u32[]{:S(2)}) collective-permute-start(bf16[2,2,192,256]{3,2,1,0:T(8,128)(2,1)S(1)} %get-tuple-element.24), channel_id=1, source_target_pairs={{0,192},{1,193},{2,194},{3,195},{4,7},{5,6},{6,5},{7,4},{8,200},{9... | collective-permute-start | bytes 1179656 | tf_op jit(solution)/shard_map/ppermute | solution.py:185
  7.4 6.9 %copy-start = (s32[4]{0:T(128)S(1)}, s32[4]{0:T(128)}, u32[]{:S(2)}) copy-start(s32[4]{0:T(128)} %slot_ref.3) | copy-start | bytes 52
  9.9 10.7 %collective-permute-start.2 = (bf16[2,2,192,256]{3,2,1,0:T(8,128)(2,1)S(1)}, bf16[2,2,192,256]{3,2,1,0:T(8,128)(2,1)S(1)}, u32[]{:S(2)}, u32[]{:S(2)}) collective-permute-start(bf16[2,2,192,256]{3,2,1,0:T(8,128)(2,1)S(1)} %get-tuple-element.20), channel_id=1, source_target_pairs={{0,1},{1,0},{2,3},{3,2},{4,68},{5,69},{6,70},{7,71},{8,9},{9,8},{1... | collective-permute-start | bytes 1179656 | tf_op jit(solution)/shard_map/ppermute | solution.py:185
  11.4 11.5 %collective-permute-start.3 = (bf16[2,2,192,256]{3,2,1,0:T(8,128)(2,1)S(1)}, bf16[2,2,192,256]{3,2,1,0:T(8,128)(2,1)S(1)}, u32[]{:S(2)}, u32[]{:S(2)}) collective-permute-start(bf16[2,2,192,256]{3,2,1,0:T(8,128)(2,1)S(1)} %get-tuple-element.21), channel_id=1, source_target_pairs={{0,3},{1,2},{2,1},{3,0},{4,196},{5,197},{6,198},{7,199},{8,11},{9,... | collective-permute-start | bytes 1179656 | tf_op jit(solution)/shard_map/ppermute | solution.py:185

commit v3 on v2

v3 whole, which is shorter than its diff:
```python
import functools

import jax
import jax.numpy as jnp
from jax import lax
from jax.experimental import pallas as pl
from jax.experimental.pallas import tpu as pltpu
from jax.sharding import PartitionSpec as P

C = 192
C2 = 96
W = 128
VMEM_LIMIT = 16 * 1024 * 1024
AXES = ("dp", "tm", "rows")


def activate(x, gain):
    meansq = jnp.mean(x * x, axis=0, keepdims=True)
    g = x * lax.rsqrt(meansq + 1e-06) * gain
    return (g * jax.nn.sigmoid(g)).astype(jnp.bfloat16)


def column(row):
    i = lax.broadcasted_iota(jnp.int32, (C, C), 0)
    j = lax.broadcasted_iota(jnp.int32, (C, C), 1)
    return jnp.sum(jnp.where(i == j, row, 0.0), axis=1, keepdims=True)


def pair(ref, frame, row):
    return jnp.concatenate([ref[0, frame, row], ref[1, frame, row]], axis=1)


def shifted(p, by):
    lane = lax.broadcasted_iota(jnp.int32, (p.shape[0], W), 1)
    edge = 0 if by == 1 else W - 1
    halves = []
    for t in range(2):
        moved = pltpu.roll(p[:, t * W : (t + 1) * W], by % W, 1)
        halves.append(jnp.where(lane == edge, 0.0, moved))
    return jnp.concatenate(halves, axis=1)


def conv_terms(acts, w_ref, row_out, flip):
    acc = None
    for kt, panels in acts:
        for row in range(2):
            kh = row - row_out + 2
            if 0 <= kh <= 2:
                tap = kt * 3 + jnp.where(flip, 2 - kh, kh)
                term = jnp.dot(w_ref[tap], panels[row], preferred_element_type=jnp.float32)
                acc = term if acc is None else acc + term
    return shifted(acc[:C], 1) + acc[C : 2 * C] + shifted(acc[2 * C :], -1)


def flipped():
    return lax.rem(lax.axis_index("rows"), 2) == 1


def panels(x_ref, flip):
    rows = [jnp.where(flip, 1 - r, r) for r in range(2)]
    return [[pair(x_ref, f, r).astype(jnp.float32) for r in rows] for f in range(2)]


def own_kernel(x_hbm, gain_hbm, w_hbm, uw_hbm, s_ref, w_ref, uw_ref, gain_ref, x_ref, sem, w_sem):
    copies = [
        pltpu.make_async_copy(x_hbm, x_ref, sem.at[0]),
        pltpu.make_async_copy(gain_hbm, gain_ref, sem.at[1]),
    ]
    order = [6, 7, 8, 3, 4, 5, 0, 1, 2]
    weights = {k: pltpu.make_async_copy(w_hbm.at[k], w_ref.at[k], w_sem.at[k]) for k in order}
    last = pltpu.make_async_copy(uw_hbm, uw_ref, sem.at[2])
    for copy in copies + [weights[k] for k in order] + [last]:
        copy.start()
    for copy in copies:
        copy.wait()
    flip = flipped()
    gain = column(gain_ref[...])
    xs = panels(x_ref, flip)
    a = [[activate(xs[f][r], gain) for r in range(2)] for f in range(2)]
    for fo in range(2):
        for k in ((6, 7, 8), (3, 4, 5))[fo]:
            weights[k].wait()
        for ro in range(4):
            total = conv_terms([(2 - (fo - fi), a[fi]) for fi in range(fo + 1)], w_ref, ro, flip)
            if ro in (1, 2):
                total = total + xs[fo][ro - 1]
            s_ref[fo, ro] = total
    for k in (0, 1, 2):
        weights[k].wait()
    last.wait()


def previous_kernel(core, x_ref, gain_ref, w_ref, s1_ref, uw_ref, *refs):
    s_ref, first_ref, second_ref, u_ref = refs[-4:]
    tm = lax.axis_index("tm")
    flip = flipped()

    @pl.when(lax.rem(tm, 2) == core)
    def _():
        gain = jnp.where(tm > 0, column(gain_ref[...]), 0.0)
        a = [[activate(x, gain) for x in xs] for xs in panels(x_ref, flip)]
        for fo in range(2):
            acts = [(0, a[0]), (1, a[1])] if fo == 0 else [(0, a[1])]
            for ro in range(4):
                total = s1_ref[fo, ro] + conv_terms(acts, w_ref, ro, flip)
                s_ref[fo, ro] = total
                to_ref = first_ref if ro >= 2 else second_ref
                to_ref[fo, ro % 2] = total.astype(jnp.bfloat16)

    @pl.when(lax.rem(tm, 2) != core)
    def _():
        w0, w1, w2 = (uw_ref[jnp.where(flip, 2 - kh, kh)].astype(jnp.float32) for kh in range(3))
        u_ref[0] = jnp.concatenate([w0, w1 + w2], axis=1).astype(jnp.bfloat16)
        u_ref[1] = jnp.concatenate([w0 + w1, w2], axis=1).astype(jnp.bfloat16)


def upsample_kernel(core, s_ref, first_ref, second_ref, u_ref, slot_ref, *refs):
    out_ref, h_ref, b_ref, buf_ref, sem = refs[-5:]
    row, rows = lax.axis_index("rows"), lax.axis_size("rows")

    @pl.when(lax.rem(lax.axis_index("tm"), 2) == core)
    def _():
        flip = flipped()
        src = lax.broadcasted_iota(jnp.int32, (2 * W, 2 * W), 0)
        dst = lax.broadcasted_iota(jnp.int32, (2 * W, 2 * W), 1)
        spread = (dst == jnp.where(src < W, 2 * src, 2 * (src - W) + 1)).astype(jnp.bfloat16)
        keep = []
        for t in range(2):
            hit = slot_ref[...] == lax.axis_index("dp") * 2 + t
            keep.append(jnp.max(jnp.where(hit, 1.0, 0.0), axis=1, keepdims=True))
        inside = jnp.where(jnp.logical_and(row > 0, row < rows - 1), 1.0, 0.0)
        copies = []
        for f in range(2):
            for ro in range(4):
                got = (first_ref if ro >= 2 else second_ref)[f, 1 - ro % 2].astype(jnp.float32)
                total = s_ref[f, ro]
                if ro == 0:
                    total = (total + got) * inside
                elif ro == 1:
                    total = total + got * inside
                else:
                    total = total + got
                h_ref[f, ro * C : (ro + 1) * C] = total.astype(jnp.bfloat16)
            for q in range(2):
                for parity in range(2):
                    low = (q + parity) * C
                    total = jnp.dot(u_ref[parity], h_ref[f, low : low + 2 * C], preferred_element_type=jnp.float32)
                    k0, k1, k2 = total[:C2], total[C2 : 2 * C2], total[2 * C2 :]
                    even = (shifted(k0, 1) + k1 + k2).astype(jnp.bfloat16)
                    odd = (k0 + k1 + shifted(k2, -1)).astype(jnp.bfloat16)
                    for t in range(2):
                        at = (t * 4 + 2 * q + parity) * C2
                        b_ref[f, at : at + C2, :W] = even[:, t * W : (t + 1) * W]
                        b_ref[f, at : at + C2, W:] = odd[:, t * W : (t + 1) * W]
            for t in range(2):
                wide = jnp.dot(b_ref[f, t * 4 * C2 : (t + 1) * 4 * C2], spread, preferred_element_type=jnp.float32)
                wide = (wide * keep[t]).astype(jnp.bfloat16)
                for at_row in range(4):
                    to_row = jnp.where(flip, 3 - at_row, at_row)
                    buf_ref[f, t, to_row] = wide[at_row * C2 : (at_row + 1) * C2]
                copy = pltpu.make_async_copy(buf_ref.at[f, t], out_ref.at[t, f], sem.at[f, t])
                copy.start()
                copies.append(copy)
        for copy in copies:
            copy.wait()


VMEM = pl.BlockSpec(memory_space=pltpu.VMEM)
ANY = pl.BlockSpec(memory_space=pl.ANY)
HBM = pl.BlockSpec(memory_space=pltpu.HBM)


def call(kernel, out_shape, in_specs, flops, out_spec=VMEM, **more):
    out_specs = jax.tree.map(lambda _: out_spec, out_shape)
    return pl.pallas_call(
        kernel,
        out_shape=out_shape,
        in_specs=in_specs,
        out_specs=out_specs,
        compiler_params=pltpu.CompilerParams(vmem_limit_bytes=VMEM_LIMIT),
        cost_estimate=pl.CostEstimate(flops=flops, bytes_accessed=4_000_000, transcendentals=0),
        **more,
    )


def swap(value, partner):
    n_dp, n_tm, n_rows = (lax.axis_size(a) for a in AXES)

    def index(d, t, r):
        return (d * n_tm + t) * n_rows + r

    places = [(d, t, r) for d in range(n_dp) for t in range(n_tm) for r in range(n_rows)]
    return lax.ppermute(value, AXES, [(index(*p), index(*partner(*p))) for p in places])


def on_device(latents, slot_tile, norm_gain, conv_weight, up_weight):
    own_tiles, frames, rows = latents.shape[:3]
    n_dp, n_tm, n_rows = (lax.axis_size(a) for a in AXES)
    slots = slot_tile.reshape(1, -1)
    gain = norm_gain.reshape(1, C)
    w = conv_weight.reshape(9, 3 * C, C)
    uw = up_weight.reshape(3, 3 * C2, C)

    def idle(phase):
        return lambda d: (d ^ 1) if phase == 0 else ((d + 1) % n_dp if d % 2 else (d - 1) % n_dp)

    def across_chips(d, t, r):
        if t in (0, n_tm - 1):
            return idle(0)(d), t, r
        return d, (t + 1 if t % 2 else t - 1), r

    def rows_swap(phase, core):
        def partner(d, t, r):
            if t % 2 != core:
                return idle(phase)(d), t, r
            if phase == 0:
                return d, t, r ^ 1
            return d, t, ((r + 1) % n_rows if r % 2 else (r - 1) % n_rows)

        return partner

    part = jax.ShapeDtypeStruct((2, 4, C, 2 * W), jnp.float32)
    half = jax.ShapeDtypeStruct((2, 2, C, 2 * W), jnp.bfloat16)

    from_chip = swap(latents, lambda d, t, r: (d, t ^ 1, r))
    from_z = swap(latents, across_chips)
    s1, w, uw, gain = call(
        own_kernel,
        (part, *(jax.ShapeDtypeStruct(v.shape, v.dtype) for v in (w, uw, gain))),
        [HBM] * 4,
        1_020_000_000,
        scratch_shapes=[
            pltpu.VMEM(latents.shape, latents.dtype),
            pltpu.SemaphoreType.DMA((3,)),
            pltpu.SemaphoreType.DMA((9,)),
        ],
    )(*(pltpu.with_memory_space_constraint(v, pltpu.HBM) for v in (latents, gain, w, uw)))
    specs = [VMEM] * 5
    wide = jax.ShapeDtypeStruct((2, 3 * C2, 2 * C), jnp.bfloat16)
    s, odd1, odd2, u = call(
        functools.partial(previous_kernel, 1), (part, half, half, wide), specs, 1_020_000_000
    )(from_chip, gain, w, s1, uw)
    odd1 = swap(odd1, rows_swap(0, 1))
    odd2 = swap(odd2, rows_swap(1, 1))
    s, even1, even2, u = call(
        functools.partial(previous_kernel, 0),
        (part, half, half, wide),
        specs + [VMEM] * 2,
        1_020_000_000,
        input_output_aliases={5: 0, 6: 3},
    )(from_z, gain, w, s1, uw, s, u)
    even1 = swap(even1, rows_swap(0, 0))
    even2 = swap(even2, rows_swap(1, 0))
    out = jax.ShapeDtypeStruct((own_tiles, frames, 2 * rows, C2, 2 * W), jnp.bfloat16)
    scratch = [
        pltpu.VMEM((2, 4 * C, 2 * W), jnp.bfloat16),
        pltpu.VMEM((2, 8 * C2, 2 * W), jnp.bfloat16),
        pltpu.VMEM((2, 2, 2 * rows, C2, 2 * W), jnp.bfloat16),
        pltpu.SemaphoreType.DMA((2, 2)),
    ]
    specs = [VMEM] * 5
    pixels = call(
        functools.partial(upsample_kernel, 1), out, specs, 9_000_000_000, ANY, scratch_shapes=scratch
    )(s, odd1, odd2, u, slots)
    return call(
        functools.partial(upsample_kernel, 0),
        out,
        specs + [ANY],
        900_000_000,
        ANY,
        scratch_shapes=scratch,
        input_output_aliases={5: 0},
    )(s, even1, even2, u, slots, pixels)


def solution(mesh):
    placed = (P("dp", "tm", "rows", None, None), P(), P(), P(), P())
    return jax.shard_map(
        on_device,
        mesh=mesh,
        in_specs=placed,
        out_specs=P("dp", "tm", "rows", None, None),
        check_vma=False,
    )
```

time: 26.4 us -> 24.8 us (0.939)
  the two profiles are of different devices: /device:TPU:120 before, /device:TPU:96 now
where the time goes in v3:
time: 24.8 us
  waiting for transfers between devices  8.81 us (36%)
  Pallas kernels  8.16 us (33%)
  starting transfers between devices  7.73 us (31%)
    ppermute x6, waiting for transfers between devices, swap(): lax.ppermute(value, AXES, [(index(*p), index(*partner(*p))) for p in plac...  8.81 us
    ppermute x6, starting transfers between devices, swap(): lax.ppermute(value, AXES, [(index(*p), index(*partner(*p))) for p in plac...  7.73 us
    pallas_call x1, Pallas kernels, on_device(): call(own_kernel, (part, *(jax.ShapeDtypeStruct(v.shape, v.dtype) for v in...  3.86 us
    pallas_call x1, Pallas kernels, on_device(): call(functools.partial(upsample_kernel, 0), out, specs + [ANY], 900000000...  2.23 us
    pallas_call x1, Pallas kernels, on_device(): call(functools.partial(previous_kernel, 0), (part, half, half, wide), spe...  1.85 us
  transfers between devices with their start and end apart: 6, of which 3 were waited for; matrix products, arithmetic and copies ran while one was open for 0% of the time, Pallas kernels for 24%

profile of v3, /device:TPU:96, one launch (start us, length us, event | category | flops | bytes accessed | tf_op | source)
XLA Modules:
  0.0 24.8 jit_solution(11875084234898829015)
XLA Ops:
  0.0 0.0 collective-permute-start.1
  0.0 0.2 collective-permute-start
  0.2 3.9 %shard_map.55 = (f32[2,4,192,256]{3,2,1,0:T(8,128)S(1)}, bf16[9,576,192]{2,1,0:T(8,128)(2,1)S(1)}, bf16[3,288,192]{2,1,0:T(8,128)(2,1)S(1)}, f32[1,192]{1,0:T(1,128)S(1)}) custom-call(bf16[2,2,2,192,128]{4,3,2,1,0:T(8,128)(2,1)} %x_hbm.1, f32[1,192]{1,0:T(1,128)} %bitcast.8, bf16[9,576,192]{2,1,0:T(8,128)(2,1)} %bitcast.6, bf16[3,288,192]{2,1,0:T(8,128)(2,1)} %bitcast.7), custom_call_target="tpu_custom_call" | custom-call | flops 1020000000 | bytes 4000000 | tf_op jit(solution)/shard_map/pallas_call | solution.py:227
  4.1 0.0 collective-permute-done.1.x_ref
  4.1 0.2 shard_map.56
  4.3 1.7 %collective-permute-start.4 = (bf16[2,2,192,256]{3,2,1,0:T(8,128)(2,1)S(1)}, bf16[2,2,192,256]{3,2,1,0:T(8,128)(2,1)S(1)}, u32[]{:S(2)}, u32[]{:S(2)}) collective-permute-start(bf16[2,2,192,256]{3,2,1,0:T(8,128)(2,1)S(1)} %get-tuple-element.27), channel_id=1, source_target_pairs={{0,64},{1,65},{2,66},{3,67},{4,5},{5,4},{6,7},{7,6},{8,72},{9,73},... | collective-permute-start | bytes 1179656 | tf_op jit(solution)/shard_map/ppermute | solution.py:193
  6.0 2.2 %collective-permute-start.5 = (bf16[2,2,192,256]{3,2,1,0:T(8,128)(2,1)S(1)}, bf16[2,2,192,256]{3,2,1,0:T(8,128)(2,1)S(1)}, u32[]{:S(2)}, u32[]{:S(2)}) collective-permute-start(bf16[2,2,192,256]{3,2,1,0:T(8,128)(2,1)S(1)} %get-tuple-element.28), channel_id=1, source_target_pairs={{0,192},{1,193},{2,194},{3,195},{4,7},{5,6},{6,5},{7,4},{8,200},{9... | collective-permute-start | bytes 1179656 | tf_op jit(solution)/shard_map/ppermute | solution.py:193
  8.1 0.0 collective-permute-done.x_ref
  8.1 0.0 copy-start
  8.2 1.8 %shard_map.57 = (f32[2,4,192,256]{3,2,1,0:T(8,128)S(1)}, bf16[2,2,192,256]{3,2,1,0:T(8,128)(2,1)S(1)}, bf16[2,2,192,256]{3,2,1,0:T(8,128)(2,1)S(1)}, bf16[2,288,384]{2,1,0:T(8,128)(2,1)S(1)}) custom-call(bf16[2,2,2,192,128]{4,3,2,1,0:T(8,128)(2,1)S(1)} %collective-permute-done.x_ref, ...), custom_call_target="tpu_custom_call", output_to_operand_aliasing={{0}: (5, {}), {3}: (6, {})} | custom-call | flops 1020000000 | bytes 4000000 | tf_op jit(solution)/shard_map/pallas_call | solution.py:245
  10.0 1.6 %collective-permute-start.2 = (bf16[2,2,192,256]{3,2,1,0:T(8,128)(2,1)S(1)}, bf16[2,2,192,256]{3,2,1,0:T(8,128)(2,1)S(1)}, u32[]{:S(2)}, u32[]{:S(2)}) collective-permute-start(bf16[2,2,192,256]{3,2,1,0:T(8,128)(2,1)S(1)} %get-tuple-element.24), channel_id=1, source_target_pairs={{0,1},{1,0},{2,3},{3,2},{4,68},{5,69},{6,70},{7,71},{8,9},{9,8},{1... | collective-permute-start | bytes 1179656 | tf_op jit(solution)/shard_map/ppermute | solution.py:193
  11.6 2.1 %collective-permute-start.3 = (bf16[2,2,192,256]{3,2,1,0:T(8,128)(2,1)S(1)}, bf16[2,2,192,256]{3,2,1,0:T(8,128)(2,1)S(1)}, u32[]{:S(2)}, u32[]{:S(2)}) collective-permute-start(bf16[2,2,192,256]{3,2,1,0:T(8,128)(2,1)S(1)} %get-tuple-element.25), channel_id=1, source_target_pairs={{0,3},{1,2},{2,1},{3,0},{4,196},{5,197},{6,198},{7,199},{8,11},{9,... | collective-permute-start | bytes 1179656 | tf_op jit(solution)/shard_map/ppermute | solution.py:193
  13.7 0.0 collective-permute-done.4.first_ref
  13.7 1.3 %collective-permute-done.5.second_ref = bf16[2,2,192,256]{3,2,1,0:T(8,128)(2,1)S(1)} collective-permute-done((bf16[2,2,192,256]{3,2,1,0:T(8,128)(2,1)S(1)}, bf16[2,2,192,256]{3,2,1,0:T(8,128)(2,1)S(1)}, u32[]{:S(2)}, u32[]{:S(2)}) %collective-permute-start.5) | collective-permute-done | bytes 393248 | tf_op jit(solution)/shard_map/ppermute | solution.py:193
  14.9 0.0 copy-done
  15.0 5.1 %collective-permute-done.2.first_ref = bf16[2,2,192,256]{3,2,1,0:T(8,128)(2,1)S(1)} collective-permute-done((bf16[2,2,192,256]{3,2,1,0:T(8,128)(2,1)S(1)}, bf16[2,2,192,256]{3,2,1,0:T(8,128)(2,1)S(1)}, u32[]{:S(2)}, u32[]{:S(2)}) %collective-permute-start.2) | collective-permute-done | bytes 393248 | tf_op jit(solution)/shard_map/ppermute | solution.py:193
  20.1 2.4 %collective-permute-done.3.second_ref = bf16[2,2,192,256]{3,2,1,0:T(8,128)(2,1)S(1)} collective-permute-done((bf16[2,2,192,256]{3,2,1,0:T(8,128)(2,1)S(1)}, bf16[2,2,192,256]{3,2,1,0:T(8,128)(2,1)S(1)}, u32[]{:S(2)}, u32[]{:S(2)}) %collective-permute-start.3) | collective-permute-done | bytes 393248 | tf_op jit(solution)/shard_map/ppermute | solution.py:193
  22.5 2.2 %shard_map.59 = bf16[2,2,4,96,256]{4,3,2,1,0:T(8,128)(2,1)} custom-call(f32[2,4,192,256]{3,2,1,0:T(8,128)S(1)} %get-tuple-element.23.s_ref, bf16[2,2,192,256]{3,2,1,0:T(8,128)(2,1)S(1)} %collective-permute-done.2.first_ref, bf16[2,2,192,256]{3,2,1,0:T(8,128)(2,1)S(1)} %collective-permute-done.3.second_ref, ...), custom_call_target="tpu_custom_call", output_to_operand_aliasing={{}: (5, {})} | custom-call | flops 900000000 | bytes 4000000 | tf_op jit(solution)/shard_map/pallas_call | solution.py:265
  (1 shorter events, 0.0 us)
Async XLA Ops:
  0.0 4.1 %collective-permute-start.1 = (bf16[2,2,2,192,128]{4,3,2,1,0:T(8,128)(2,1)}, bf16[2,2,2,192,128]{4,3,2,1,0:T(8,128)(2,1)S(1)}, u32[]{:S(2)}, u32[]{:S(2)}) collective-permute-start(bf16[2,2,2,192,128]{4,3,2,1,0:T(8,128)(2,1)} %x_hbm.1), channel_id=1, source_target_pairs={{0,4},{1,5},{2,6},{3,7},{4,0},{5,1},{6,2},{7,3},{8,12},{9,13},{10,... | collective-permute-start | bytes 1179656 | tf_op jit(solution)/shard_map/ppermute | solution.py:193
  0.0 8.1 %collective-permute-start = (bf16[2,2,2,192,128]{4,3,2,1,0:T(8,128)(2,1)}, bf16[2,2,2,192,128]{4,3,2,1,0:T(8,128)(2,1)S(1)}, u32[]{:S(2)}, u32[]{:S(2)}) collective-permute-start(bf16[2,2,2,192,128]{4,3,2,1,0:T(8,128)(2,1)} %x_hbm.1), channel_id=1, source_target_pairs={{0,64},{1,65},{2,66},{3,67},{4,8},{5,9},{6,10},{7,11},{8,4},{9,5},... | collective-permute-start | bytes 1179656 | tf_op jit(solution)/shard_map/ppermute | solution.py:193
  4.3 9.4 %collective-permute-start.4 = (bf16[2,2,192,256]{3,2,1,0:T(8,128)(2,1)S(1)}, bf16[2,2,192,256]{3,2,1,0:T(8,128)(2,1)S(1)}, u32[]{:S(2)}, u32[]{:S(2)}) collective-permute-start(bf16[2,2,192,256]{3,2,1,0:T(8,128)(2,1)S(1)} %get-tuple-element.27), channel_id=1, source_target_pairs={{0,64},{1,65},{2,66},{3,67},{4,5},{5,4},{6,7},{7,6},{8,72},{9,73},... | collective-permute-start | bytes 1179656 | tf_op jit(solution)/shard_map/ppermute | solution.py:193
  6.0 9.0 %collective-permute-start.5 = (bf16[2,2,192,256]{3,2,1,0:T(8,128)(2,1)S(1)}, bf16[2,2,192,256]{3,2,1,0:T(8,128)(2,1)S(1)}, u32[]{:S(2)}, u32[]{:S(2)}) collective-permute-start(bf16[2,2,192,256]{3,2,1,0:T(8,128)(2,1)S(1)} %get-tuple-element.28), channel_id=1, source_target_pairs={{0,192},{1,193},{2,194},{3,195},{4,7},{5,6},{6,5},{7,4},{8,200},{9... | collective-permute-start | bytes 1179656 | tf_op jit(solution)/shard_map/ppermute | solution.py:193
  8.1 6.8 %copy-start = (s32[4]{0:T(128)S(1)}, s32[4]{0:T(128)}, u32[]{:S(2)}) copy-start(s32[4]{0:T(128)} %param.6) | copy-start | bytes 52
  10.0 10.1 %collective-permute-start.2 = (bf16[2,2,192,256]{3,2,1,0:T(8,128)(2,1)S(1)}, bf16[2,2,192,256]{3,2,1,0:T(8,128)(2,1)S(1)}, u32[]{:S(2)}, u32[]{:S(2)}) collective-permute-start(bf16[2,2,192,256]{3,2,1,0:T(8,128)(2,1)S(1)} %get-tuple-element.24), channel_id=1, source_target_pairs={{0,1},{1,0},{2,3},{3,2},{4,68},{5,69},{6,70},{7,71},{8,9},{9,8},{1... | collective-permute-start | bytes 1179656 | tf_op jit(solution)/shard_map/ppermute | solution.py:193
  11.6 10.9 %collective-permute-start.3 = (bf16[2,2,192,256]{3,2,1,0:T(8,128)(2,1)S(1)}, bf16[2,2,192,256]{3,2,1,0:T(8,128)(2,1)S(1)}, u32[]{:S(2)}, u32[]{:S(2)}) collective-permute-start(bf16[2,2,192,256]{3,2,1,0:T(8,128)(2,1)S(1)} %get-tuple-element.25), channel_id=1, source_target_pairs={{0,3},{1,2},{2,1},{3,0},{4,196},{5,197},{6,198},{7,199},{8,11},{9,... | collective-permute-start | bytes 1179656 | tf_op jit(solution)/shard_map/ppermute | solution.py:193

commit v4 on v3

--- a/solution.py
+++ b/solution.py
@@ -61,33 +61,23 @@
     return [[pair(x_ref, f, r).astype(jnp.float32) for r in rows] for f in range(2)]
 
 
-def own_kernel(x_hbm, gain_hbm, w_hbm, uw_hbm, s_ref, w_ref, uw_ref, gain_ref, x_ref, sem, w_sem):
-    copies = [
-        pltpu.make_async_copy(x_hbm, x_ref, sem.at[0]),
-        pltpu.make_async_copy(gain_hbm, gain_ref, sem.at[1]),
-    ]
-    order = [6, 7, 8, 3, 4, 5, 0, 1, 2]
-    weights = {k: pltpu.make_async_copy(w_hbm.at[k], w_ref.at[k], w_sem.at[k]) for k in order}
-    last = pltpu.make_async_copy(uw_hbm, uw_ref, sem.at[2])
-    for copy in copies + [weights[k] for k in order] + [last]:
-        copy.start()
-    for copy in copies:
-        copy.wait()
+def spread_kernel(spread_ref):
+    src = lax.broadcasted_iota(jnp.int32, (2 * W, 2 * W), 0)
+    dst = lax.broadcasted_iota(jnp.int32, (2 * W, 2 * W), 1)
+    spread_ref[...] = (dst == jnp.where(src < W, 2 * src, 2 * (src - W) + 1)).astype(jnp.bfloat16)
+
+
+def own_kernel(x_ref, gain_ref, w_ref, spread_ref, s_ref, _):
     flip = flipped()
     gain = column(gain_ref[...])
     xs = panels(x_ref, flip)
     a = [[activate(xs[f][r], gain) for r in range(2)] for f in range(2)]
     for fo in range(2):
-        for k in ((6, 7, 8), (3, 4, 5))[fo]:
-            weights[k].wait()
         for ro in range(4):
             total = conv_terms([(2 - (fo - fi), a[fi]) for fi in range(fo + 1)], w_ref, ro, flip)
             if ro in (1, 2):
                 total = total + xs[fo][ro - 1]
             s_ref[fo, ro] = total
-    for k in (0, 1, 2):
-        weights[k].wait()
-    last.wait()
 
 
 def previous_kernel(core, x_ref, gain_ref, w_ref, s1_ref, uw_ref, *refs):
@@ -114,32 +104,36 @@
         u_ref[1] = jnp.concatenate([w0 + w1, w2], axis=1).astype(jnp.bfloat16)
 
 
-def upsample_kernel(core, s_ref, first_ref, second_ref, u_ref, slot_ref, *refs):
+def upsample_kernel(core, edge, s_ref, u_ref, slot_ref, spread_ref, first_ref, *refs):
     out_ref, h_ref, b_ref, buf_ref, sem = refs[-5:]
+    second_ref = refs[0]
     row, rows = lax.axis_index("rows"), lax.axis_size("rows")
-
-    @pl.when(lax.rem(lax.axis_index("tm"), 2) == core)
+    mine = lax.rem(lax.axis_index("tm"), 2) == core
+    at_edge = jnp.logical_or(row == 0, row == rows - 1)
+
+    if edge is not None:
+        mine = jnp.logical_and(mine, at_edge == edge)
+
+    @pl.when(mine)
     def _():
         flip = flipped()
-        src = lax.broadcasted_iota(jnp.int32, (2 * W, 2 * W), 0)
-        dst = lax.broadcasted_iota(jnp.int32, (2 * W, 2 * W), 1)
-        spread = (dst == jnp.where(src < W, 2 * src, 2 * (src - W) + 1)).astype(jnp.bfloat16)
+        spread = spread_ref[...]
         keep = []
         for t in range(2):
             hit = slot_ref[...] == lax.axis_index("dp") * 2 + t
             keep.append(jnp.max(jnp.where(hit, 1.0, 0.0), axis=1, keepdims=True))
-        inside = jnp.where(jnp.logical_and(row > 0, row < rows - 1), 1.0, 0.0)
         copies = []
         for f in range(2):
             for ro in range(4):
-                got = (first_ref if ro >= 2 else second_ref)[f, 1 - ro % 2].astype(jnp.float32)
                 total = s_ref[f, ro]
-                if ro == 0:
-                    total = (total + got) * inside
-                elif ro == 1:
-                    total = total + got * inside
-                else:
-                    total = total + got
+                if ro >= 2 or not edge:
+                    got = (first_ref if ro >= 2 else second_ref)[f, 1 - ro % 2]
+                    total = total + got.astype(jnp.float32)
+                if edge is None and ro < 2:
+                    alone = s_ref[f, ro] if ro == 1 else jnp.zeros_like(total)
+                    total = jnp.where(at_edge, alone, total)
+                elif edge and ro == 0:
+                    total = jnp.zeros_like(total)
                 h_ref[f, ro * C : (ro + 1) * C] = total.astype(jnp.bfloat16)
             for q in range(2):
                 for parity in range(2):
@@ -167,7 +161,6 @@
 
 VMEM = pl.BlockSpec(memory_space=pltpu.VMEM)
 ANY = pl.BlockSpec(memory_space=pl.ANY)
-HBM = pl.BlockSpec(memory_space=pltpu.HBM)
 
 
 def call(kernel, out_shape, in_specs, flops, out_spec=VMEM, **more):
@@ -224,17 +217,11 @@
 
     from_chip = swap(latents, lambda d, t, r: (d, t ^ 1, r))
     from_z = swap(latents, across_chips)
-    s1, w, uw, gain = call(
-        own_kernel,
-        (part, *(jax.ShapeDtypeStruct(v.shape, v.dtype) for v in (w, uw, gain))),
-        [HBM] * 4,
-        1_020_000_000,
-        scratch_shapes=[
-            pltpu.VMEM(latents.shape, latents.dtype),
-            pltpu.SemaphoreType.DMA((3,)),
-            pltpu.SemaphoreType.DMA((9,)),
-        ],
-    )(*(pltpu.with_memory_space_constraint(v, pltpu.HBM) for v in (latents, gain, w, uw)))
+    square = jax.ShapeDtypeStruct((2 * W, 2 * W), jnp.bfloat16)
+    spread = call(spread_kernel, square, [], 9_000_000_000)()
+    s1, spread = call(own_kernel, (part, square), [VMEM] * 4, 1_020_000_000, input_output_aliases={3: 1})(
+        latents, gain, w, spread
+    )
     specs = [VMEM] * 5
     wide = jax.ShapeDtypeStruct((2, 3 * C2, 2 * C), jnp.bfloat16)
     s, odd1, odd2, u = call(
@@ -258,19 +245,21 @@
         pltpu.VMEM((2, 2, 2 * rows, C2, 2 * W), jnp.bfloat16),
         pltpu.SemaphoreType.DMA((2, 2)),
     ]
-    specs = [VMEM] * 5
-    pixels = call(
-        functools.partial(upsample_kernel, 1), out, specs, 9_000_000_000, ANY, scratch_shapes=scratch
-    )(s, odd1, odd2, u, slots)
-    return call(
-        functools.partial(upsample_kernel, 0),
-        out,
-        specs + [ANY],
-        900_000_000,
-        ANY,
-        scratch_shapes=scratch,
-        input_output_aliases={5: 0},
-    )(s, even1, even2, u, slots, pixels)
+
+    def upsample(core, edge, first, second, pixels):
+        args = (s, u, slots, spread, first) + (() if edge else (second,))
+        specs = [VMEM] * len(args)
+        aliases = {}
+        if pixels is not None:
+            aliases = {len(args): 0}
+            args, specs = args + (pixels,), specs + [ANY]
+        flops = 9_000_000_000 if core else 900_000_000
+        kernel = functools.partial(upsample_kernel, core, edge)
+        return call(kernel, out, specs, flops, ANY, scratch_shapes=scratch, input_output_aliases=aliases)(*args)
+
+    pixels = upsample(1, None, odd1, odd2, None)
+    pixels = upsample(0, True, even1, even2, pixels)
+    return upsample(0, False, even1, even2, pixels)
 
 
 def solution(mesh):

time: 24.8 us -> 22.6 us (0.911)
  the two profiles are of different devices: /device:TPU:96 before, /device:TPU:2 now
where the time goes in v4:
time: 22.6 us; the launch traced here: 22.2 us
  starting transfers between devices  8.74 us (39%)
  waiting for transfers between devices  7.15 us (32%)
  Pallas kernels  6.22 us (28%)
    ppermute x6, starting transfers between devices, swap(): lax.ppermute(value, AXES, [(index(*p), index(*partner(*p))) for p in plac...  8.74 us
    ppermute x6, waiting for transfers between devices, swap(): lax.ppermute(value, AXES, [(index(*p), index(*partner(*p))) for p in plac...  7.15 us
    pallas_call x3, Pallas kernels, upsample(): call(kernel, out, specs, flops, ANY, scratch_shapes=scratch, input_output...  2.29 us
    pallas_call x1, Pallas kernels, on_device(): call(functools.partial(previous_kernel, 0), (part, half, half, wide), spe...  1.88 us
    pallas_call x1, Pallas kernels, on_device(): call(own_kernel, (part, square), [VMEM] * 4, 1020000000, input_output_ali...  1.83 us
  transfers between devices with their start and end apart: 6, of which 4 were waited for; matrix products, arithmetic and copies ran while one was open for 0% of the time, Pallas kernels for 18%

profile of v4, /device:TPU:2, one launch (start us, length us, event | category | flops | bytes accessed | tf_op | source)
XLA Modules:
  0.0 22.2 jit_solution(12476570670677774971)
XLA Ops:
  0.0 0.0 copy-start.4
  0.0 0.0 copy-start
  0.0 0.0 copy-start.2
  0.0 1.7 %collective-permute-start = (bf16[2,2,2,192,128]{4,3,2,1,0:T(8,128)(2,1)}, bf16[2,2,2,192,128]{4,3,2,1,0:T(8,128)(2,1)S(1)}, u32[]{:S(2)}, u32[]{:S(2)}) collective-permute-start(bf16[2,2,2,192,128]{4,3,2,1,0:T(8,128)(2,1)} %x_ref.1), channel_id=1, source_target_pairs={{0,64},{1,65},{2,66},{3,67},{4,8},{5,9},{6,10},{7,11},{8,4},{9,5},... | collective-permute-start | bytes 1179656 | tf_op jit(solution)/shard_map/ppermute | solution.py:186
  1.7 0.5 %collective-permute-start.1 = (bf16[2,2,2,192,128]{4,3,2,1,0:T(8,128)(2,1)}, bf16[2,2,2,192,128]{4,3,2,1,0:T(8,128)(2,1)S(1)}, u32[]{:S(2)}, u32[]{:S(2)}) collective-permute-start(bf16[2,2,2,192,128]{4,3,2,1,0:T(8,128)(2,1)} %x_ref.1), channel_id=1, source_target_pairs={{0,4},{1,5},{2,6},{3,7},{4,0},{5,1},{6,2},{7,3},{8,12},{9,13},{10,... | collective-permute-start | bytes 1179656 | tf_op jit(solution)/shard_map/ppermute | solution.py:186
  2.2 0.0 copy-done.4
  2.2 0.0 copy-done
  2.2 0.0 copy-done.2
  2.2 0.0 copy-start.1
  2.2 1.8 %shard_map.56 = (f32[2,4,192,256]{3,2,1,0:T(8,128)S(1)}, bf16[256,256]{1,0:T(8,128)(2,1)S(1)}) custom-call(bf16[2,2,2,192,128]{4,3,2,1,0:T(8,128)(2,1)S(1)} %copy-done.4, f32[1,192]{1,0:T(1,128)S(1)} %bitcast.9, bf16[9,576,192]{2,1,0:T(8,128)(2,1)S(1)} %bitcast.4, bf16[256,256]{1,0:T(8,128)(2,1)S(1)} %shard_map.55.spread_ref), custom_call_target="tpu_custom_call", output_to_operand_aliasing={{1}: (3, {})} | custom-call | flops 1020000000 | bytes 4000000 | tf_op jit(solution)/shard_map/pallas_call | solution.py:222
  4.0 0.0 collective-permute-done.1.x_ref
  4.1 0.0 copy-done.1
  4.1 0.2 shard_map.57
  4.3 1.7 %collective-permute-start.4 = (bf16[2,2,192,256]{3,2,1,0:T(8,128)(2,1)S(1)}, bf16[2,2,192,256]{3,2,1,0:T(8,128)(2,1)S(1)}, u32[]{:S(2)}, u32[]{:S(2)}) collective-permute-start(bf16[2,2,192,256]{3,2,1,0:T(8,128)(2,1)S(1)} %get-tuple-element.23), channel_id=1, source_target_pairs={{0,64},{1,65},{2,66},{3,67},{4,5},{5,4},{6,7},{7,6},{8,72},{9,73},... | collective-permute-start | bytes 1179656 | tf_op jit(solution)/shard_map/ppermute | solution.py:186
  5.9 2.2 %collective-permute-start.5 = (bf16[2,2,192,256]{3,2,1,0:T(8,128)(2,1)S(1)}, bf16[2,2,192,256]{3,2,1,0:T(8,128)(2,1)S(1)}, u32[]{:S(2)}, u32[]{:S(2)}) collective-permute-start(bf16[2,2,192,256]{3,2,1,0:T(8,128)(2,1)S(1)} %get-tuple-element.24), channel_id=1, source_target_pairs={{0,192},{1,193},{2,194},{3,195},{4,7},{5,6},{6,5},{7,4},{8,200},{9... | collective-permute-start | bytes 1179656 | tf_op jit(solution)/shard_map/ppermute | solution.py:186
  8.1 0.0 collective-permute-done.x_ref
  8.1 0.0 copy-start.3
  8.1 1.9 %shard_map.58 = (f32[2,4,192,256]{3,2,1,0:T(8,128)S(1)}, bf16[2,2,192,256]{3,2,1,0:T(8,128)(2,1)S(1)}, bf16[2,2,192,256]{3,2,1,0:T(8,128)(2,1)S(1)}, bf16[2,288,384]{2,1,0:T(8,128)(2,1)S(1)}) custom-call(bf16[2,2,2,192,128]{4,3,2,1,0:T(8,128)(2,1)S(1)} %collective-permute-done.x_ref, ...), custom_call_target="tpu_custom_call", output_to_operand_aliasing={{0}: (5, {}), {3}: (6, {})} | custom-call | flops 1020000000 | bytes 4000000 | tf_op jit(solution)/shard_map/pallas_call | solution.py:232
  10.0 2.2 %collective-permute-start.2 = (bf16[2,2,192,256]{3,2,1,0:T(8,128)(2,1)S(1)}, bf16[2,2,192,256]{3,2,1,0:T(8,128)(2,1)S(1)}, u32[]{:S(2)}, u32[]{:S(2)}) collective-permute-start(bf16[2,2,192,256]{3,2,1,0:T(8,128)(2,1)S(1)} %get-tuple-element.21), channel_id=1, source_target_pairs={{0,1},{1,0},{2,3},{3,2},{4,68},{5,69},{6,70},{7,71},{8,9},{9,8},{1... | collective-permute-start | bytes 1179656 | tf_op jit(solution)/shard_map/ppermute | solution.py:186
  12.2 0.5 %collective-permute-start.3 = (bf16[2,2,192,256]{3,2,1,0:T(8,128)(2,1)S(1)}, bf16[2,2,192,256]{3,2,1,0:T(8,128)(2,1)S(1)}, u32[]{:S(2)}, u32[]{:S(2)}) collective-permute-start(bf16[2,2,192,256]{3,2,1,0:T(8,128)(2,1)S(1)} %get-tuple-element.22), channel_id=1, source_target_pairs={{0,3},{1,2},{2,1},{3,0},{4,196},{5,197},{6,198},{7,199},{8,11},{9,... | collective-permute-start | bytes 1179656 | tf_op jit(solution)/shard_map/ppermute | solution.py:186
  12.8 0.7 %collective-permute-done.4.first_ref = bf16[2,2,192,256]{3,2,1,0:T(8,128)(2,1)S(1)} collective-permute-done((bf16[2,2,192,256]{3,2,1,0:T(8,128)(2,1)S(1)}, bf16[2,2,192,256]{3,2,1,0:T(8,128)(2,1)S(1)}, u32[]{:S(2)}, u32[]{:S(2)}) %collective-permute-start.4) | collective-permute-done | bytes 393248 | tf_op jit(solution)/shard_map/ppermute | solution.py:186
  13.4 2.8 %collective-permute-done.5.refs_0_ = bf16[2,2,192,256]{3,2,1,0:T(8,128)(2,1)S(1)} collective-permute-done((bf16[2,2,192,256]{3,2,1,0:T(8,128)(2,1)S(1)}, bf16[2,2,192,256]{3,2,1,0:T(8,128)(2,1)S(1)}, u32[]{:S(2)}, u32[]{:S(2)}) %collective-permute-start.5) | collective-permute-done | bytes 393248 | tf_op jit(solution)/shard_map/ppermute | solution.py:186
  16.2 0.0 copy-done.3
  16.3 1.7 %collective-permute-done.2.first_ref = bf16[2,2,192,256]{3,2,1,0:T(8,128)(2,1)S(1)} collective-permute-done((bf16[2,2,192,256]{3,2,1,0:T(8,128)(2,1)S(1)}, bf16[2,2,192,256]{3,2,1,0:T(8,128)(2,1)S(1)}, u32[]{:S(2)}, u32[]{:S(2)}) %collective-permute-start.2) | collective-permute-done | bytes 393248 | tf_op jit(solution)/shard_map/ppermute | solution.py:186
  18.0 2.0 %collective-permute-done.3.refs_0_ = bf16[2,2,192,256]{3,2,1,0:T(8,128)(2,1)S(1)} collective-permute-done((bf16[2,2,192,256]{3,2,1,0:T(8,128)(2,1)S(1)}, bf16[2,2,192,256]{3,2,1,0:T(8,128)(2,1)S(1)}, u32[]{:S(2)}, u32[]{:S(2)}) %collective-permute-start.3) | collective-permute-done | bytes 393248 | tf_op jit(solution)/shard_map/ppermute | solution.py:186
  20.0 2.2 %shard_map.61 = bf16[2,2,4,96,256]{4,3,2,1,0:T(8,128)(2,1)} custom-call(f32[2,4,192,256]{3,2,1,0:T(8,128)S(1)} %get-tuple-element.18.s_ref, bf16[2,288,384]{2,1,0:T(8,128)(2,1)S(1)} %get-tuple-element.19.u_ref, s32[1,4]{1,0:T(1,128)S(1)} %bitcast.14, bf16[256,256]{1,0:T(8,128)(2,1)S(1)} %get-tuple-element.20.spread_ref, ...), custom_call_target="tpu_custom_call", output_to_operand_aliasing={{}: (6, {})} | custom-call | flops 900000000 | bytes 4000000 | tf_op jit(solution)/shard_map/pallas_call | solution.py:258
  (3 shorter events, 0.1 us)
Async XLA Ops:
  0.0 2.2 %copy-start.4 = (bf16[2,2,2,192,128]{4,3,2,1,0:T(8,128)(2,1)S(1)}, bf16[2,2,2,192,128]{4,3,2,1,0:T(8,128)(2,1)}, u32[]{:S(2)}) copy-start(bf16[2,2,2,192,128]{4,3,2,1,0:T(8,128)(2,1)} %x_ref.1) | copy-start | bytes 1179652
  0.0 2.2 %copy-start = (bf16[3,3,3,192,192]{4,3,2,1,0:T(8,128)(2,1)S(1)}, bf16[3,3,3,192,192]{4,3,2,1,0:T(8,128)(2,1)}, u32[]{:S(2)}) copy-start(bf16[3,3,3,192,192]{4,3,2,1,0:T(8,128)(2,1)} %param.8) | copy-start | bytes 5971972
  0.0 2.2 %copy-start.2 = (f32[192]{0:T(256)S(1)}, f32[192]{0:T(256)}, u32[]{:S(2)}) copy-start(f32[192]{0:T(256)} %param.7) | copy-start | bytes 2308
  0.0 8.1 %collective-permute-start = (bf16[2,2,2,192,128]{4,3,2,1,0:T(8,128)(2,1)}, bf16[2,2,2,192,128]{4,3,2,1,0:T(8,128)(2,1)S(1)}, u32[]{:S(2)}, u32[]{:S(2)}) collective-permute-start(bf16[2,2,2,192,128]{4,3,2,1,0:T(8,128)(2,1)} %x_ref.1), channel_id=1, source_target_pairs={{0,64},{1,65},{2,66},{3,67},{4,8},{5,9},{6,10},{7,11},{8,4},{9,5},... | collective-permute-start | bytes 1179656 | tf_op jit(solution)/shard_map/ppermute | solution.py:186
  1.7 2.4 %collective-permute-start.1 = (bf16[2,2,2,192,128]{4,3,2,1,0:T(8,128)(2,1)}, bf16[2,2,2,192,128]{4,3,2,1,0:T(8,128)(2,1)S(1)}, u32[]{:S(2)}, u32[]{:S(2)}) collective-permute-start(bf16[2,2,2,192,128]{4,3,2,1,0:T(8,128)(2,1)} %x_ref.1), channel_id=1, source_target_pairs={{0,4},{1,5},{2,6},{3,7},{4,0},{5,1},{6,2},{7,3},{8,12},{9,13},{10,... | collective-permute-start | bytes 1179656 | tf_op jit(solution)/shard_map/ppermute | solution.py:186
  2.2 1.9 %copy-start.1 = (bf16[3,3,96,192]{3,2,1,0:T(8,128)(2,1)S(1)}, bf16[3,3,96,192]{3,2,1,0:T(8,128)(2,1)}, u32[]{:S(2)}) copy-start(bf16[3,3,96,192]{3,2,1,0:T(8,128)(2,1)} %param.9) | copy-start | bytes 995332
  4.3 9.2 %collective-permute-start.4 = (bf16[2,2,192,256]{3,2,1,0:T(8,128)(2,1)S(1)}, bf16[2,2,192,256]{3,2,1,0:T(8,128)(2,1)S(1)}, u32[]{:S(2)}, u32[]{:S(2)}) collective-permute-start(bf16[2,2,192,256]{3,2,1,0:T(8,128)(2,1)S(1)} %get-tuple-element.23), channel_id=1, source_target_pairs={{0,64},{1,65},{2,66},{3,67},{4,5},{5,4},{6,7},{7,6},{8,72},{9,73},... | collective-permute-start | bytes 1179656 | tf_op jit(solution)/shard_map/ppermute | solution.py:186
  5.9 10.3 %collective-permute-start.5 = (bf16[2,2,192,256]{3,2,1,0:T(8,128)(2,1)S(1)}, bf16[2,2,192,256]{3,2,1,0:T(8,128)(2,1)S(1)}, u32[]{:S(2)}, u32[]{:S(2)}) collective-permute-start(bf16[2,2,192,256]{3,2,1,0:T(8,128)(2,1)S(1)} %get-tuple-element.24), channel_id=1, source_target_pairs={{0,192},{1,193},{2,194},{3,195},{4,7},{5,6},{6,5},{7,4},{8,200},{9... | collective-permute-start | bytes 1179656 | tf_op jit(solution)/shard_map/ppermute | solution.py:186
  8.1 8.1 %copy-start.3 = (s32[4]{0:T(128)S(1)}, s32[4]{0:T(128)}, u32[]{:S(2)}) copy-start(s32[4]{0:T(128)} %param.6) | copy-start | bytes 52
  10.0 8.0 %collective-permute-start.2 = (bf16[2,2,192,256]{3,2,1,0:T(8,128)(2,1)S(1)}, bf16[2,2,192,256]{3,2,1,0:T(8,128)(2,1)S(1)}, u32[]{:S(2)}, u32[]{:S(2)}) collective-permute-start(bf16[2,2,192,256]{3,2,1,0:T(8,128)(2,1)S(1)} %get-tuple-element.21), channel_id=1, source_target_pairs={{0,1},{1,0},{2,3},{3,2},{4,68},{5,69},{6,70},{7,71},{8,9},{9,8},{1... | collective-permute-start | bytes 1179656 | tf_op jit(solution)/shard_map/ppermute | solution.py:186
  12.2 7.8 %collective-permute-start.3 = (bf16[2,2,192,256]{3,2,1,0:T(8,128)(2,1)S(1)}, bf16[2,2,192,256]{3,2,1,0:T(8,128)(2,1)S(1)}, u32[]{:S(2)}, u32[]{:S(2)}) collective-permute-start(bf16[2,2,192,256]{3,2,1,0:T(8,128)(2,1)S(1)} %get-tuple-element.22), channel_id=1, source_target_pairs={{0,3},{1,2},{2,1},{3,0},{4,196},{5,197},{6,198},{7,199},{8,11},{9,... | collective-permute-start | bytes 1179656 | tf_op jit(solution)/shard_map/ppermute | solution.py:186

commit v5 on v4

--- a/solution.py
+++ b/solution.py
@@ -146,12 +146,14 @@
                         at = (t * 4 + 2 * q + parity) * C2
                         b_ref[f, at : at + C2, :W] = even[:, t * W : (t + 1) * W]
                         b_ref[f, at : at + C2, W:] = odd[:, t * W : (t + 1) * W]
+        for f in range(2):
             for t in range(2):
                 wide = jnp.dot(b_ref[f, t * 4 * C2 : (t + 1) * 4 * C2], spread, preferred_element_type=jnp.float32)
                 wide = (wide * keep[t]).astype(jnp.bfloat16)
                 for at_row in range(4):
                     to_row = jnp.where(flip, 3 - at_row, at_row)
                     buf_ref[f, t, to_row] = wide[at_row * C2 : (at_row + 1) * C2]
+            for t in range(2):
                 copy = pltpu.make_async_copy(buf_ref.at[f, t], out_ref.at[t, f], sem.at[f, t])
                 copy.start()
                 copies.append(copy)
@@ -218,7 +220,7 @@
     from_chip = swap(latents, lambda d, t, r: (d, t ^ 1, r))
     from_z = swap(latents, across_chips)
     square = jax.ShapeDtypeStruct((2 * W, 2 * W), jnp.bfloat16)
-    spread = call(spread_kernel, square, [], 9_000_000_000)()
+    spread = call(spread_kernel, square, [], 1_500_000_000)()
     s1, spread = call(own_kernel, (part, square), [VMEM] * 4, 1_020_000_000, input_output_aliases={3: 1})(
         latents, gain, w, spread
     )

time: 22.6 us -> 22.1 us (0.978); the launches traced: 22.2 us -> 22 us
  waiting for transfers between devices: 7.15 us -> 7.57 us
  starting transfers between devices: 8.74 us -> 8.37 us
  Pallas kernels: 6.22 us -> 5.88 us
    ppermute x6, waiting for transfers between devices: 7.15 us -> 7.57 us  [swap(): lax.ppermute(value, AXES, [(index(*p), index(*partner(*p))) for p in plac...]
    ppermute x6, starting transfers between devices: 8.74 us -> 8.37 us  [swap(): lax.ppermute(value, AXES, [(index(*p), index(*partner(*p))) for p in plac...]
    pallas_call x3, Pallas kernels: 2.29 us -> 1.95 us  [upsample(): call(kernel, out, specs, flops, ANY, scratch_shapes=scratch, input_output...]
  transfers between devices with their start and end apart: 6 -> 6, of which waited for: 4 -> 5; matrix products, arithmetic and copies ran while one was open for 0% -> 0% of each run, Pallas kernels for 18% -> 18%
where the time goes in v5:
time: 22.1 us; the launch traced here: 22 us
  starting transfers between devices  8.37 us (38%)
  waiting for transfers between devices  7.57 us (34%)
  Pallas kernels  5.88 us (27%)
    ppermute x6, starting transfers between devices, swap(): lax.ppermute(value, AXES, [(index(*p), index(*partner(*p))) for p in plac...  8.37 us
    ppermute x6, waiting for transfers between devices, swap(): lax.ppermute(value, AXES, [(index(*p), index(*partner(*p))) for p in plac...  7.57 us
    pallas_call x3, Pallas kernels, upsample(): call(kernel, out, specs, flops, ANY, scratch_shapes=scratch, input_output...  1.95 us
    pallas_call x1, Pallas kernels, on_device(): call(functools.partial(previous_kernel, 0), (part, half, half, wide), spe...  1.88 us
    pallas_call x1, Pallas kernels, on_device(): call(own_kernel, (part, square), [VMEM] * 4, 1020000000, input_output_ali...  1.83 us
  transfers between devices with their start and end apart: 6, of which 5 were waited for; matrix products, arithmetic and copies ran while one was open for 0% of the time, Pallas kernels for 18%

profile of v5, /device:TPU:2, one launch (start us, length us, event | category | flops | bytes accessed | tf_op | source)
XLA Modules:
  0.0 22.0 jit_solution(8376377554780381875)
XLA Ops:
  0.0 0.0 copy-start.4
  0.0 0.0 copy-start
  0.0 0.0 copy-start.2
  0.0 0.1 collective-permute-start.1
  0.1 1.7 %collective-permute-start = (bf16[2,2,2,192,128]{4,3,2,1,0:T(8,128)(2,1)}, bf16[2,2,2,192,128]{4,3,2,1,0:T(8,128)(2,1)S(1)}, u32[]{:S(2)}, u32[]{:S(2)}) collective-permute-start(bf16[2,2,2,192,128]{4,3,2,1,0:T(8,128)(2,1)} %x_ref.1), channel_id=1, source_target_pairs={{0,64},{1,65},{2,66},{3,67},{4,8},{5,9},{6,10},{7,11},{8,4},{9,5},... | collective-permute-start | bytes 1179656 | tf_op jit(solution)/shard_map/ppermute | solution.py:188
  1.8 0.0 copy-done.4
  1.8 0.1 copy-done
  1.9 0.0 copy-done.2
  1.9 0.0 copy-start.1
  1.9 1.8 %shard_map.56 = (f32[2,4,192,256]{3,2,1,0:T(8,128)S(1)}, bf16[256,256]{1,0:T(8,128)(2,1)S(1)}) custom-call(bf16[2,2,2,192,128]{4,3,2,1,0:T(8,128)(2,1)S(1)} %copy-done.4, f32[1,192]{1,0:T(1,128)S(1)} %bitcast.9, bf16[9,576,192]{2,1,0:T(8,128)(2,1)S(1)} %bitcast.4, bf16[256,256]{1,0:T(8,128)(2,1)S(1)} %shard_map.55.spread_ref), custom_call_target="tpu_custom_call", output_to_operand_aliasing={{1}: (3, {})} | custom-call | flops 1020000000 | bytes 4000000 | tf_op jit(solution)/shard_map/pallas_call | solution.py:224
  3.7 0.0 collective-permute-done.1.x_ref
  3.7 0.0 copy-done.1
  3.7 0.2 shard_map.57
  3.9 1.7 %collective-permute-start.4 = (bf16[2,2,192,256]{3,2,1,0:T(8,128)(2,1)S(1)}, bf16[2,2,192,256]{3,2,1,0:T(8,128)(2,1)S(1)}, u32[]{:S(2)}, u32[]{:S(2)}) collective-permute-start(bf16[2,2,192,256]{3,2,1,0:T(8,128)(2,1)S(1)} %get-tuple-element.23), channel_id=1, source_target_pairs={{0,64},{1,65},{2,66},{3,67},{4,5},{5,4},{6,7},{7,6},{8,72},{9,73},... | collective-permute-start | bytes 1179656 | tf_op jit(solution)/shard_map/ppermute | solution.py:188
  5.6 2.2 %collective-permute-start.5 = (bf16[2,2,192,256]{3,2,1,0:T(8,128)(2,1)S(1)}, bf16[2,2,192,256]{3,2,1,0:T(8,128)(2,1)S(1)}, u32[]{:S(2)}, u32[]{:S(2)}) collective-permute-start(bf16[2,2,192,256]{3,2,1,0:T(8,128)(2,1)S(1)} %get-tuple-element.24), channel_id=1, source_target_pairs={{0,192},{1,193},{2,194},{3,195},{4,7},{5,6},{6,5},{7,4},{8,200},{9... | collective-permute-start | bytes 1179656 | tf_op jit(solution)/shard_map/ppermute | solution.py:188
  7.8 0.4 %collective-permute-done.x_ref = bf16[2,2,2,192,128]{4,3,2,1,0:T(8,128)(2,1)S(1)} collective-permute-done((bf16[2,2,2,192,128]{4,3,2,1,0:T(8,128)(2,1)}, bf16[2,2,2,192,128]{4,3,2,1,0:T(8,128)(2,1)S(1)}, u32[]{:S(2)}, u32[]{:S(2)}) %collective-permute-start) | collective-permute-done | bytes 393248 | tf_op jit(solution)/shard_map/ppermute | solution.py:188
  8.2 0.0 copy-start.3
  8.2 1.9 %shard_map.58 = (f32[2,4,192,256]{3,2,1,0:T(8,128)S(1)}, bf16[2,2,192,256]{3,2,1,0:T(8,128)(2,1)S(1)}, bf16[2,2,192,256]{3,2,1,0:T(8,128)(2,1)S(1)}, bf16[2,288,384]{2,1,0:T(8,128)(2,1)S(1)}) custom-call(bf16[2,2,2,192,128]{4,3,2,1,0:T(8,128)(2,1)S(1)} %collective-permute-done.x_ref, ...), custom_call_target="tpu_custom_call", output_to_operand_aliasing={{0}: (5, {}), {3}: (6, {})} | custom-call | flops 1020000000 | bytes 4000000 | tf_op jit(solution)/shard_map/pallas_call | solution.py:234
  10.1 2.3 %collective-permute-start.2 = (bf16[2,2,192,256]{3,2,1,0:T(8,128)(2,1)S(1)}, bf16[2,2,192,256]{3,2,1,0:T(8,128)(2,1)S(1)}, u32[]{:S(2)}, u32[]{:S(2)}) collective-permute-start(bf16[2,2,192,256]{3,2,1,0:T(8,128)(2,1)S(1)} %get-tuple-element.21), channel_id=1, source_target_pairs={{0,1},{1,0},{2,3},{3,2},{4,68},{5,69},{6,70},{7,71},{8,9},{9,8},{1... | collective-permute-start | bytes 1179656 | tf_op jit(solution)/shard_map/ppermute | solution.py:188
  12.3 0.5 %collective-permute-start.3 = (bf16[2,2,192,256]{3,2,1,0:T(8,128)(2,1)S(1)}, bf16[2,2,192,256]{3,2,1,0:T(8,128)(2,1)S(1)}, u32[]{:S(2)}, u32[]{:S(2)}) collective-permute-start(bf16[2,2,192,256]{3,2,1,0:T(8,128)(2,1)S(1)} %get-tuple-element.22), channel_id=1, source_target_pairs={{0,3},{1,2},{2,1},{3,0},{4,196},{5,197},{6,198},{7,199},{8,11},{9,... | collective-permute-start | bytes 1179656 | tf_op jit(solution)/shard_map/ppermute | solution.py:188
  12.8 0.7 %collective-permute-done.4.first_ref = bf16[2,2,192,256]{3,2,1,0:T(8,128)(2,1)S(1)} collective-permute-done((bf16[2,2,192,256]{3,2,1,0:T(8,128)(2,1)S(1)}, bf16[2,2,192,256]{3,2,1,0:T(8,128)(2,1)S(1)}, u32[]{:S(2)}, u32[]{:S(2)}) %collective-permute-start.4) | collective-permute-done | bytes 393248 | tf_op jit(solution)/shard_map/ppermute | solution.py:188
  13.6 1.9 %collective-permute-done.5.refs_0_ = bf16[2,2,192,256]{3,2,1,0:T(8,128)(2,1)S(1)} collective-permute-done((bf16[2,2,192,256]{3,2,1,0:T(8,128)(2,1)S(1)}, bf16[2,2,192,256]{3,2,1,0:T(8,128)(2,1)S(1)}, u32[]{:S(2)}, u32[]{:S(2)}) %collective-permute-start.5) | collective-permute-done | bytes 393248 | tf_op jit(solution)/shard_map/ppermute | solution.py:188
  15.4 0.0 copy-done.3
  15.5 2.6 %collective-permute-done.2.first_ref = bf16[2,2,192,256]{3,2,1,0:T(8,128)(2,1)S(1)} collective-permute-done((bf16[2,2,192,256]{3,2,1,0:T(8,128)(2,1)S(1)}, bf16[2,2,192,256]{3,2,1,0:T(8,128)(2,1)S(1)}, u32[]{:S(2)}, u32[]{:S(2)}) %collective-permute-start.2) | collective-permute-done | bytes 393248 | tf_op jit(solution)/shard_map/ppermute | solution.py:188
  18.1 2.0 %collective-permute-done.3.refs_0_ = bf16[2,2,192,256]{3,2,1,0:T(8,128)(2,1)S(1)} collective-permute-done((bf16[2,2,192,256]{3,2,1,0:T(8,128)(2,1)S(1)}, bf16[2,2,192,256]{3,2,1,0:T(8,128)(2,1)S(1)}, u32[]{:S(2)}, u32[]{:S(2)}) %collective-permute-start.3) | collective-permute-done | bytes 393248 | tf_op jit(solution)/shard_map/ppermute | solution.py:188
  20.1 1.9 %shard_map.61 = bf16[2,2,4,96,256]{4,3,2,1,0:T(8,128)(2,1)} custom-call(f32[2,4,192,256]{3,2,1,0:T(8,128)S(1)} %get-tuple-element.18.s_ref, bf16[2,288,384]{2,1,0:T(8,128)(2,1)S(1)} %get-tuple-element.19.u_ref, s32[1,4]{1,0:T(1,128)S(1)} %bitcast.14, bf16[256,256]{1,0:T(8,128)(2,1)S(1)} %get-tuple-element.20.spread_ref, ...), custom_call_target="tpu_custom_call", output_to_operand_aliasing={{}: (6, {})} | custom-call | flops 900000000 | bytes 4000000 | tf_op jit(solution)/shard_map/pallas_call | solution.py:260
  (3 shorter events, 0.1 us)
Async XLA Ops:
  0.0 1.8 %copy-start.4 = (bf16[2,2,2,192,128]{4,3,2,1,0:T(8,128)(2,1)S(1)}, bf16[2,2,2,192,128]{4,3,2,1,0:T(8,128)(2,1)}, u32[]{:S(2)}) copy-start(bf16[2,2,2,192,128]{4,3,2,1,0:T(8,128)(2,1)} %x_ref.1) | copy-start | bytes 1179652
  0.0 1.9 %copy-start = (bf16[3,3,3,192,192]{4,3,2,1,0:T(8,128)(2,1)S(1)}, bf16[3,3,3,192,192]{4,3,2,1,0:T(8,128)(2,1)}, u32[]{:S(2)}) copy-start(bf16[3,3,3,192,192]{4,3,2,1,0:T(8,128)(2,1)} %param.8) | copy-start | bytes 5971972
  0.0 1.9 %copy-start.2 = (f32[192]{0:T(256)S(1)}, f32[192]{0:T(256)}, u32[]{:S(2)}) copy-start(f32[192]{0:T(256)} %param.7) | copy-start | bytes 2308
  0.0 3.7 %collective-permute-start.1 = (bf16[2,2,2,192,128]{4,3,2,1,0:T(8,128)(2,1)}, bf16[2,2,2,192,128]{4,3,2,1,0:T(8,128)(2,1)S(1)}, u32[]{:S(2)}, u32[]{:S(2)}) collective-permute-start(bf16[2,2,2,192,128]{4,3,2,1,0:T(8,128)(2,1)} %x_ref.1), channel_id=1, source_target_pairs={{0,4},{1,5},{2,6},{3,7},{4,0},{5,1},{6,2},{7,3},{8,12},{9,13},{10,... | collective-permute-start | bytes 1179656 | tf_op jit(solution)/shard_map/ppermute | solution.py:188
  0.1 8.1 %collective-permute-start = (bf16[2,2,2,192,128]{4,3,2,1,0:T(8,128)(2,1)}, bf16[2,2,2,192,128]{4,3,2,1,0:T(8,128)(2,1)S(1)}, u32[]{:S(2)}, u32[]{:S(2)}) collective-permute-start(bf16[2,2,2,192,128]{4,3,2,1,0:T(8,128)(2,1)} %x_ref.1), channel_id=1, source_target_pairs={{0,64},{1,65},{2,66},{3,67},{4,8},{5,9},{6,10},{7,11},{8,4},{9,5},... | collective-permute-start | bytes 1179656 | tf_op jit(solution)/shard_map/ppermute | solution.py:188
  1.9 1.8 %copy-start.1 = (bf16[3,3,96,192]{3,2,1,0:T(8,128)(2,1)S(1)}, bf16[3,3,96,192]{3,2,1,0:T(8,128)(2,1)}, u32[]{:S(2)}) copy-start(bf16[3,3,96,192]{3,2,1,0:T(8,128)(2,1)} %param.9) | copy-start | bytes 995332
  3.9 9.6 %collective-permute-start.4 = (bf16[2,2,192,256]{3,2,1,0:T(8,128)(2,1)S(1)}, bf16[2,2,192,256]{3,2,1,0:T(8,128)(2,1)S(1)}, u32[]{:S(2)}, u32[]{:S(2)}) collective-permute-start(bf16[2,2,192,256]{3,2,1,0:T(8,128)(2,1)S(1)} %get-tuple-element.23), channel_id=1, source_target_pairs={{0,64},{1,65},{2,66},{3,67},{4,5},{5,4},{6,7},{7,6},{8,72},{9,73},... | collective-permute-start | bytes 1179656 | tf_op jit(solution)/shard_map/ppermute | solution.py:188
  5.6 9.8 %collective-permute-start.5 = (bf16[2,2,192,256]{3,2,1,0:T(8,128)(2,1)S(1)}, bf16[2,2,192,256]{3,2,1,0:T(8,128)(2,1)S(1)}, u32[]{:S(2)}, u32[]{:S(2)}) collective-permute-start(bf16[2,2,192,256]{3,2,1,0:T(8,128)(2,1)S(1)} %get-tuple-element.24), channel_id=1, source_target_pairs={{0,192},{1,193},{2,194},{3,195},{4,7},{5,6},{6,5},{7,4},{8,200},{9... | collective-permute-start | bytes 1179656 | tf_op jit(solution)/shard_map/ppermute | solution.py:188
  8.2 7.3 %copy-start.3 = (s32[4]{0:T(128)S(1)}, s32[4]{0:T(128)}, u32[]{:S(2)}) copy-start(s32[4]{0:T(128)} %param.6) | copy-start | bytes 52
  10.1 8.0 %collective-permute-start.2 = (bf16[2,2,192,256]{3,2,1,0:T(8,128)(2,1)S(1)}, bf16[2,2,192,256]{3,2,1,0:T(8,128)(2,1)S(1)}, u32[]{:S(2)}, u32[]{:S(2)}) collective-permute-start(bf16[2,2,192,256]{3,2,1,0:T(8,128)(2,1)S(1)} %get-tuple-element.21), channel_id=1, source_target_pairs={{0,1},{1,0},{2,3},{3,2},{4,68},{5,69},{6,70},{7,71},{8,9},{9,8},{1... | collective-permute-start | bytes 1179656 | tf_op jit(solution)/shard_map/ppermute | solution.py:188
  12.3 7.8 %collective-permute-start.3 = (bf16[2,2,192,256]{3,2,1,0:T(8,128)(2,1)S(1)}, bf16[2,2,192,256]{3,2,1,0:T(8,128)(2,1)S(1)}, u32[]{:S(2)}, u32[]{:S(2)}) collective-permute-start(bf16[2,2,192,256]{3,2,1,0:T(8,128)(2,1)S(1)} %get-tuple-element.22), channel_id=1, source_target_pairs={{0,3},{1,2},{2,1},{3,0},{4,196},{5,197},{6,198},{7,199},{8,11},{9,... | collective-permute-start | bytes 1179656 | tf_op jit(solution)/shard_map/ppermute | solution.py:188

commit v6 on v5

--- a/solution.py
+++ b/solution.py
@@ -104,60 +104,110 @@
         u_ref[1] = jnp.concatenate([w0 + w1, w2], axis=1).astype(jnp.bfloat16)
 
 
-def upsample_kernel(core, edge, s_ref, u_ref, slot_ref, spread_ref, first_ref, *refs):
-    out_ref, h_ref, b_ref, buf_ref, sem = refs[-5:]
-    second_ref = refs[0]
-    row, rows = lax.axis_index("rows"), lax.axis_size("rows")
-    mine = lax.rem(lax.axis_index("tm"), 2) == core
-    at_edge = jnp.logical_or(row == 0, row == rows - 1)
-
-    if edge is not None:
-        mine = jnp.logical_and(mine, at_edge == edge)
-
-    @pl.when(mine)
-    def _():
-        flip = flipped()
-        spread = spread_ref[...]
-        keep = []
+def hidden_row(s_ref, f, ro, got_ref):
+    total = s_ref[f, ro]
+    if got_ref is not None:
+        total = total + got_ref[f, 1 - ro % 2].astype(jnp.float32)
+    return total
+
+
+def upsample(h_ref, u_ref, slot_ref, spread_ref, b_ref, buf_ref, out_ref, sem, todo, flip):
+    spread = spread_ref[...]
+    n = len(todo)
+    for f in range(2):
+        for i, at_row in enumerate(todo):
+            low = (at_row // 2 + at_row % 2) * C
+            total = jnp.dot(u_ref[at_row % 2], h_ref[f, low : low + 2 * C], preferred_element_type=jnp.float32)
+            k0, k1, k2 = total[:C2], total[C2 : 2 * C2], total[2 * C2 :]
+            even = (shifted(k0, 1) + k1 + k2).astype(jnp.bfloat16)
+            odd = (k0 + k1 + shifted(k2, -1)).astype(jnp.bfloat16)
+            for t in range(2):
+                at = (t * n + i) * C2
+                b_ref[f, at : at + C2, :W] = even[:, t * W : (t + 1) * W]
+                b_ref[f, at : at + C2, W:] = odd[:, t * W : (t + 1) * W]
+    copies = []
+    for f in range(2):
         for t in range(2):
             hit = slot_ref[...] == lax.axis_index("dp") * 2 + t
-            keep.append(jnp.max(jnp.where(hit, 1.0, 0.0), axis=1, keepdims=True))
-        copies = []
+            keep = jnp.max(jnp.where(hit, 1.0, 0.0), axis=1, keepdims=True)
+            wide = jnp.dot(b_ref[f, t * n * C2 : (t + 1) * n * C2], spread, preferred_element_type=jnp.float32)
+            wide = (wide * keep).astype(jnp.bfloat16)
+            for i in range(n):
+                buf_ref[f, t, jnp.where(flip, n - 1 - i, i)] = wide[i * C2 : (i + 1) * C2]
+        if out_ref is not None:
+            for t in range(2):
+                copies.append(out_copy(buf_ref, out_ref, sem, f, t, todo, flip))
+                copies[-1].start()
+    for copy in copies:
+        copy.wait()
+
+
+def out_copy(buf_ref, out_ref, sem, f, t, todo, flip):
+    first, n = jnp.where(flip, 3 - todo[-1], todo[0]), len(todo)
+    return pltpu.make_async_copy(buf_ref.at[f, t, pl.ds(0, n)], out_ref.at[t, f, pl.ds(first, n)], sem.at[f, t])
+
+
+def place(core):
+    row = lax.axis_index("rows")
+    mine = lax.rem(lax.axis_index("tm"), 2) == core
+    return mine, jnp.logical_or(row == 0, row == lax.axis_size("rows") - 1)
+
+
+def odd_kernel(s_ref, u_ref, slot_ref, spread_ref, first_ref, second_ref, out_ref, h_ref, b_ref, buf_ref, sem):
+    mine, edge = place(1)
+
+    @pl.when(mine)
+    def _():
         for f in range(2):
             for ro in range(4):
-                total = s_ref[f, ro]
-                if ro >= 2 or not edge:
-                    got = (first_ref if ro >= 2 else second_ref)[f, 1 - ro % 2]
-                    total = total + got.astype(jnp.float32)
-                if edge is None and ro < 2:
+                total = hidden_row(s_ref, f, ro, first_ref if ro >= 2 else second_ref)
+                if ro < 2:
                     alone = s_ref[f, ro] if ro == 1 else jnp.zeros_like(total)
-                    total = jnp.where(at_edge, alone, total)
-                elif edge and ro == 0:
-                    total = jnp.zeros_like(total)
+                    total = jnp.where(edge, alone, total)
                 h_ref[f, ro * C : (ro + 1) * C] = total.astype(jnp.bfloat16)
-            for q in range(2):
-                for parity in range(2):
-                    low = (q + parity) * C
-                    total = jnp.dot(u_ref[parity], h_ref[f, low : low + 2 * C], preferred_element_type=jnp.float32)
-                    k0, k1, k2 = total[:C2], total[C2 : 2 * C2], total[2 * C2 :]
-                    even = (shifted(k0, 1) + k1 + k2).astype(jnp.bfloat16)
-                    odd = (k0 + k1 + shifted(k2, -1)).astype(jnp.bfloat16)
-                    for t in range(2):
-                        at = (t * 4 + 2 * q + parity) * C2
-                        b_ref[f, at : at + C2, :W] = even[:, t * W : (t + 1) * W]
-                        b_ref[f, at : at + C2, W:] = odd[:, t * W : (t + 1) * W]
+        upsample(h_ref, u_ref, slot_ref, spread_ref, b_ref, buf_ref, out_ref, sem, (0, 1, 2, 3), flipped())
+
+
+def even_first_kernel(
+    s_ref, u_ref, slot_ref, spread_ref, first_ref, _, out_ref, h_ref, kept_ref, b_ref, buf_ref, sem
+):
+    mine, edge = place(0)
+
+    def lower():
         for f in range(2):
-            for t in range(2):
-                wide = jnp.dot(b_ref[f, t * 4 * C2 : (t + 1) * 4 * C2], spread, preferred_element_type=jnp.float32)
-                wide = (wide * keep[t]).astype(jnp.bfloat16)
-                for at_row in range(4):
-                    to_row = jnp.where(flip, 3 - at_row, at_row)
-                    buf_ref[f, t, to_row] = wide[at_row * C2 : (at_row + 1) * C2]
-            for t in range(2):
-                copy = pltpu.make_async_copy(buf_ref.at[f, t], out_ref.at[t, f], sem.at[f, t])
-                copy.start()
-                copies.append(copy)
-        for copy in copies:
+            for ro in (2, 3):
+                h_ref[f, ro * C : (ro + 1) * C] = hidden_row(s_ref, f, ro, first_ref).astype(jnp.bfloat16)
+
+    @pl.when(jnp.logical_and(mine, edge))
+    def _():
+        lower()
+        for f in range(2):
+            h_ref[f, :C] = jnp.zeros((C, 2 * W), jnp.bfloat16)
+            h_ref[f, C : 2 * C] = hidden_row(s_ref, f, 1, None).astype(jnp.bfloat16)
+        upsample(h_ref, u_ref, slot_ref, spread_ref, b_ref, buf_ref, out_ref, sem, (0, 1, 2, 3), flipped())
+
+    @pl.when(jnp.logical_and(mine, jnp.logical_not(edge)))
+    def _():
+        lower()
+        upsample(h_ref, u_ref, slot_ref, spread_ref, b_ref, kept_ref, None, sem, (3,), flipped())
+
+
+def even_second_kernel(
+    s_ref, u_ref, slot_ref, spread_ref, _, second_ref, low_ref, kept_ref, __, out_ref, h_ref, b_ref, buf_ref, sem, kept_sem
+):
+    mine, edge = place(0)
+
+    @pl.when(jnp.logical_and(mine, jnp.logical_not(edge)))
+    def _():
+        kept = [out_copy(kept_ref, out_ref, kept_sem, f, t, (3,), flipped()) for f in range(2) for t in range(2)]
+        for copy in kept:
+            copy.start()
+        for f in range(2):
+            for ro in range(2):
+                h_ref[f, ro * C : (ro + 1) * C] = hidden_row(s_ref, f, ro, second_ref).astype(jnp.bfloat16)
+            h_ref[f, 2 * C : 3 * C] = low_ref[f, 2 * C : 3 * C]
+        upsample(h_ref, u_ref, slot_ref, spread_ref, b_ref, buf_ref, out_ref, sem, (0, 1, 2), flipped())
+        for copy in kept:
             copy.wait()
 
 
@@ -166,7 +216,7 @@
 
 
 def call(kernel, out_shape, in_specs, flops, out_spec=VMEM, **more):
-    out_specs = jax.tree.map(lambda _: out_spec, out_shape)
+    out_specs = out_spec if isinstance(out_spec, tuple) else jax.tree.map(lambda _: out_spec, out_shape)
     return pl.pallas_call(
         kernel,
         out_shape=out_shape,
@@ -213,6 +263,9 @@
             return d, t, ((r + 1) % n_rows if r % 2 else (r - 1) % n_rows)
 
         return partner
+
+    def shape(*dims, dtype=jnp.bfloat16):
+        return jax.ShapeDtypeStruct(dims, dtype)
 
     part = jax.ShapeDtypeStruct((2, 4, C, 2 * W), jnp.float32)
     half = jax.ShapeDtypeStruct((2, 2, C, 2 * W), jnp.bfloat16)
@@ -241,27 +294,35 @@
     even1 = swap(even1, rows_swap(0, 0))
     even2 = swap(even2, rows_swap(1, 0))
     out = jax.ShapeDtypeStruct((own_tiles, frames, 2 * rows, C2, 2 * W), jnp.bfloat16)
+    rows_of = shape(2, 4 * C, 2 * W)
     scratch = [
-        pltpu.VMEM((2, 4 * C, 2 * W), jnp.bfloat16),
         pltpu.VMEM((2, 8 * C2, 2 * W), jnp.bfloat16),
         pltpu.VMEM((2, 2, 2 * rows, C2, 2 * W), jnp.bfloat16),
         pltpu.SemaphoreType.DMA((2, 2)),
     ]
-
-    def upsample(core, edge, first, second, pixels):
-        args = (s, u, slots, spread, first) + (() if edge else (second,))
-        specs = [VMEM] * len(args)
-        aliases = {}
-        if pixels is not None:
-            aliases = {len(args): 0}
-            args, specs = args + (pixels,), specs + [ANY]
-        flops = 9_000_000_000 if core else 900_000_000
-        kernel = functools.partial(upsample_kernel, core, edge)
-        return call(kernel, out, specs, flops, ANY, scratch_shapes=scratch, input_output_aliases=aliases)(*args)
-
-    pixels = upsample(1, None, odd1, odd2, None)
-    pixels = upsample(0, True, even1, even2, pixels)
-    return upsample(0, False, even1, even2, pixels)
+    ahead = pltpu.VMEM(rows_of.shape, rows_of.dtype)
+    common = (s, u, slots, spread)
+    pixels = call(odd_kernel, out, [VMEM] * 6, 9_000_000_000, ANY, scratch_shapes=[ahead] + scratch)(
+        *common, odd1, odd2
+    )
+    pixels, lower, kept = call(
+        even_first_kernel,
+        (out, rows_of, shape(2, 2, 1, C2, 2 * W)),
+        [VMEM] * 5 + [ANY],
+        900_000_000,
+        (ANY, VMEM, VMEM),
+        scratch_shapes=scratch,
+        input_output_aliases={5: 0},
+    )(*common, even1, pixels)
+    return call(
+        even_second_kernel,
+        out,
+        [VMEM] * 8 + [ANY],
+        700_000_000,
+        ANY,
+        scratch_shapes=[ahead] + scratch + [pltpu.SemaphoreType.DMA((2, 2))],
+        input_output_aliases={8: 0},
+    )(*common, even1, even2, lower, kept, pixels)
 
 
 def solution(mesh):

time: 22.1 us -> 21.9 us (level)
  waiting for transfers between devices: 7.57 us -> 6.98 us
  Pallas kernels: 5.88 us -> 6.31 us
    ppermute x6, waiting for transfers between devices: 7.57 us -> 6.98 us  [swap(): lax.ppermute(value, AXES, [(index(*p), index(*partner(*p))) for p in plac...]
    pallas_call x3, Pallas kernels: 1.95 us -> 2.38 us  [the longest x1 1.71 us: on_device(): call(even_second_kernel, out, [VMEM] * 8 + [ANY], 700000000, ANY, scratch...]
  transfers between devices with their start and end apart: 6 -> 6, of which waited for: 5 -> 5; matrix products, arithmetic and copies ran while one was open for 0% -> 0% of each run, Pallas kernels for 18% -> 21%
where the time goes in v6:
time: 21.9 us; the launch traced here: 21.8 us
  starting transfers between devices  8.37 us (38%)
  waiting for transfers between devices  6.98 us (32%)
  Pallas kernels  6.31 us (29%)
    ppermute x6, starting transfers between devices, swap(): lax.ppermute(value, AXES, [(index(*p), index(*partner(*p))) for p in plac...  8.37 us
    ppermute x6, waiting for transfers between devices, swap(): lax.ppermute(value, AXES, [(index(*p), index(*partner(*p))) for p in plac...  6.98 us
    pallas_call x1, Pallas kernels, on_device(): call(functools.partial(previous_kernel, 0), (part, half, half, wide), spe...  1.88 us
    pallas_call x1, Pallas kernels, on_device(): call(own_kernel, (part, square), [VMEM] * 4, 1020000000, input_output_ali...  1.83 us
    pallas_call x1, Pallas kernels, on_device(): call(even_second_kernel, out, [VMEM] * 8 + [ANY], 700000000, ANY, scratch...  1.71 us
    pallas_call x1, Pallas kernels, on_device(): call(even_first_kernel, (out, rows_of, shape(2, 2, 1, C2, 2 * W)), [VMEM]...  0.62 us
  transfers between devices with their start and end apart: 6, of which 5 were waited for; matrix products, arithmetic and copies ran while one was open for 0% of the time, Pallas kernels for 21%

profile of v6, /device:TPU:2, one launch (start us, length us, event | category | flops | bytes accessed | tf_op | source)
XLA Modules:
  0.0 21.8 jit_solution(13343317298411276610)
XLA Ops:
  0.0 0.0 copy-start.4
  0.0 0.0 copy-start
  0.0 0.0 copy-start.2
  0.0 0.1 collective-permute-start.1
  0.1 1.7 %collective-permute-start = (bf16[2,2,2,192,128]{4,3,2,1,0:T(8,128)(2,1)}, bf16[2,2,2,192,128]{4,3,2,1,0:T(8,128)(2,1)S(1)}, u32[]{:S(2)}, u32[]{:S(2)}) collective-permute-start(bf16[2,2,2,192,128]{4,3,2,1,0:T(8,128)(2,1)} %x_ref.1), channel_id=1, source_target_pairs={{0,64},{1,65},{2,66},{3,67},{4,8},{5,9},{6,10},{7,11},{8,4},{9,5},... | collective-permute-start | bytes 1179656 | tf_op jit(solution)/shard_map/ppermute | solution.py:238
  1.8 0.0 copy-done.4
  1.8 0.1 copy-done
  1.9 0.0 copy-done.2
  1.9 0.0 copy-start.1
  1.9 1.8 %shard_map.56 = (f32[2,4,192,256]{3,2,1,0:T(8,128)S(1)}, bf16[256,256]{1,0:T(8,128)(2,1)S(1)}) custom-call(bf16[2,2,2,192,128]{4,3,2,1,0:T(8,128)(2,1)S(1)} %copy-done.4, f32[1,192]{1,0:T(1,128)S(1)} %bitcast.9, bf16[9,576,192]{2,1,0:T(8,128)(2,1)S(1)} %bitcast.4, bf16[256,256]{1,0:T(8,128)(2,1)S(1)} %shard_map.55.spread_ref), custom_call_target="tpu_custom_call", output_to_operand_aliasing={{1}: (3, {})} | custom-call | flops 1020000000 | bytes 4000000 | tf_op jit(solution)/shard_map/pallas_call | solution.py:277
  3.7 0.0 collective-permute-done.1.x_ref
  3.7 0.0 copy-done.1
  3.7 0.2 shard_map.57
  3.9 1.7 %collective-permute-start.4 = (bf16[2,2,192,256]{3,2,1,0:T(8,128)(2,1)S(1)}, bf16[2,2,192,256]{3,2,1,0:T(8,128)(2,1)S(1)}, u32[]{:S(2)}, u32[]{:S(2)}) collective-permute-start(bf16[2,2,192,256]{3,2,1,0:T(8,128)(2,1)S(1)} %get-tuple-element.26), channel_id=1, source_target_pairs={{0,64},{1,65},{2,66},{3,67},{4,5},{5,4},{6,7},{7,6},{8,72},{9,73},... | collective-permute-start | bytes 1179656 | tf_op jit(solution)/shard_map/ppermute | solution.py:238
  5.6 2.2 %collective-permute-start.5 = (bf16[2,2,192,256]{3,2,1,0:T(8,128)(2,1)S(1)}, bf16[2,2,192,256]{3,2,1,0:T(8,128)(2,1)S(1)}, u32[]{:S(2)}, u32[]{:S(2)}) collective-permute-start(bf16[2,2,192,256]{3,2,1,0:T(8,128)(2,1)S(1)} %get-tuple-element.27), channel_id=1, source_target_pairs={{0,192},{1,193},{2,194},{3,195},{4,7},{5,6},{6,5},{7,4},{8,200},{9... | collective-permute-start | bytes 1179656 | tf_op jit(solution)/shard_map/ppermute | solution.py:238
  7.8 0.4 %collective-permute-done.x_ref = bf16[2,2,2,192,128]{4,3,2,1,0:T(8,128)(2,1)S(1)} collective-permute-done((bf16[2,2,2,192,128]{4,3,2,1,0:T(8,128)(2,1)}, bf16[2,2,2,192,128]{4,3,2,1,0:T(8,128)(2,1)S(1)}, u32[]{:S(2)}, u32[]{:S(2)}) %collective-permute-start) | collective-permute-done | bytes 393248 | tf_op jit(solution)/shard_map/ppermute | solution.py:238
  8.2 0.0 copy-start.3
  8.2 1.9 %shard_map.58 = (f32[2,4,192,256]{3,2,1,0:T(8,128)S(1)}, bf16[2,2,192,256]{3,2,1,0:T(8,128)(2,1)S(1)}, bf16[2,2,192,256]{3,2,1,0:T(8,128)(2,1)S(1)}, bf16[2,288,384]{2,1,0:T(8,128)(2,1)S(1)}) custom-call(bf16[2,2,2,192,128]{4,3,2,1,0:T(8,128)(2,1)S(1)} %collective-permute-done.x_ref, ...), custom_call_target="tpu_custom_call", output_to_operand_aliasing={{0}: (5, {}), {3}: (6, {})} | custom-call | flops 1020000000 | bytes 4000000 | tf_op jit(solution)/shard_map/pallas_call | solution.py:287
  10.1 2.3 %collective-permute-start.2 = (bf16[2,2,192,256]{3,2,1,0:T(8,128)(2,1)S(1)}, bf16[2,2,192,256]{3,2,1,0:T(8,128)(2,1)S(1)}, u32[]{:S(2)}, u32[]{:S(2)}) collective-permute-start(bf16[2,2,192,256]{3,2,1,0:T(8,128)(2,1)S(1)} %get-tuple-element.24), channel_id=1, source_target_pairs={{0,1},{1,0},{2,3},{3,2},{4,68},{5,69},{6,70},{7,71},{8,9},{9,8},{1... | collective-permute-start | bytes 1179656 | tf_op jit(solution)/shard_map/ppermute | solution.py:238
  12.3 0.5 %collective-permute-start.3 = (bf16[2,2,192,256]{3,2,1,0:T(8,128)(2,1)S(1)}, bf16[2,2,192,256]{3,2,1,0:T(8,128)(2,1)S(1)}, u32[]{:S(2)}, u32[]{:S(2)}) collective-permute-start(bf16[2,2,192,256]{3,2,1,0:T(8,128)(2,1)S(1)} %get-tuple-element.25), channel_id=1, source_target_pairs={{0,3},{1,2},{2,1},{3,0},{4,196},{5,197},{6,198},{7,199},{8,11},{9,... | collective-permute-start | bytes 1179656 | tf_op jit(solution)/shard_map/ppermute | solution.py:238
  12.8 0.7 %collective-permute-done.4.first_ref = bf16[2,2,192,256]{3,2,1,0:T(8,128)(2,1)S(1)} collective-permute-done((bf16[2,2,192,256]{3,2,1,0:T(8,128)(2,1)S(1)}, bf16[2,2,192,256]{3,2,1,0:T(8,128)(2,1)S(1)}, u32[]{:S(2)}, u32[]{:S(2)}) %collective-permute-start.4) | collective-permute-done | bytes 393248 | tf_op jit(solution)/shard_map/ppermute | solution.py:238
  13.6 1.9 %collective-permute-done.5.second_ref = bf16[2,2,192,256]{3,2,1,0:T(8,128)(2,1)S(1)} collective-permute-done((bf16[2,2,192,256]{3,2,1,0:T(8,128)(2,1)S(1)}, bf16[2,2,192,256]{3,2,1,0:T(8,128)(2,1)S(1)}, u32[]{:S(2)}, u32[]{:S(2)}) %collective-permute-start.5) | collective-permute-done | bytes 393248 | tf_op jit(solution)/shard_map/ppermute | solution.py:238
  15.4 0.0 copy-done.3
  15.5 2.6 %collective-permute-done.2.first_ref._ = bf16[2,2,192,256]{3,2,1,0:T(8,128)(2,1)S(1)} collective-permute-done((bf16[2,2,192,256]{3,2,1,0:T(8,128)(2,1)S(1)}, bf16[2,2,192,256]{3,2,1,0:T(8,128)(2,1)S(1)}, u32[]{:S(2)}, u32[]{:S(2)}) %collective-permute-start.2) | collective-permute-done | bytes 393248 | tf_op jit(solution)/shard_map/ppermute | solution.py:238
  18.1 0.6 %shard_map.60 = (bf16[2,2,4,96,256]{4,3,2,1,0:T(8,128)(2,1)}, bf16[2,768,256]{2,1,0:T(8,128)(2,1)S(1)}, bf16[2,2,1,96,256]{4,3,2,1,0:T(8,128)(2,1)S(1)}) custom-call(f32[2,4,192,256]{3,2,1,0:T(8,128)S(1)} %get-tuple-element.21.s_ref, bf16[2,288,384]{2,1,0:T(8,128)(2,1)S(1)} %get-tuple-element.22.u_ref, ...), custom_call_target="tpu_custom_call", output_to_operand_aliasing={{0}: (5, {})} | custom-call | flops 900000000 | bytes 4000000 | tf_op jit(solution)/shard_map/pallas_call | solution.py:308
  18.7 1.4 %collective-permute-done.3.second_ref = bf16[2,2,192,256]{3,2,1,0:T(8,128)(2,1)S(1)} collective-permute-done((bf16[2,2,192,256]{3,2,1,0:T(8,128)(2,1)S(1)}, bf16[2,2,192,256]{3,2,1,0:T(8,128)(2,1)S(1)}, u32[]{:S(2)}, u32[]{:S(2)}) %collective-permute-start.3) | collective-permute-done | bytes 393248 | tf_op jit(solution)/shard_map/ppermute | solution.py:238
  20.1 1.7 %shard_map.61 = bf16[2,2,4,96,256]{4,3,2,1,0:T(8,128)(2,1)} custom-call(f32[2,4,192,256]{3,2,1,0:T(8,128)S(1)} %get-tuple-element.21.s_ref, bf16[2,288,384]{2,1,0:T(8,128)(2,1)S(1)} %get-tuple-element.22.u_ref, s32[1,4]{1,0:T(1,128)S(1)} %bitcast.14, bf16[256,256]{1,0:T(8,128)(2,1)S(1)} %get-tuple-element.23.spread_ref, ...), custom_call_target="tpu_custom_call", output_to_operand_aliasing={{}: (8, {})} | custom-call | flops 700000000 | bytes 4000000 | tf_op jit(solution)/shard_map/pallas_call | solution.py:317
  (2 shorter events, 0.1 us)
Async XLA Ops:
  0.0 1.8 %copy-start.4 = (bf16[2,2,2,192,128]{4,3,2,1,0:T(8,128)(2,1)S(1)}, bf16[2,2,2,192,128]{4,3,2,1,0:T(8,128)(2,1)}, u32[]{:S(2)}) copy-start(bf16[2,2,2,192,128]{4,3,2,1,0:T(8,128)(2,1)} %x_ref.1) | copy-start | bytes 1179652
  0.0 1.9 %copy-start = (bf16[3,3,3,192,192]{4,3,2,1,0:T(8,128)(2,1)S(1)}, bf16[3,3,3,192,192]{4,3,2,1,0:T(8,128)(2,1)}, u32[]{:S(2)}) copy-start(bf16[3,3,3,192,192]{4,3,2,1,0:T(8,128)(2,1)} %param.8) | copy-start | bytes 5971972
  0.0 1.9 %copy-start.2 = (f32[192]{0:T(256)S(1)}, f32[192]{0:T(256)}, u32[]{:S(2)}) copy-start(f32[192]{0:T(256)} %param.7) | copy-start | bytes 2308
  0.0 3.7 %collective-permute-start.1 = (bf16[2,2,2,192,128]{4,3,2,1,0:T(8,128)(2,1)}, bf16[2,2,2,192,128]{4,3,2,1,0:T(8,128)(2,1)S(1)}, u32[]{:S(2)}, u32[]{:S(2)}) collective-permute-start(bf16[2,2,2,192,128]{4,3,2,1,0:T(8,128)(2,1)} %x_ref.1), channel_id=1, source_target_pairs={{0,4},{1,5},{2,6},{3,7},{4,0},{5,1},{6,2},{7,3},{8,12},{9,13},{10,... | collective-permute-start | bytes 1179656 | tf_op jit(solution)/shard_map/ppermute | solution.py:238
  0.1 8.1 %collective-permute-start = (bf16[2,2,2,192,128]{4,3,2,1,0:T(8,128)(2,1)}, bf16[2,2,2,192,128]{4,3,2,1,0:T(8,128)(2,1)S(1)}, u32[]{:S(2)}, u32[]{:S(2)}) collective-permute-start(bf16[2,2,2,192,128]{4,3,2,1,0:T(8,128)(2,1)} %x_ref.1), channel_id=1, source_target_pairs={{0,64},{1,65},{2,66},{3,67},{4,8},{5,9},{6,10},{7,11},{8,4},{9,5},... | collective-permute-start | bytes 1179656 | tf_op jit(solution)/shard_map/ppermute | solution.py:238
  1.9 1.8 %copy-start.1 = (bf16[3,3,96,192]{3,2,1,0:T(8,128)(2,1)S(1)}, bf16[3,3,96,192]{3,2,1,0:T(8,128)(2,1)}, u32[]{:S(2)}) copy-start(bf16[3,3,96,192]{3,2,1,0:T(8,128)(2,1)} %param.9) | copy-start | bytes 995332
  3.9 9.6 %collective-permute-start.4 = (bf16[2,2,192,256]{3,2,1,0:T(8,128)(2,1)S(1)}, bf16[2,2,192,256]{3,2,1,0:T(8,128)(2,1)S(1)}, u32[]{:S(2)}, u32[]{:S(2)}) collective-permute-start(bf16[2,2,192,256]{3,2,1,0:T(8,128)(2,1)S(1)} %get-tuple-element.26), channel_id=1, source_target_pairs={{0,64},{1,65},{2,66},{3,67},{4,5},{5,4},{6,7},{7,6},{8,72},{9,73},... | collective-permute-start | bytes 1179656 | tf_op jit(solution)/shard_map/ppermute | solution.py:238
  5.6 9.8 %collective-permute-start.5 = (bf16[2,2,192,256]{3,2,1,0:T(8,128)(2,1)S(1)}, bf16[2,2,192,256]{3,2,1,0:T(8,128)(2,1)S(1)}, u32[]{:S(2)}, u32[]{:S(2)}) collective-permute-start(bf16[2,2,192,256]{3,2,1,0:T(8,128)(2,1)S(1)} %get-tuple-element.27), channel_id=1, source_target_pairs={{0,192},{1,193},{2,194},{3,195},{4,7},{5,6},{6,5},{7,4},{8,200},{9... | collective-permute-start | bytes 1179656 | tf_op jit(solution)/shard_map/ppermute | solution.py:238
  8.2 7.3 %copy-start.3 = (s32[4]{0:T(128)S(1)}, s32[4]{0:T(128)}, u32[]{:S(2)}) copy-start(s32[4]{0:T(128)} %param.6) | copy-start | bytes 52
  10.1 8.0 %collective-permute-start.2 = (bf16[2,2,192,256]{3,2,1,0:T(8,128)(2,1)S(1)}, bf16[2,2,192,256]{3,2,1,0:T(8,128)(2,1)S(1)}, u32[]{:S(2)}, u32[]{:S(2)}) collective-permute-start(bf16[2,2,192,256]{3,2,1,0:T(8,128)(2,1)S(1)} %get-tuple-element.24), channel_id=1, source_target_pairs={{0,1},{1,0},{2,3},{3,2},{4,68},{5,69},{6,70},{7,71},{8,9},{9,8},{1... | collective-permute-start | bytes 1179656 | tf_op jit(solution)/shard_map/ppermute | solution.py:238
  12.3 7.8 %collective-permute-start.3 = (bf16[2,2,192,256]{3,2,1,0:T(8,128)(2,1)S(1)}, bf16[2,2,192,256]{3,2,1,0:T(8,128)(2,1)S(1)}, u32[]{:S(2)}, u32[]{:S(2)}) collective-permute-start(bf16[2,2,192,256]{3,2,1,0:T(8,128)(2,1)S(1)} %get-tuple-element.25), channel_id=1, source_target_pairs={{0,3},{1,2},{2,1},{3,0},{4,196},{5,197},{6,198},{7,199},{8,11},{9,... | collective-permute-start | bytes 1179656 | tf_op jit(solution)/shard_map/ppermute | solution.py:238

commit v7 on v6

--- a/solution.py
+++ b/solution.py
@@ -49,6 +49,10 @@
                 tap = kt * 3 + jnp.where(flip, 2 - kh, kh)
                 term = jnp.dot(w_ref[tap], panels[row], preferred_element_type=jnp.float32)
                 acc = term if acc is None else acc + term
+    return columns(acc)
+
+
+def columns(acc):
     return shifted(acc[:C], 1) + acc[C : 2 * C] + shifted(acc[2 * C :], -1)
 
 
@@ -81,7 +85,8 @@
 
 
 def previous_kernel(core, x_ref, gain_ref, w_ref, s1_ref, uw_ref, *refs):
-    s_ref, first_ref, second_ref, u_ref = refs[-4:]
+    s_ref, first_ref, second_ref, u_ref = refs[-4:] if core == 0 else refs[:4]
+    four_ref = refs[0] if core == 0 else refs[4]
     tm = lax.axis_index("tm")
     flip = flipped()
 
@@ -92,7 +97,12 @@
         for fo in range(2):
             acts = [(0, a[0]), (1, a[1])] if fo == 0 else [(0, a[1])]
             for ro in range(4):
-                total = s1_ref[fo, ro] + conv_terms(acts, w_ref, ro, flip)
+                if core == 0 and fo == 0 and ro in (1, 2):
+                    four = jnp.concatenate(a[0] + a[1], axis=0)
+                    terms = columns(jnp.dot(four_ref[ro - 1], four, preferred_element_type=jnp.float32))
+                else:
+                    terms = conv_terms(acts, w_ref, ro, flip)
+                total = s1_ref[fo, ro] + terms
                 s_ref[fo, ro] = total
                 to_ref = first_ref if ro >= 2 else second_ref
                 to_ref[fo, ro % 2] = total.astype(jnp.bfloat16)
@@ -102,6 +112,11 @@
         w0, w1, w2 = (uw_ref[jnp.where(flip, 2 - kh, kh)].astype(jnp.float32) for kh in range(3))
         u_ref[0] = jnp.concatenate([w0, w1 + w2], axis=1).astype(jnp.bfloat16)
         u_ref[1] = jnp.concatenate([w0 + w1, w2], axis=1).astype(jnp.bfloat16)
+        if core == 1:
+            for ro in (1, 2):
+                khs = [row - ro + 2 for row in range(2)]
+                taps = [w_ref[kt * 3 + jnp.where(flip, 2 - kh, kh)] for kt in range(2) for kh in khs]
+                four_ref[ro - 1] = jnp.concatenate(taps, axis=1)
 
 
 def hidden_row(s_ref, f, ro, got_ref):
@@ -257,7 +272,7 @@
     def rows_swap(phase, core):
         def partner(d, t, r):
             if t % 2 != core:
-                return idle(phase)(d), t, r
+                return idle(1 - phase)(d), t, r
             if phase == 0:
                 return d, t, r ^ 1
             return d, t, ((r + 1) % n_rows if r % 2 else (r - 1) % n_rows)
@@ -279,18 +294,18 @@
     )
     specs = [VMEM] * 5
     wide = jax.ShapeDtypeStruct((2, 3 * C2, 2 * C), jnp.bfloat16)
-    s, odd1, odd2, u = call(
-        functools.partial(previous_kernel, 1), (part, half, half, wide), specs, 1_020_000_000
+    s, odd1, odd2, u, four = call(
+        functools.partial(previous_kernel, 1), (part, half, half, wide, shape(2, 3 * C, 4 * C)), specs, 1_020_000_000
     )(from_chip, gain, w, s1, uw)
     odd1 = swap(odd1, rows_swap(0, 1))
     odd2 = swap(odd2, rows_swap(1, 1))
     s, even1, even2, u = call(
         functools.partial(previous_kernel, 0),
         (part, half, half, wide),
-        specs + [VMEM] * 2,
+        specs + [VMEM] * 3,
         1_020_000_000,
-        input_output_aliases={5: 0, 6: 3},
-    )(from_z, gain, w, s1, uw, s, u)
+        input_output_aliases={6: 0, 7: 3},
+    )(from_z, gain, w, s1, uw, four, s, u)
     even1 = swap(even1, rows_swap(0, 0))
     even2 = swap(even2, rows_swap(1, 0))
     out = jax.ShapeDtypeStruct((own_tiles, frames, 2 * rows, C2, 2 * W), jnp.bfloat16)

time: 21.9 us -> 21.8 us (level)
  starting transfers between devices: 8.37 us -> 7.77 us
  waiting for transfers between devices: 6.98 us -> 7.26 us
  Pallas kernels: 6.31 us -> 6.55 us
    ppermute x6, starting transfers between devices: 8.37 us -> 7.77 us  [swap(): lax.ppermute(value, AXES, [(index(*p), index(*partner(*p))) for p in plac...]
    pallas_call x1, Pallas kernels: 0.19 us -> 0.49 us  [on_device(): call(functools.partial(previous_kernel, 1), (part, half, half, wide, shap...]
    ppermute x6, waiting for transfers between devices: 6.98 us -> 7.26 us  [swap(): lax.ppermute(value, AXES, [(index(*p), index(*partner(*p))) for p in plac...]
  transfers between devices with their start and end apart: 6 -> 6, of which waited for: 5 -> 5; matrix products, arithmetic and copies ran while one was open for 0% -> 0% of each run, Pallas kernels for 21% -> 22%
where the time goes in v7:
time: 21.8 us; the launch traced here: 21.7 us
  starting transfers between devices  7.77 us (36%)
  waiting for transfers between devices  7.26 us (33%)
  Pallas kernels  6.55 us (30%)
    ppermute x6, starting transfers between devices, swap(): lax.ppermute(value, AXES, [(index(*p), index(*partner(*p))) for p in plac...  7.77 us
    ppermute x6, waiting for transfers between devices, swap(): lax.ppermute(value, AXES, [(index(*p), index(*partner(*p))) for p in plac...  7.26 us
    pallas_call x1, Pallas kernels, on_device(): call(own_kernel, (part, square), [VMEM] * 4, 1020000000, input_output_ali...  1.83 us
    pallas_call x1, Pallas kernels, on_device(): call(functools.partial(previous_kernel, 0), (part, half, half, wide), spe...  1.77 us
    pallas_call x1, Pallas kernels, on_device(): call(even_second_kernel, out, [VMEM] * 8 + [ANY], 700000000, ANY, scratch...  1.73 us
    pallas_call x1, Pallas kernels, on_device(): call(even_first_kernel, (out, rows_of, shape(2, 2, 1, C2, 2 * W)), [VMEM]...  0.65 us
    pallas_call x1, Pallas kernels, on_device(): call(functools.partial(previous_kernel, 1), (part, half, half, wide, shap...  0.49 us
  transfers between devices with their start and end apart: 6, of which 5 were waited for; matrix products, arithmetic and copies ran while one was open for 0% of the time, Pallas kernels for 22%

profile of v7, /device:TPU:2, one launch (start us, length us, event | category | flops | bytes accessed | tf_op | source)
XLA Modules:
  0.0 21.7 jit_solution(5850815818421904701)
XLA Ops:
  0.0 0.0 copy-start.4
  0.0 0.0 copy-start
  0.0 0.0 copy-start.2
  0.0 0.1 collective-permute-start.1
  0.1 1.7 %collective-permute-start = (bf16[2,2,2,192,128]{4,3,2,1,0:T(8,128)(2,1)}, bf16[2,2,2,192,128]{4,3,2,1,0:T(8,128)(2,1)S(1)}, u32[]{:S(2)}, u32[]{:S(2)}) collective-permute-start(bf16[2,2,2,192,128]{4,3,2,1,0:T(8,128)(2,1)} %x_ref.1), channel_id=1, source_target_pairs={{0,64},{1,65},{2,66},{3,67},{4,8},{5,9},{6,10},{7,11},{8,4},{9,5},... | collective-permute-start | bytes 1179656 | tf_op jit(solution)/shard_map/ppermute | solution.py:253
  1.8 0.0 copy-done.4
  1.8 0.1 copy-done
  1.9 0.0 copy-done.2
  1.9 0.0 copy-start.1
  1.9 1.8 %shard_map.56 = (f32[2,4,192,256]{3,2,1,0:T(8,128)S(1)}, bf16[256,256]{1,0:T(8,128)(2,1)S(1)}) custom-call(bf16[2,2,2,192,128]{4,3,2,1,0:T(8,128)(2,1)S(1)} %copy-done.4, f32[1,192]{1,0:T(1,128)S(1)} %bitcast.9, bf16[9,576,192]{2,1,0:T(8,128)(2,1)S(1)} %bitcast.4, bf16[256,256]{1,0:T(8,128)(2,1)S(1)} %shard_map.55.spread_ref), custom_call_target="tpu_custom_call", output_to_operand_aliasing={{1}: (3, {})} | custom-call | flops 1020000000 | bytes 4000000 | tf_op jit(solution)/shard_map/pallas_call | solution.py:292
  3.7 0.0 collective-permute-done.1.x_ref
  3.7 0.0 copy-done.1
  3.7 0.5 %shard_map.57 = (f32[2,4,192,256]{3,2,1,0:T(8,128)S(1)}, bf16[2,2,192,256]{3,2,1,0:T(8,128)(2,1)S(1)}, bf16[2,2,192,256]{3,2,1,0:T(8,128)(2,1)S(1)}, bf16[2,288,...) custom-call(bf16[2,2,2,192,128]{4,3,2,1,0:T(8,128)(2,1)S(1)} %collective-permute-done.1.x_ref, f32[1,192]{1,0:T(1,128)S(1)} %bitcast.10, ...), custom_call_target="tpu_custom_call" | custom-call | flops 1020000000 | bytes 4000000 | tf_op jit(solution)/shard_map/pallas_call | solution.py:297
  4.2 3.1 %collective-permute-start.4 = (bf16[2,2,192,256]{3,2,1,0:T(8,128)(2,1)S(1)}, bf16[2,2,192,256]{3,2,1,0:T(8,128)(2,1)S(1)}, u32[]{:S(2)}, u32[]{:S(2)}) collective-permute-start(bf16[2,2,192,256]{3,2,1,0:T(8,128)(2,1)S(1)} %get-tuple-element.28), channel_id=1, source_target_pairs={{0,192},{1,193},{2,194},{3,195},{4,5},{5,4},{6,7},{7,6},{8,200},{9... | collective-permute-start | bytes 1179656 | tf_op jit(solution)/shard_map/ppermute | solution.py:253
  7.3 0.1 collective-permute-start.5
  7.5 0.7 %collective-permute-done.x_ref = bf16[2,2,2,192,128]{4,3,2,1,0:T(8,128)(2,1)S(1)} collective-permute-done((bf16[2,2,2,192,128]{4,3,2,1,0:T(8,128)(2,1)}, bf16[2,2,2,192,128]{4,3,2,1,0:T(8,128)(2,1)S(1)}, u32[]{:S(2)}, u32[]{:S(2)}) %collective-permute-start) | collective-permute-done | bytes 393248 | tf_op jit(solution)/shard_map/ppermute | solution.py:253
  8.2 0.0 copy-start.3
  8.2 1.8 %shard_map.58 = (f32[2,4,192,256]{3,2,1,0:T(8,128)S(1)}, bf16[2,2,192,256]{3,2,1,0:T(8,128)(2,1)S(1)}, bf16[2,2,192,256]{3,2,1,0:T(8,128)(2,1)S(1)}, bf16[2,288,384]{2,1,0:T(8,128)(2,1)S(1)}) custom-call(bf16[2,2,2,192,128]{4,3,2,1,0:T(8,128)(2,1)S(1)} %collective-permute-done.x_ref, ...), custom_call_target="tpu_custom_call", output_to_operand_aliasing={{0}: (6, {}), {3}: (7, {})} | custom-call | flops 1020000000 | bytes 4000000 | tf_op jit(solution)/shard_map/pallas_call | solution.py:302
  10.0 2.3 %collective-permute-start.2 = (bf16[2,2,192,256]{3,2,1,0:T(8,128)(2,1)S(1)}, bf16[2,2,192,256]{3,2,1,0:T(8,128)(2,1)S(1)}, u32[]{:S(2)}, u32[]{:S(2)}) collective-permute-start(bf16[2,2,192,256]{3,2,1,0:T(8,128)(2,1)S(1)} %get-tuple-element.26), channel_id=1, source_target_pairs={{0,1},{1,0},{2,3},{3,2},{4,196},{5,197},{6,198},{7,199},{8,9},{9,8... | collective-permute-start | bytes 1179656 | tf_op jit(solution)/shard_map/ppermute | solution.py:253
  12.2 0.5 %collective-permute-start.3 = (bf16[2,2,192,256]{3,2,1,0:T(8,128)(2,1)S(1)}, bf16[2,2,192,256]{3,2,1,0:T(8,128)(2,1)S(1)}, u32[]{:S(2)}, u32[]{:S(2)}) collective-permute-start(bf16[2,2,192,256]{3,2,1,0:T(8,128)(2,1)S(1)} %get-tuple-element.27), channel_id=1, source_target_pairs={{0,3},{1,2},{2,1},{3,0},{4,68},{5,69},{6,70},{7,71},{8,11},{9,10},... | collective-permute-start | bytes 1179656 | tf_op jit(solution)/shard_map/ppermute | solution.py:253
  12.7 1.4 %collective-permute-done.4.first_ref = bf16[2,2,192,256]{3,2,1,0:T(8,128)(2,1)S(1)} collective-permute-done((bf16[2,2,192,256]{3,2,1,0:T(8,128)(2,1)S(1)}, bf16[2,2,192,256]{3,2,1,0:T(8,128)(2,1)S(1)}, u32[]{:S(2)}, u32[]{:S(2)}) %collective-permute-start.4) | collective-permute-done | bytes 393248 | tf_op jit(solution)/shard_map/ppermute | solution.py:253
  14.1 2.1 %collective-permute-done.5.second_ref = bf16[2,2,192,256]{3,2,1,0:T(8,128)(2,1)S(1)} collective-permute-done((bf16[2,2,192,256]{3,2,1,0:T(8,128)(2,1)S(1)}, bf16[2,2,192,256]{3,2,1,0:T(8,128)(2,1)S(1)}, u32[]{:S(2)}, u32[]{:S(2)}) %collective-permute-start.5) | collective-permute-done | bytes 393248 | tf_op jit(solution)/shard_map/ppermute | solution.py:253
  16.3 0.0 copy-done.3
  16.3 1.7 %collective-permute-done.2.first_ref._ = bf16[2,2,192,256]{3,2,1,0:T(8,128)(2,1)S(1)} collective-permute-done((bf16[2,2,192,256]{3,2,1,0:T(8,128)(2,1)S(1)}, bf16[2,2,192,256]{3,2,1,0:T(8,128)(2,1)S(1)}, u32[]{:S(2)}, u32[]{:S(2)}) %collective-permute-start.2) | collective-permute-done | bytes 393248 | tf_op jit(solution)/shard_map/ppermute | solution.py:253
  18.0 0.6 %shard_map.60 = (bf16[2,2,4,96,256]{4,3,2,1,0:T(8,128)(2,1)}, bf16[2,768,256]{2,1,0:T(8,128)(2,1)S(1)}, bf16[2,2,1,96,256]{4,3,2,1,0:T(8,128)(2,1)S(1)}) custom-call(f32[2,4,192,256]{3,2,1,0:T(8,128)S(1)} %get-tuple-element.23.s_ref, bf16[2,288,384]{2,1,0:T(8,128)(2,1)S(1)} %get-tuple-element.24.u_ref, ...), custom_call_target="tpu_custom_call", output_to_operand_aliasing={{0}: (5, {})} | custom-call | flops 900000000 | bytes 4000000 | tf_op jit(solution)/shard_map/pallas_call | solution.py:323
  18.6 1.4 %collective-permute-done.3.second_ref = bf16[2,2,192,256]{3,2,1,0:T(8,128)(2,1)S(1)} collective-permute-done((bf16[2,2,192,256]{3,2,1,0:T(8,128)(2,1)S(1)}, bf16[2,2,192,256]{3,2,1,0:T(8,128)(2,1)S(1)}, u32[]{:S(2)}, u32[]{:S(2)}) %collective-permute-start.3) | collective-permute-done | bytes 393248 | tf_op jit(solution)/shard_map/ppermute | solution.py:253
  20.0 1.7 %shard_map.61 = bf16[2,2,4,96,256]{4,3,2,1,0:T(8,128)(2,1)} custom-call(f32[2,4,192,256]{3,2,1,0:T(8,128)S(1)} %get-tuple-element.23.s_ref, bf16[2,288,384]{2,1,0:T(8,128)(2,1)S(1)} %get-tuple-element.24.u_ref, s32[1,4]{1,0:T(1,128)S(1)} %bitcast.14, bf16[256,256]{1,0:T(8,128)(2,1)S(1)} %get-tuple-element.25.spread_ref, ...), custom_call_target="tpu_custom_call", output_to_operand_aliasing={{}: (8, {})} | custom-call | flops 700000000 | bytes 4000000 | tf_op jit(solution)/shard_map/pallas_call | solution.py:332
  (2 shorter events, 0.1 us)
Async XLA Ops:
  0.0 1.8 %copy-start.4 = (bf16[2,2,2,192,128]{4,3,2,1,0:T(8,128)(2,1)S(1)}, bf16[2,2,2,192,128]{4,3,2,1,0:T(8,128)(2,1)}, u32[]{:S(2)}) copy-start(bf16[2,2,2,192,128]{4,3,2,1,0:T(8,128)(2,1)} %x_ref.1) | copy-start | bytes 1179652
  0.0 1.9 %copy-start = (bf16[3,3,3,192,192]{4,3,2,1,0:T(8,128)(2,1)S(1)}, bf16[3,3,3,192,192]{4,3,2,1,0:T(8,128)(2,1)}, u32[]{:S(2)}) copy-start(bf16[3,3,3,192,192]{4,3,2,1,0:T(8,128)(2,1)} %param.8) | copy-start | bytes 5971972
  0.0 1.9 %copy-start.2 = (f32[192]{0:T(256)S(1)}, f32[192]{0:T(256)}, u32[]{:S(2)}) copy-start(f32[192]{0:T(256)} %param.7) | copy-start | bytes 2308
  0.0 3.7 %collective-permute-start.1 = (bf16[2,2,2,192,128]{4,3,2,1,0:T(8,128)(2,1)}, bf16[2,2,2,192,128]{4,3,2,1,0:T(8,128)(2,1)S(1)}, u32[]{:S(2)}, u32[]{:S(2)}) collective-permute-start(bf16[2,2,2,192,128]{4,3,2,1,0:T(8,128)(2,1)} %x_ref.1), channel_id=1, source_target_pairs={{0,4},{1,5},{2,6},{3,7},{4,0},{5,1},{6,2},{7,3},{8,12},{9,13},{10,... | collective-permute-start | bytes 1179656 | tf_op jit(solution)/shard_map/ppermute | solution.py:253
  0.1 8.1 %collective-permute-start = (bf16[2,2,2,192,128]{4,3,2,1,0:T(8,128)(2,1)}, bf16[2,2,2,192,128]{4,3,2,1,0:T(8,128)(2,1)S(1)}, u32[]{:S(2)}, u32[]{:S(2)}) collective-permute-start(bf16[2,2,2,192,128]{4,3,2,1,0:T(8,128)(2,1)} %x_ref.1), channel_id=1, source_target_pairs={{0,64},{1,65},{2,66},{3,67},{4,8},{5,9},{6,10},{7,11},{8,4},{9,5},... | collective-permute-start | bytes 1179656 | tf_op jit(solution)/shard_map/ppermute | solution.py:253
  1.9 1.8 %copy-start.1 = (bf16[3,3,96,192]{3,2,1,0:T(8,128)(2,1)S(1)}, bf16[3,3,96,192]{3,2,1,0:T(8,128)(2,1)}, u32[]{:S(2)}) copy-start(bf16[3,3,96,192]{3,2,1,0:T(8,128)(2,1)} %param.9) | copy-start | bytes 995332
  4.2 9.9 %collective-permute-start.4 = (bf16[2,2,192,256]{3,2,1,0:T(8,128)(2,1)S(1)}, bf16[2,2,192,256]{3,2,1,0:T(8,128)(2,1)S(1)}, u32[]{:S(2)}, u32[]{:S(2)}) collective-permute-start(bf16[2,2,192,256]{3,2,1,0:T(8,128)(2,1)S(1)} %get-tuple-element.28), channel_id=1, source_target_pairs={{0,192},{1,193},{2,194},{3,195},{4,5},{5,4},{6,7},{7,6},{8,200},{9... | collective-permute-start | bytes 1179656 | tf_op jit(solution)/shard_map/ppermute | solution.py:253
  7.3 8.9 %collective-permute-start.5 = (bf16[2,2,192,256]{3,2,1,0:T(8,128)(2,1)S(1)}, bf16[2,2,192,256]{3,2,1,0:T(8,128)(2,1)S(1)}, u32[]{:S(2)}, u32[]{:S(2)}) collective-permute-start(bf16[2,2,192,256]{3,2,1,0:T(8,128)(2,1)S(1)} %get-tuple-element.29), channel_id=1, source_target_pairs={{0,64},{1,65},{2,66},{3,67},{4,7},{5,6},{6,5},{7,4},{8,72},{9,73},... | collective-permute-start | bytes 1179656 | tf_op jit(solution)/shard_map/ppermute | solution.py:253
  8.2 8.1 %copy-start.3 = (s32[4]{0:T(128)S(1)}, s32[4]{0:T(128)}, u32[]{:S(2)}) copy-start(s32[4]{0:T(128)} %param.6) | copy-start | bytes 52
  10.0 8.0 %collective-permute-start.2 = (bf16[2,2,192,256]{3,2,1,0:T(8,128)(2,1)S(1)}, bf16[2,2,192,256]{3,2,1,0:T(8,128)(2,1)S(1)}, u32[]{:S(2)}, u32[]{:S(2)}) collective-permute-start(bf16[2,2,192,256]{3,2,1,0:T(8,128)(2,1)S(1)} %get-tuple-element.26), channel_id=1, source_target_pairs={{0,1},{1,0},{2,3},{3,2},{4,196},{5,197},{6,198},{7,199},{8,9},{9,8... | collective-permute-start | bytes 1179656 | tf_op jit(solution)/shard_map/ppermute | solution.py:253
  12.2 7.8 %collective-permute-start.3 = (bf16[2,2,192,256]{3,2,1,0:T(8,128)(2,1)S(1)}, bf16[2,2,192,256]{3,2,1,0:T(8,128)(2,1)S(1)}, u32[]{:S(2)}, u32[]{:S(2)}) collective-permute-start(bf16[2,2,192,256]{3,2,1,0:T(8,128)(2,1)S(1)} %get-tuple-element.27), channel_id=1, source_target_pairs={{0,3},{1,2},{2,1},{3,0},{4,68},{5,69},{6,70},{7,71},{8,11},{9,10},... | collective-permute-start | bytes 1179656 | tf_op jit(solution)/shard_map/ppermute | solution.py:253

commit v8 on v7

--- a/solution.py
+++ b/solution.py
@@ -152,7 +152,7 @@
         if out_ref is not None:
             for t in range(2):
                 copies.append(out_copy(buf_ref, out_ref, sem, f, t, todo, flip))
-                copies[-1].start()
+                copies[-1].start(priority=1)
     for copy in copies:
         copy.wait()
 

time: 21.8 us -> 21.8 us (level)
  no operation moved by 1% of the time
where the time goes in v8:
time: 21.8 us; the launch traced here: 21.7 us
  starting transfers between devices  7.77 us (36%)
  waiting for transfers between devices  7.26 us (33%)
  Pallas kernels  6.55 us (30%)
    ppermute x6, starting transfers between devices, swap(): lax.ppermute(value, AXES, [(index(*p), index(*partner(*p))) for p in plac...  7.77 us
    ppermute x6, waiting for transfers between devices, swap(): lax.ppermute(value, AXES, [(index(*p), index(*partner(*p))) for p in plac...  7.26 us
    pallas_call x1, Pallas kernels, on_device(): call(own_kernel, (part, square), [VMEM] * 4, 1020000000, input_output_ali...  1.83 us
    pallas_call x1, Pallas kernels, on_device(): call(functools.partial(previous_kernel, 0), (part, half, half, wide), spe...  1.77 us
    pallas_call x1, Pallas kernels, on_device(): call(even_second_kernel, out, [VMEM] * 8 + [ANY], 700000000, ANY, scratch...  1.73 us
    pallas_call x1, Pallas kernels, on_device(): call(even_first_kernel, (out, rows_of, shape(2, 2, 1, C2, 2 * W)), [VMEM]...  0.65 us
    pallas_call x1, Pallas kernels, on_device(): call(functools.partial(previous_kernel, 1), (part, half, half, wide, shap...  0.49 us
  transfers between devices with their start and end apart: 6, of which 5 were waited for; matrix products, arithmetic and copies ran while one was open for 0% of the time, Pallas kernels for 22%

profile of v8, /device:TPU:2, one launch (start us, length us, event | category | flops | bytes accessed | tf_op | source)
XLA Modules:
  0.0 21.7 jit_solution(352022701142979384)
XLA Ops:
  0.0 0.0 copy-start.4
  0.0 0.0 copy-start
  0.0 0.0 copy-start.2
  0.0 0.1 collective-permute-start.1
  0.1 1.7 %collective-permute-start = (bf16[2,2,2,192,128]{4,3,2,1,0:T(8,128)(2,1)}, bf16[2,2,2,192,128]{4,3,2,1,0:T(8,128)(2,1)S(1)}, u32[]{:S(2)}, u32[]{:S(2)}) collective-permute-start(bf16[2,2,2,192,128]{4,3,2,1,0:T(8,128)(2,1)} %x_ref.1), channel_id=1, source_target_pairs={{0,64},{1,65},{2,66},{3,67},{4,8},{5,9},{6,10},{7,11},{8,4},{9,5},... | collective-permute-start | bytes 1179656 | tf_op jit(solution)/shard_map/ppermute | solution.py:253
  1.8 0.0 copy-done.4
  1.8 0.1 copy-done
  1.9 0.0 copy-done.2
  1.9 0.0 copy-start.1
  1.9 1.8 %shard_map.56 = (f32[2,4,192,256]{3,2,1,0:T(8,128)S(1)}, bf16[256,256]{1,0:T(8,128)(2,1)S(1)}) custom-call(bf16[2,2,2,192,128]{4,3,2,1,0:T(8,128)(2,1)S(1)} %copy-done.4, f32[1,192]{1,0:T(1,128)S(1)} %bitcast.9, bf16[9,576,192]{2,1,0:T(8,128)(2,1)S(1)} %bitcast.4, bf16[256,256]{1,0:T(8,128)(2,1)S(1)} %shard_map.55.spread_ref), custom_call_target="tpu_custom_call", output_to_operand_aliasing={{1}: (3, {})} | custom-call | flops 1020000000 | bytes 4000000 | tf_op jit(solution)/shard_map/pallas_call | solution.py:292
  3.7 0.0 collective-permute-done.1.x_ref
  3.7 0.0 copy-done.1
  3.7 0.5 %shard_map.57 = (f32[2,4,192,256]{3,2,1,0:T(8,128)S(1)}, bf16[2,2,192,256]{3,2,1,0:T(8,128)(2,1)S(1)}, bf16[2,2,192,256]{3,2,1,0:T(8,128)(2,1)S(1)}, bf16[2,288,...) custom-call(bf16[2,2,2,192,128]{4,3,2,1,0:T(8,128)(2,1)S(1)} %collective-permute-done.1.x_ref, f32[1,192]{1,0:T(1,128)S(1)} %bitcast.10, ...), custom_call_target="tpu_custom_call" | custom-call | flops 1020000000 | bytes 4000000 | tf_op jit(solution)/shard_map/pallas_call | solution.py:297
  4.2 3.1 %collective-permute-start.4 = (bf16[2,2,192,256]{3,2,1,0:T(8,128)(2,1)S(1)}, bf16[2,2,192,256]{3,2,1,0:T(8,128)(2,1)S(1)}, u32[]{:S(2)}, u32[]{:S(2)}) collective-permute-start(bf16[2,2,192,256]{3,2,1,0:T(8,128)(2,1)S(1)} %get-tuple-element.28), channel_id=1, source_target_pairs={{0,192},{1,193},{2,194},{3,195},{4,5},{5,4},{6,7},{7,6},{8,200},{9... | collective-permute-start | bytes 1179656 | tf_op jit(solution)/shard_map/ppermute | solution.py:253
  7.3 0.1 collective-permute-start.5
  7.5 0.7 %collective-permute-done.x_ref = bf16[2,2,2,192,128]{4,3,2,1,0:T(8,128)(2,1)S(1)} collective-permute-done((bf16[2,2,2,192,128]{4,3,2,1,0:T(8,128)(2,1)}, bf16[2,2,2,192,128]{4,3,2,1,0:T(8,128)(2,1)S(1)}, u32[]{:S(2)}, u32[]{:S(2)}) %collective-permute-start) | collective-permute-done | bytes 393248 | tf_op jit(solution)/shard_map/ppermute | solution.py:253
  8.2 0.0 copy-start.3
  8.2 1.8 %shard_map.58 = (f32[2,4,192,256]{3,2,1,0:T(8,128)S(1)}, bf16[2,2,192,256]{3,2,1,0:T(8,128)(2,1)S(1)}, bf16[2,2,192,256]{3,2,1,0:T(8,128)(2,1)S(1)}, bf16[2,288,384]{2,1,0:T(8,128)(2,1)S(1)}) custom-call(bf16[2,2,2,192,128]{4,3,2,1,0:T(8,128)(2,1)S(1)} %collective-permute-done.x_ref, ...), custom_call_target="tpu_custom_call", output_to_operand_aliasing={{0}: (6, {}), {3}: (7, {})} | custom-call | flops 1020000000 | bytes 4000000 | tf_op jit(solution)/shard_map/pallas_call | solution.py:302
  10.0 2.3 %collective-permute-start.2 = (bf16[2,2,192,256]{3,2,1,0:T(8,128)(2,1)S(1)}, bf16[2,2,192,256]{3,2,1,0:T(8,128)(2,1)S(1)}, u32[]{:S(2)}, u32[]{:S(2)}) collective-permute-start(bf16[2,2,192,256]{3,2,1,0:T(8,128)(2,1)S(1)} %get-tuple-element.26), channel_id=1, source_target_pairs={{0,1},{1,0},{2,3},{3,2},{4,196},{5,197},{6,198},{7,199},{8,9},{9,8... | collective-permute-start | bytes 1179656 | tf_op jit(solution)/shard_map/ppermute | solution.py:253
  12.2 0.5 %collective-permute-start.3 = (bf16[2,2,192,256]{3,2,1,0:T(8,128)(2,1)S(1)}, bf16[2,2,192,256]{3,2,1,0:T(8,128)(2,1)S(1)}, u32[]{:S(2)}, u32[]{:S(2)}) collective-permute-start(bf16[2,2,192,256]{3,2,1,0:T(8,128)(2,1)S(1)} %get-tuple-element.27), channel_id=1, source_target_pairs={{0,3},{1,2},{2,1},{3,0},{4,68},{5,69},{6,70},{7,71},{8,11},{9,10},... | collective-permute-start | bytes 1179656 | tf_op jit(solution)/shard_map/ppermute | solution.py:253
  12.7 1.4 %collective-permute-done.4.first_ref = bf16[2,2,192,256]{3,2,1,0:T(8,128)(2,1)S(1)} collective-permute-done((bf16[2,2,192,256]{3,2,1,0:T(8,128)(2,1)S(1)}, bf16[2,2,192,256]{3,2,1,0:T(8,128)(2,1)S(1)}, u32[]{:S(2)}, u32[]{:S(2)}) %collective-permute-start.4) | collective-permute-done | bytes 393248 | tf_op jit(solution)/shard_map/ppermute | solution.py:253
  14.1 2.1 %collective-permute-done.5.second_ref = bf16[2,2,192,256]{3,2,1,0:T(8,128)(2,1)S(1)} collective-permute-done((bf16[2,2,192,256]{3,2,1,0:T(8,128)(2,1)S(1)}, bf16[2,2,192,256]{3,2,1,0:T(8,128)(2,1)S(1)}, u32[]{:S(2)}, u32[]{:S(2)}) %collective-permute-start.5) | collective-permute-done | bytes 393248 | tf_op jit(solution)/shard_map/ppermute | solution.py:253
  16.3 0.0 copy-done.3
  16.3 1.7 %collective-permute-done.2.first_ref._ = bf16[2,2,192,256]{3,2,1,0:T(8,128)(2,1)S(1)} collective-permute-done((bf16[2,2,192,256]{3,2,1,0:T(8,128)(2,1)S(1)}, bf16[2,2,192,256]{3,2,1,0:T(8,128)(2,1)S(1)}, u32[]{:S(2)}, u32[]{:S(2)}) %collective-permute-start.2) | collective-permute-done | bytes 393248 | tf_op jit(solution)/shard_map/ppermute | solution.py:253
  18.0 0.6 %shard_map.60 = (bf16[2,2,4,96,256]{4,3,2,1,0:T(8,128)(2,1)}, bf16[2,768,256]{2,1,0:T(8,128)(2,1)S(1)}, bf16[2,2,1,96,256]{4,3,2,1,0:T(8,128)(2,1)S(1)}) custom-call(f32[2,4,192,256]{3,2,1,0:T(8,128)S(1)} %get-tuple-element.23.s_ref, bf16[2,288,384]{2,1,0:T(8,128)(2,1)S(1)} %get-tuple-element.24.u_ref, ...), custom_call_target="tpu_custom_call", output_to_operand_aliasing={{0}: (5, {})} | custom-call | flops 900000000 | bytes 4000000 | tf_op jit(solution)/shard_map/pallas_call | solution.py:323
  18.6 1.4 %collective-permute-done.3.second_ref = bf16[2,2,192,256]{3,2,1,0:T(8,128)(2,1)S(1)} collective-permute-done((bf16[2,2,192,256]{3,2,1,0:T(8,128)(2,1)S(1)}, bf16[2,2,192,256]{3,2,1,0:T(8,128)(2,1)S(1)}, u32[]{:S(2)}, u32[]{:S(2)}) %collective-permute-start.3) | collective-permute-done | bytes 393248 | tf_op jit(solution)/shard_map/ppermute | solution.py:253
  20.0 1.7 %shard_map.61 = bf16[2,2,4,96,256]{4,3,2,1,0:T(8,128)(2,1)} custom-call(f32[2,4,192,256]{3,2,1,0:T(8,128)S(1)} %get-tuple-element.23.s_ref, bf16[2,288,384]{2,1,0:T(8,128)(2,1)S(1)} %get-tuple-element.24.u_ref, s32[1,4]{1,0:T(1,128)S(1)} %bitcast.14, bf16[256,256]{1,0:T(8,128)(2,1)S(1)} %get-tuple-element.25.spread_ref, ...), custom_call_target="tpu_custom_call", output_to_operand_aliasing={{}: (8, {})} | custom-call | flops 700000000 | bytes 4000000 | tf_op jit(solution)/shard_map/pallas_call | solution.py:332
  (2 shorter events, 0.1 us)
Async XLA Ops:
  0.0 1.8 %copy-start.4 = (bf16[2,2,2,192,128]{4,3,2,1,0:T(8,128)(2,1)S(1)}, bf16[2,2,2,192,128]{4,3,2,1,0:T(8,128)(2,1)}, u32[]{:S(2)}) copy-start(bf16[2,2,2,192,128]{4,3,2,1,0:T(8,128)(2,1)} %x_ref.1) | copy-start | bytes 1179652
  0.0 1.9 %copy-start = (bf16[3,3,3,192,192]{4,3,2,1,0:T(8,128)(2,1)S(1)}, bf16[3,3,3,192,192]{4,3,2,1,0:T(8,128)(2,1)}, u32[]{:S(2)}) copy-start(bf16[3,3,3,192,192]{4,3,2,1,0:T(8,128)(2,1)} %param.8) | copy-start | bytes 5971972
  0.0 1.9 %copy-start.2 = (f32[192]{0:T(256)S(1)}, f32[192]{0:T(256)}, u32[]{:S(2)}) copy-start(f32[192]{0:T(256)} %param.7) | copy-start | bytes 2308
  0.0 3.7 %collective-permute-start.1 = (bf16[2,2,2,192,128]{4,3,2,1,0:T(8,128)(2,1)}, bf16[2,2,2,192,128]{4,3,2,1,0:T(8,128)(2,1)S(1)}, u32[]{:S(2)}, u32[]{:S(2)}) collective-permute-start(bf16[2,2,2,192,128]{4,3,2,1,0:T(8,128)(2,1)} %x_ref.1), channel_id=1, source_target_pairs={{0,4},{1,5},{2,6},{3,7},{4,0},{5,1},{6,2},{7,3},{8,12},{9,13},{10,... | collective-permute-start | bytes 1179656 | tf_op jit(solution)/shard_map/ppermute | solution.py:253
  0.1 8.1 %collective-permute-start = (bf16[2,2,2,192,128]{4,3,2,1,0:T(8,128)(2,1)}, bf16[2,2,2,192,128]{4,3,2,1,0:T(8,128)(2,1)S(1)}, u32[]{:S(2)}, u32[]{:S(2)}) collective-permute-start(bf16[2,2,2,192,128]{4,3,2,1,0:T(8,128)(2,1)} %x_ref.1), channel_id=1, source_target_pairs={{0,64},{1,65},{2,66},{3,67},{4,8},{5,9},{6,10},{7,11},{8,4},{9,5},... | collective-permute-start | bytes 1179656 | tf_op jit(solution)/shard_map/ppermute | solution.py:253
  1.9 1.8 %copy-start.1 = (bf16[3,3,96,192]{3,2,1,0:T(8,128)(2,1)S(1)}, bf16[3,3,96,192]{3,2,1,0:T(8,128)(2,1)}, u32[]{:S(2)}) copy-start(bf16[3,3,96,192]{3,2,1,0:T(8,128)(2,1)} %param.9) | copy-start | bytes 995332
  4.2 9.9 %collective-permute-start.4 = (bf16[2,2,192,256]{3,2,1,0:T(8,128)(2,1)S(1)}, bf16[2,2,192,256]{3,2,1,0:T(8,128)(2,1)S(1)}, u32[]{:S(2)}, u32[]{:S(2)}) collective-permute-start(bf16[2,2,192,256]{3,2,1,0:T(8,128)(2,1)S(1)} %get-tuple-element.28), channel_id=1, source_target_pairs={{0,192},{1,193},{2,194},{3,195},{4,5},{5,4},{6,7},{7,6},{8,200},{9... | collective-permute-start | bytes 1179656 | tf_op jit(solution)/shard_map/ppermute | solution.py:253
  7.3 8.9 %collective-permute-start.5 = (bf16[2,2,192,256]{3,2,1,0:T(8,128)(2,1)S(1)}, bf16[2,2,192,256]{3,2,1,0:T(8,128)(2,1)S(1)}, u32[]{:S(2)}, u32[]{:S(2)}) collective-permute-start(bf16[2,2,192,256]{3,2,1,0:T(8,128)(2,1)S(1)} %get-tuple-element.29), channel_id=1, source_target_pairs={{0,64},{1,65},{2,66},{3,67},{4,7},{5,6},{6,5},{7,4},{8,72},{9,73},... | collective-permute-start | bytes 1179656 | tf_op jit(solution)/shard_map/ppermute | solution.py:253
  8.2 8.1 %copy-start.3 = (s32[4]{0:T(128)S(1)}, s32[4]{0:T(128)}, u32[]{:S(2)}) copy-start(s32[4]{0:T(128)} %param.6) | copy-start | bytes 52
  10.0 8.0 %collective-permute-start.2 = (bf16[2,2,192,256]{3,2,1,0:T(8,128)(2,1)S(1)}, bf16[2,2,192,256]{3,2,1,0:T(8,128)(2,1)S(1)}, u32[]{:S(2)}, u32[]{:S(2)}) collective-permute-start(bf16[2,2,192,256]{3,2,1,0:T(8,128)(2,1)S(1)} %get-tuple-element.26), channel_id=1, source_target_pairs={{0,1},{1,0},{2,3},{3,2},{4,196},{5,197},{6,198},{7,199},{8,9},{9,8... | collective-permute-start | bytes 1179656 | tf_op jit(solution)/shard_map/ppermute | solution.py:253
  12.2 7.8 %collective-permute-start.3 = (bf16[2,2,192,256]{3,2,1,0:T(8,128)(2,1)S(1)}, bf16[2,2,192,256]{3,2,1,0:T(8,128)(2,1)S(1)}, u32[]{:S(2)}, u32[]{:S(2)}) collective-permute-start(bf16[2,2,192,256]{3,2,1,0:T(8,128)(2,1)S(1)} %get-tuple-element.27), channel_id=1, source_target_pairs={{0,3},{1,2},{2,1},{3,0},{4,68},{5,69},{6,70},{7,71},{8,11},{9,10},... | collective-permute-start | bytes 1179656 | tf_op jit(solution)/shard_map/ppermute | solution.py:253

commit v9 on v7

--- a/solution.py
+++ b/solution.py
@@ -272,7 +272,7 @@
     def rows_swap(phase, core):
         def partner(d, t, r):
             if t % 2 != core:
-                return idle(1 - phase)(d), t, r
+                return idle(1 - phase if core else phase)(d), t, r
             if phase == 0:
                 return d, t, r ^ 1
             return d, t, ((r + 1) % n_rows if r % 2 else (r - 1) % n_rows)

time: 21.8 us -> 21.9 us (level)
  transfers between devices with their start and end apart: 6 -> 6, of which waited for: 5 -> 4; matrix products, arithmetic and copies ran while one was open for 0% -> 0% of each run, Pallas kernels for 22% -> 22%
where the time goes in v9:
time: 21.9 us; the launch traced here: 21.7 us
  starting transfers between devices  7.77 us (35%)
  waiting for transfers between devices  7.23 us (33%)
  Pallas kernels  6.57 us (30%)
    ppermute x6, starting transfers between devices, swap(): lax.ppermute(value, AXES, [(index(*p), index(*partner(*p))) for p in plac...  7.77 us
    ppermute x6, waiting for transfers between devices, swap(): lax.ppermute(value, AXES, [(index(*p), index(*partner(*p))) for p in plac...  7.23 us
    pallas_call x1, Pallas kernels, on_device(): call(own_kernel, (part, square), [VMEM] * 4, 1020000000, input_output_ali...  1.83 us
    pallas_call x1, Pallas kernels, on_device(): call(functools.partial(previous_kernel, 0), (part, half, half, wide), spe...  1.77 us
    pallas_call x1, Pallas kernels, on_device(): call(even_second_kernel, out, [VMEM] * 8 + [ANY], 700000000, ANY, scratch...  1.73 us
    pallas_call x1, Pallas kernels, on_device(): call(even_first_kernel, (out, rows_of, shape(2, 2, 1, C2, 2 * W)), [VMEM]...  0.68 us
    pallas_call x1, Pallas kernels, on_device(): call(functools.partial(previous_kernel, 1), (part, half, half, wide, shap...  0.49 us
  transfers between devices with their start and end apart: 6, of which 4 were waited for; matrix products, arithmetic and copies ran while one was open for 0% of the time, Pallas kernels for 22%

profile of v9, /device:TPU:2, one launch (start us, length us, event | category | flops | bytes accessed | tf_op | source)
XLA Modules:
  0.0 21.7 jit_solution(1012488068476665107)
XLA Ops:
  0.0 0.0 copy-start.4
  0.0 0.0 copy-start
  0.0 0.0 copy-start.2
  0.0 0.1 collective-permute-start.1
  0.1 1.7 %collective-permute-start = (bf16[2,2,2,192,128]{4,3,2,1,0:T(8,128)(2,1)}, bf16[2,2,2,192,128]{4,3,2,1,0:T(8,128)(2,1)S(1)}, u32[]{:S(2)}, u32[]{:S(2)}) collective-permute-start(bf16[2,2,2,192,128]{4,3,2,1,0:T(8,128)(2,1)} %x_ref.1), channel_id=1, source_target_pairs={{0,64},{1,65},{2,66},{3,67},{4,8},{5,9},{6,10},{7,11},{8,4},{9,5},... | collective-permute-start | bytes 1179656 | tf_op jit(solution)/shard_map/ppermute | solution.py:253
  1.8 0.0 copy-done.4
  1.8 0.1 copy-done
  1.9 0.0 copy-done.2
  1.9 0.0 copy-start.1
  1.9 1.8 %shard_map.56 = (f32[2,4,192,256]{3,2,1,0:T(8,128)S(1)}, bf16[256,256]{1,0:T(8,128)(2,1)S(1)}) custom-call(bf16[2,2,2,192,128]{4,3,2,1,0:T(8,128)(2,1)S(1)} %copy-done.4, f32[1,192]{1,0:T(1,128)S(1)} %bitcast.9, bf16[9,576,192]{2,1,0:T(8,128)(2,1)S(1)} %bitcast.4, bf16[256,256]{1,0:T(8,128)(2,1)S(1)} %shard_map.55.spread_ref), custom_call_target="tpu_custom_call", output_to_operand_aliasing={{1}: (3, {})} | custom-call | flops 1020000000 | bytes 4000000 | tf_op jit(solution)/shard_map/pallas_call | solution.py:292
  3.7 0.0 collective-permute-done.1.x_ref
  3.7 0.0 copy-done.1
  3.7 0.5 %shard_map.57 = (f32[2,4,192,256]{3,2,1,0:T(8,128)S(1)}, bf16[2,2,192,256]{3,2,1,0:T(8,128)(2,1)S(1)}, bf16[2,2,192,256]{3,2,1,0:T(8,128)(2,1)S(1)}, bf16[2,288,...) custom-call(bf16[2,2,2,192,128]{4,3,2,1,0:T(8,128)(2,1)S(1)} %collective-permute-done.1.x_ref, f32[1,192]{1,0:T(1,128)S(1)} %bitcast.10, ...), custom_call_target="tpu_custom_call" | custom-call | flops 1020000000 | bytes 4000000 | tf_op jit(solution)/shard_map/pallas_call | solution.py:297
  4.2 3.1 %collective-permute-start.4 = (bf16[2,2,192,256]{3,2,1,0:T(8,128)(2,1)S(1)}, bf16[2,2,192,256]{3,2,1,0:T(8,128)(2,1)S(1)}, u32[]{:S(2)}, u32[]{:S(2)}) collective-permute-start(bf16[2,2,192,256]{3,2,1,0:T(8,128)(2,1)S(1)} %get-tuple-element.28), channel_id=1, source_target_pairs={{0,192},{1,193},{2,194},{3,195},{4,5},{5,4},{6,7},{7,6},{8,200},{9... | collective-permute-start | bytes 1179656 | tf_op jit(solution)/shard_map/ppermute | solution.py:253
  7.3 0.1 collective-permute-start.5
  7.5 0.7 %collective-permute-done.x_ref = bf16[2,2,2,192,128]{4,3,2,1,0:T(8,128)(2,1)S(1)} collective-permute-done((bf16[2,2,2,192,128]{4,3,2,1,0:T(8,128)(2,1)}, bf16[2,2,2,192,128]{4,3,2,1,0:T(8,128)(2,1)S(1)}, u32[]{:S(2)}, u32[]{:S(2)}) %collective-permute-start) | collective-permute-done | bytes 393248 | tf_op jit(solution)/shard_map/ppermute | solution.py:253
  8.2 0.0 copy-start.3
  8.2 1.8 %shard_map.58 = (f32[2,4,192,256]{3,2,1,0:T(8,128)S(1)}, bf16[2,2,192,256]{3,2,1,0:T(8,128)(2,1)S(1)}, bf16[2,2,192,256]{3,2,1,0:T(8,128)(2,1)S(1)}, bf16[2,288,384]{2,1,0:T(8,128)(2,1)S(1)}) custom-call(bf16[2,2,2,192,128]{4,3,2,1,0:T(8,128)(2,1)S(1)} %collective-permute-done.x_ref, ...), custom_call_target="tpu_custom_call", output_to_operand_aliasing={{0}: (6, {}), {3}: (7, {})} | custom-call | flops 1020000000 | bytes 4000000 | tf_op jit(solution)/shard_map/pallas_call | solution.py:302
  10.0 2.3 %collective-permute-start.2 = (bf16[2,2,192,256]{3,2,1,0:T(8,128)(2,1)S(1)}, bf16[2,2,192,256]{3,2,1,0:T(8,128)(2,1)S(1)}, u32[]{:S(2)}, u32[]{:S(2)}) collective-permute-start(bf16[2,2,192,256]{3,2,1,0:T(8,128)(2,1)S(1)} %get-tuple-element.26), channel_id=1, source_target_pairs={{0,1},{1,0},{2,3},{3,2},{4,68},{5,69},{6,70},{7,71},{8,9},{9,8},{1... | collective-permute-start | bytes 1179656 | tf_op jit(solution)/shard_map/ppermute | solution.py:253
  12.2 0.5 %collective-permute-start.3 = (bf16[2,2,192,256]{3,2,1,0:T(8,128)(2,1)S(1)}, bf16[2,2,192,256]{3,2,1,0:T(8,128)(2,1)S(1)}, u32[]{:S(2)}, u32[]{:S(2)}) collective-permute-start(bf16[2,2,192,256]{3,2,1,0:T(8,128)(2,1)S(1)} %get-tuple-element.27), channel_id=1, source_target_pairs={{0,3},{1,2},{2,1},{3,0},{4,196},{5,197},{6,198},{7,199},{8,11},{9,... | collective-permute-start | bytes 1179656 | tf_op jit(solution)/shard_map/ppermute | solution.py:253
  12.7 0.6 %collective-permute-done.4.first_ref = bf16[2,2,192,256]{3,2,1,0:T(8,128)(2,1)S(1)} collective-permute-done((bf16[2,2,192,256]{3,2,1,0:T(8,128)(2,1)S(1)}, bf16[2,2,192,256]{3,2,1,0:T(8,128)(2,1)S(1)}, u32[]{:S(2)}, u32[]{:S(2)}) %collective-permute-start.4) | collective-permute-done | bytes 393248 | tf_op jit(solution)/shard_map/ppermute | solution.py:253
  13.3 5.8 %collective-permute-done.5.second_ref = bf16[2,2,192,256]{3,2,1,0:T(8,128)(2,1)S(1)} collective-permute-done((bf16[2,2,192,256]{3,2,1,0:T(8,128)(2,1)S(1)}, bf16[2,2,192,256]{3,2,1,0:T(8,128)(2,1)S(1)}, u32[]{:S(2)}, u32[]{:S(2)}) %collective-permute-start.5) | collective-permute-done | bytes 393248 | tf_op jit(solution)/shard_map/ppermute | solution.py:253
  19.1 0.0 copy-done.3
  19.1 0.0 collective-permute-done.2.first_ref._
  19.1 0.7 %shard_map.60 = (bf16[2,2,4,96,256]{4,3,2,1,0:T(8,128)(2,1)}, bf16[2,768,256]{2,1,0:T(8,128)(2,1)S(1)}, bf16[2,2,1,96,256]{4,3,2,1,0:T(8,128)(2,1)S(1)}) custom-call(f32[2,4,192,256]{3,2,1,0:T(8,128)S(1)} %get-tuple-element.23.s_ref, bf16[2,288,384]{2,1,0:T(8,128)(2,1)S(1)} %get-tuple-element.24.u_ref, ...), custom_call_target="tpu_custom_call", output_to_operand_aliasing={{0}: (5, {})} | custom-call | flops 900000000 | bytes 4000000 | tf_op jit(solution)/shard_map/pallas_call | solution.py:323
  19.8 0.2 collective-permute-done.3.second_ref
  20.0 1.7 %shard_map.61 = bf16[2,2,4,96,256]{4,3,2,1,0:T(8,128)(2,1)} custom-call(f32[2,4,192,256]{3,2,1,0:T(8,128)S(1)} %get-tuple-element.23.s_ref, bf16[2,288,384]{2,1,0:T(8,128)(2,1)S(1)} %get-tuple-element.24.u_ref, s32[1,4]{1,0:T(1,128)S(1)} %bitcast.14, bf16[256,256]{1,0:T(8,128)(2,1)S(1)} %get-tuple-element.25.spread_ref, ...), custom_call_target="tpu_custom_call", output_to_operand_aliasing={{}: (8, {})} | custom-call | flops 700000000 | bytes 4000000 | tf_op jit(solution)/shard_map/pallas_call | solution.py:332
  (2 shorter events, 0.1 us)
Async XLA Ops:
  0.0 1.8 %copy-start.4 = (bf16[2,2,2,192,128]{4,3,2,1,0:T(8,128)(2,1)S(1)}, bf16[2,2,2,192,128]{4,3,2,1,0:T(8,128)(2,1)}, u32[]{:S(2)}) copy-start(bf16[2,2,2,192,128]{4,3,2,1,0:T(8,128)(2,1)} %x_ref.1) | copy-start | bytes 1179652
  0.0 1.9 %copy-start = (bf16[3,3,3,192,192]{4,3,2,1,0:T(8,128)(2,1)S(1)}, bf16[3,3,3,192,192]{4,3,2,1,0:T(8,128)(2,1)}, u32[]{:S(2)}) copy-start(bf16[3,3,3,192,192]{4,3,2,1,0:T(8,128)(2,1)} %param.8) | copy-start | bytes 5971972
  0.0 1.9 %copy-start.2 = (f32[192]{0:T(256)S(1)}, f32[192]{0:T(256)}, u32[]{:S(2)}) copy-start(f32[192]{0:T(256)} %param.7) | copy-start | bytes 2308
  0.0 3.7 %collective-permute-start.1 = (bf16[2,2,2,192,128]{4,3,2,1,0:T(8,128)(2,1)}, bf16[2,2,2,192,128]{4,3,2,1,0:T(8,128)(2,1)S(1)}, u32[]{:S(2)}, u32[]{:S(2)}) collective-permute-start(bf16[2,2,2,192,128]{4,3,2,1,0:T(8,128)(2,1)} %x_ref.1), channel_id=1, source_target_pairs={{0,4},{1,5},{2,6},{3,7},{4,0},{5,1},{6,2},{7,3},{8,12},{9,13},{10,... | collective-permute-start | bytes 1179656 | tf_op jit(solution)/shard_map/ppermute | solution.py:253
  0.1 8.1 %collective-permute-start = (bf16[2,2,2,192,128]{4,3,2,1,0:T(8,128)(2,1)}, bf16[2,2,2,192,128]{4,3,2,1,0:T(8,128)(2,1)S(1)}, u32[]{:S(2)}, u32[]{:S(2)}) collective-permute-start(bf16[2,2,2,192,128]{4,3,2,1,0:T(8,128)(2,1)} %x_ref.1), channel_id=1, source_target_pairs={{0,64},{1,65},{2,66},{3,67},{4,8},{5,9},{6,10},{7,11},{8,4},{9,5},... | collective-permute-start | bytes 1179656 | tf_op jit(solution)/shard_map/ppermute | solution.py:253
  1.9 1.8 %copy-start.1 = (bf16[3,3,96,192]{3,2,1,0:T(8,128)(2,1)S(1)}, bf16[3,3,96,192]{3,2,1,0:T(8,128)(2,1)}, u32[]{:S(2)}) copy-start(bf16[3,3,96,192]{3,2,1,0:T(8,128)(2,1)} %param.9) | copy-start | bytes 995332
  4.2 9.1 %collective-permute-start.4 = (bf16[2,2,192,256]{3,2,1,0:T(8,128)(2,1)S(1)}, bf16[2,2,192,256]{3,2,1,0:T(8,128)(2,1)S(1)}, u32[]{:S(2)}, u32[]{:S(2)}) collective-permute-start(bf16[2,2,192,256]{3,2,1,0:T(8,128)(2,1)S(1)} %get-tuple-element.28), channel_id=1, source_target_pairs={{0,192},{1,193},{2,194},{3,195},{4,5},{5,4},{6,7},{7,6},{8,200},{9... | collective-permute-start | bytes 1179656 | tf_op jit(solution)/shard_map/ppermute | solution.py:253
  7.3 11.7 %collective-permute-start.5 = (bf16[2,2,192,256]{3,2,1,0:T(8,128)(2,1)S(1)}, bf16[2,2,192,256]{3,2,1,0:T(8,128)(2,1)S(1)}, u32[]{:S(2)}, u32[]{:S(2)}) collective-permute-start(bf16[2,2,192,256]{3,2,1,0:T(8,128)(2,1)S(1)} %get-tuple-element.29), channel_id=1, source_target_pairs={{0,64},{1,65},{2,66},{3,67},{4,7},{5,6},{6,5},{7,4},{8,72},{9,73},... | collective-permute-start | bytes 1179656 | tf_op jit(solution)/shard_map/ppermute | solution.py:253
  8.2 10.9 %copy-start.3 = (s32[4]{0:T(128)S(1)}, s32[4]{0:T(128)}, u32[]{:S(2)}) copy-start(s32[4]{0:T(128)} %param.6) | copy-start | bytes 52
  10.0 9.2 %collective-permute-start.2 = (bf16[2,2,192,256]{3,2,1,0:T(8,128)(2,1)S(1)}, bf16[2,2,192,256]{3,2,1,0:T(8,128)(2,1)S(1)}, u32[]{:S(2)}, u32[]{:S(2)}) collective-permute-start(bf16[2,2,192,256]{3,2,1,0:T(8,128)(2,1)S(1)} %get-tuple-element.26), channel_id=1, source_target_pairs={{0,1},{1,0},{2,3},{3,2},{4,68},{5,69},{6,70},{7,71},{8,9},{9,8},{1... | collective-permute-start | bytes 1179656 | tf_op jit(solution)/shard_map/ppermute | solution.py:253
  12.2 7.8 %collective-permute-start.3 = (bf16[2,2,192,256]{3,2,1,0:T(8,128)(2,1)S(1)}, bf16[2,2,192,256]{3,2,1,0:T(8,128)(2,1)S(1)}, u32[]{:S(2)}, u32[]{:S(2)}) collective-permute-start(bf16[2,2,192,256]{3,2,1,0:T(8,128)(2,1)S(1)} %get-tuple-element.27), channel_id=1, source_target_pairs={{0,3},{1,2},{2,1},{3,0},{4,196},{5,197},{6,198},{7,199},{8,11},{9,... | collective-permute-start | bytes 1179656 | tf_op jit(solution)/shard_map/ppermute | solution.py:253
